TPU v7x, 256 devices: a whole 4x4x8 slice. The times are simulated.
256 devices in a mesh: ctx: 32 (over z_lo, x, core), ch: 8 (over z_hi, y).
Axes of the slice: x: 4, y: 4, z: 8 (z_hi: 2, z_lo: 4; z = z_hi * 4 + z_lo), core: 2. Of those that a mesh axis runs over, the one named last changes fastest.
Arguments:
- stream: bfloat16 [8192, 8192], P('ctx', 'ch'), may hold values from -6 to 6
- projected: bfloat16 [8192, 3, 8192], P('ctx', None, 'ch'), may hold values from -6 to 6
- short_taps: float32 [3, 3, 8192], P(None, None, 'ch'), may hold values from -3 to 3
- decay_rates: float32 [16, 8192], P(None, 'ch'), may hold values from 3.0517578e-05 to 0.05, as said below
- residues: float32 [16, 8192], P(None, 'ch'), may hold values from -0.5 to 0.5
- out_weight: bfloat16 [8192, 8192], P('ctx', 'ch'), may hold values from -0.0625 to 0.0625
Outputs:
- block_out: bfloat16 [8192, 8192], P('ctx', 'ch')
Inputs may be any that keep to these rules, and one draw needn't show every extreme that they name: `decay_rates`: rates of each channel's modes.
All inputs are finite; a program needn't handle non-finite values.
Results may differ from a plain program's by a relative error of at most 0.009.
Values may be sent and summed in bfloat16 or wider, within the bound.
No kernel may reach another device: no remote copies, remote signals or barrier semaphores. Data moves between devices by JAX's collectives and lax.ppermute only.
A program may use at most 128 MiB of HBM per device.

v0:
```python
import jax
import jax.numpy as jnp
from jax import lax
from jax.sharding import PartitionSpec as P

highest = lax.Precision.HIGHEST


def from_behind(x, axis, by):
    devices = lax.axis_size(axis)
    pairs = [(i, i + by) for i in range(devices) if 0 <= i + by < devices]
    return lax.ppermute(x, axis, pairs)


def channel_response(drive_field, decay_rates, residues):
    row_count, chan_count = drive_field.shape
    part_count = lax.axis_size("ctx")
    my_index = lax.axis_index("ctx")
    narrow = chan_count // part_count
    moved = lax.all_to_all(drive_field, "ctx", split_axis=1, concat_axis=0, tiled=True)
    my_rates = lax.dynamic_slice_in_dim(decay_rates, my_index * narrow, narrow, 1)
    my_weights = lax.dynamic_slice_in_dim(residues, my_index * narrow, narrow, 1)
    blocks = moved.reshape(part_count, row_count, narrow)
    lag_steps = jnp.arange(row_count, dtype=jnp.float32)
    decays = jnp.exp(-my_rates[:, None, :] * lag_steps[None, :, None])
    kernel = jnp.sum(my_weights[:, None, :] * decays, axis=0)
    offset = (
        jnp.arange(row_count, dtype=jnp.int32)[:, None]
        - jnp.arange(row_count, dtype=jnp.int32)[None, :]
    )
    toeplitz = jnp.where((offset >= 0)[:, :, None], kernel[jnp.maximum(offset, 0)], 0.0)
    inside = jnp.einsum("jic,bic->bjc", toeplitz, blocks, precision=highest)
    end_weights = jnp.exp(-my_rates[:, None, :] * (row_count - 1.0 - lag_steps)[None, :, None])
    end_states = jnp.einsum("nic,bic->bnc", end_weights, blocks, precision=highest)
    slab_decay = jnp.exp(-my_rates * row_count)

    def advance(state, end_state):
        return (state * slab_decay + end_state, state)

    start_state = jnp.zeros((decay_rates.shape[0], narrow), jnp.float32)
    carried = lax.scan(advance, start_state, end_states)[1]
    entering = my_weights[:, None, :] * jnp.exp(
        -my_rates[:, None, :] * (lag_steps + 1.0)[None, :, None]
    )
    outside = jnp.einsum("njc,bnc->bjc", entering, carried, precision=highest)
    answer = (inside + outside).reshape(part_count * row_count, narrow)
    return lax.all_to_all(answer, "ctx", split_axis=0, concat_axis=1, tiled=True)


def body(stream, projected, short_taps, decay_rates, residues, out_weight):
    row_count = projected.shape[0]
    prior = from_behind(projected[row_count - 2 :], "ctx", 1)
    extended = jnp.concatenate([prior, projected], axis=0).astype(jnp.float32)
    filtered = (
        short_taps[0] * extended[2:]
        + short_taps[1] * extended[1:-1]
        + short_taps[2] * extended[:-2]
    )
    queries = filtered[:, 0]
    drive_field = filtered[:, 1] * filtered[:, 2]
    response = channel_response(drive_field, decay_rates, residues)
    gated_rows = (queries * response).astype(jnp.bfloat16)
    whole = lax.all_gather(gated_rows, "ch", axis=1, tiled=True)
    summed = jnp.dot(
        whole,
        lax.all_gather(out_weight, "ctx", axis=0, tiled=True),
        preferred_element_type=jnp.float32,
    )
    return (stream.astype(jnp.float32) + summed).astype(jnp.bfloat16)


def solution(mesh):
    in_specs = (
        P("ctx", "ch"),
        P("ctx", None, "ch"),
        P(None, None, "ch"),
        P(None, "ch"),
        P(None, "ch"),
        P("ctx", "ch"),
    )
    out_specs = P("ctx", "ch")
    return jax.shard_map(body, mesh=mesh, in_specs=in_specs, out_specs=out_specs, check_vma=False)
```

profile of v0, /device:TPU:35, one launch (start us, length us, event | category | flops | bytes accessed | tf_op | source)
XLA Modules:
  0.0 607.5 jit_solution(4036214893482292375)
XLA Ops:
  6.5 0.8 slice.31
  7.4 3.7 collective-permute-start
  11.0 0.8 multiply_exponential_fusion
  12.0 1.4 slice_bitcast_fusion.3
  13.7 1.7 copy.20
  16.1 1.0 maximum_convert_fusion
  17.1 3.9 fusion.4
  21.0 1.2 slice_multiply_fusion.3
  22.1 8.1 %all-to-all-start = ((f32[256,32,32]{0,2,1:T(8,128)}), f32[256,32,32]{0,2,1:T(8,128)}, u32[]{:S(2)}, u32[]{:S(2)}) async-start(f32[256,32,32]{0,2,1:T(8,128)} %bitcast.38), calls=%async_computation | async-start | bytes 2097152 | tf_op jit(solution)/shard_map/all_to_all | solution.py:20
  30.5 0.7 broadcast_clamp_fusion
  31.2 236.7 %gather_fusion = f32[65536,32]{1,0:T(8,128)} fusion(f32[256,32]{1,0:T(8,128)S(1)} %copy.23, s32[65536]{0:T(1024)} %broadcast_clamp_fusion), kind=kCustom, calls=%fused_computation | custom fusion | bytes 17039360 | tf_op jit(solution)/shard_map/gather | solution.py:31
  268.0 22.2 %copy.24 = f32[256,256,32]{1,0,2:T(8,128)} copy(f32[256,256,32]{2,1,0:T(8,128)} %bitcast.37) | data formatting | bytes 16777216 | tf_op jit(solution)/shard_map/gather | solution.py:31
  290.2 2.8 convolution_bitcast_fusion
  293.0 0.9 copy.27
  293.9 41.6 %while.13 = (s32[]{:T(128)}, f32[16,32]{1,0:T(8,128)S(1)}, f32[32,16,32]{2,1,0:T(8,128)}, f32[16,32]{1,0:T(8,128)S(1)}, f32[32,16,32]{2,1,0:T(8,128)}, /*index=5*/s32[]{:T(128)}, s32[]{:T(128)}) while((s32[]{:T(128)}, f32[16,32]{1,0:T(8,128)S(1)}, f32[32,16,32]{2,1,0:T(8,128)}, f32[16,32]{1,0:T(8,128)S(1)}, ...), condition=%wide.region_2.3_spmd.clone, body=%wide.region_1.2_spmd.clone.sunk | while | flops 2051 | bytes 19036 | solution.py:41
  297.1 0.7 bitcast_add_fusion.2
  299.7 0.7 bitcast_add_fusion.2
  302.3 0.7 bitcast_add_fusion.2
  303.6 0.7 bitcast_add_fusion.2
  304.9 0.7 bitcast_add_fusion.2
  307.5 0.7 bitcast_add_fusion.2
  308.8 0.7 bitcast_add_fusion.2
  310.1 0.7 bitcast_add_fusion.2
  314.0 0.7 bitcast_add_fusion.2
  335.5 1.1 copy.28
  336.7 11.6 %fusion = f32[32,32,256]{2,1,0:T(8,128)S(1)} fusion(f32[256,256,32]{1,0,2:T(8,128)} %copy.24, pred[256,256]{1,0:T(8,128)(4,1)S(1)} %subtract_compare_fusion, f32[256,32,32]{0,2,1:T(8,128)} %all-to-all-done), kind=kOutput, calls=%fused_computation.3 | convolution fusion | flops 807403520 | bytes 10551296 | tf_op jit(solution)/shard_map/jic,bic->bjc/dot_general | solution.py:32
  348.2 1.3 fusion.6
  350.1 33.4 %all_to_all.26 = f32[32,256,32]{1,2,0:T(8,128)S(1)} all-to-all(f32[32,256,32]{1,2,0:T(8,128)S(1)} %copy.29), channel_id=1, replica_groups=mesh['ctx'=32,'ch'=8] {'ctx'}, dimensions={0} | all-to-all | bytes 2097152 | tf_op jit(solution)/shard_map/all_to_all | solution.py:47
  383.5 0.9 fusion.9
  385.3 105.3 %all-gather.3.cloned.1.call-done = bf16[256,8192]{0,1:T(8,128)(2,1)} async-done(((bf16[256,1024]{0,1:T(8,128)(2,1)}), bf16[256,8192]{0,1:T(8,128)(2,1)}) %all-gather.3.cloned.1.call-update) | async-done | bytes 4194320 | tf_op jit(solution)/shard_map/all_gather | solution.py:63
  490.5 97.9 %all-gather.5.cloned.1.call-done = bf16[8192,1024]{1,0:T(8,128)(2,1)} async-done(((bf16[256,1024]{1,0:T(8,128)(2,1)}), bf16[8192,1024]{1,0:T(8,128)(2,1)}) %all-gather.5.cloned.1.call-update) | async-done | bytes 16777232 | tf_op jit(solution)/shard_map/all_gather | solution.py:66
  588.4 12.3 %fusion.7 = bf16[256,1024]{1,0:T(8,128)(2,1)} fusion(bf16[256,8192]{0,1:T(8,128)(2,1)} %all-gather.3.cloned.1.call-done, bf16[8192,1024]{1,0:T(8,128)(2,1)} %all-gather.5.cloned.1.call-done, bf16[256,1024]{1,0:T(8,128)(2,1)} %param.8), kind=kOutput, calls=%fused_computation.16 | convolution fusion | flops 4295753728 | bytes 22020096 | tf_op jit(solution)/shard_map/dot_general | solution.py:64
  (82 shorter events, 38.0 us)
Async XLA Ops:
  7.4 8.3 %collective-permute-start = (bf16[2,3,1024]{2,0,1:T(2,128)(2,1)S(1)}, bf16[2,3,1024]{2,0,1:T(2,128)(2,1)S(1)}, u32[]{:S(2)}, u32[]{:S(2)}) collective-permute-start(bf16[2,3,1024]{2,0,1:T(2,128)(2,1)S(1)} %slice.31), channel_id=1, source_target_pairs={{0,8},{8,16},{16,24},{24,32},{32,40},{40,48},{48,56},{56,64},{64,7... | collective-permute-start | bytes 36872 | tf_op jit(solution)/shard_map/ppermute | solution.py:12
  11.9 1.7 copy-start
  12.0 1.7 copy-start.2
  22.1 268.1 %all-to-all-start = ((f32[256,32,32]{0,2,1:T(8,128)}), f32[256,32,32]{0,2,1:T(8,128)}, u32[]{:S(2)}, u32[]{:S(2)}) async-start(f32[256,32,32]{0,2,1:T(8,128)} %bitcast.38), calls=%async_computation | async-start | bytes 2097152 | tf_op jit(solution)/shard_map/all_to_all | solution.py:20
  30.3 460.3 %all-gather.3.cloned.1.call-start = ((), (), s32[]{:S(2)}) async-start(), calls=%async_computation.2 | async-start | bytes 4718592 | tf_op jit(solution)/shard_map/all_gather | solution.py:63
  268.0 22.2 %copy-start.1 = (f32[16,32]{0,1:T(8,128)S(1)}, f32[16,32]{0,1:T(8,128)}, u32[]{:S(2)}) copy-start(f32[16,32]{0,1:T(8,128)} %copy-done) | copy-start | bytes 6148
  336.6 11.6 %copy-start.3 = (f32[16,32]{0,1:T(8,128)S(1)}, f32[16,32]{0,1:T(8,128)}, u32[]{:S(2)}) copy-start(f32[16,32]{0,1:T(8,128)} %copy-done.2) | copy-start | bytes 6148
  384.5 203.9 %all-gather.5.cloned.1.call-start = ((), (), s32[]{:S(2)}) async-start(), calls=%async_computation.3 | async-start | bytes 17301504 | tf_op jit(solution)/shard_map/all_gather | solution.py:66
Sparse Core Ops, SparseCore 0:
  384.6 105.8 all-gather.2
  492.4 95.9 all-gather.4
where the time goes:
time: 616 us; the launch traced here: 608 us
  local copies, waits for them, and re-layouts  266 us (43%)
  waiting for transfers between devices  204 us (33%)
  other arithmetic  50.4 us (8%)
  blocking collectives  33.4 us (5%)
  matrix products  28 us (5%)
  between operations  13.6 us (2%)
  starting transfers between devices  12.3 us (2%)
    gather x2, local copies, waits for them, and re-layouts, channel_response(): kernel[jnp.maximum(offset, 0)]  259 us
    all_gather x1, waiting for transfers between devices, body(): whole = lax.all_gather(gated_rows, 'ch', axis=1, tiled=True)  105 us
    all_gather x1, waiting for transfers between devices, body(): lax.all_gather(out_weight, 'ctx', axis=0, tiled=True)  97.9 us
    all_to_all x1, blocking collectives, channel_response(): lax.all_to_all(answer, 'ctx', split_axis=0, concat_axis=1, tiled=True)  33.4 us
    add x32, other arithmetic, advance(): return (state * slab_decay + end_state, state)  22.4 us
    dynamic_update_slice x32, other arithmetic, channel_response(): carried = lax.scan(advance, start_state, end_states)[1]  19.1 us
  transfers between devices with their start and end apart: 4, of which 2 were waited for; matrix products, arithmetic and copies ran while one was open for 43% of the time, Pallas kernels for 0%

commit v1 on v0

v1 whole, which is shorter than its diff:
```python
import functools

import jax
import jax.numpy as jnp
from jax import lax
from jax.experimental import pallas as pl
from jax.experimental.pallas import tpu as pltpu
from jax.sharding import PartitionSpec as P

F32, BF16 = jnp.float32, jnp.bfloat16
ZL, X, CORE, ZH, Y = 4, 4, 2, 2, 4
ROWS, CHANS, MODES = 256, 1024, 16
LANES = CHANS // 128
PITCH = ROWS + 8
HALF = CHANS // 2
VMEM_LIMIT = 48 * 1024 * 1024


def ctx_pairs(move):
    pairs = []
    for p in range(ZL * X * CORE):
        target = move(p // (X * CORE), (p // CORE) % X, p % CORE)
        if target is not None:
            z, x, c = target
            pairs.append((p, (z * X + x) * CORE + c))
    return pairs


def ch_pairs(move):
    pairs = []
    for q in range(ZH * Y):
        h, y = move(q // Y, q % Y)
        pairs.append((q, h * Y + y))
    return pairs


def swap_core(v):
    return lax.ppermute(v, "ctx", ctx_pairs(lambda z, x, c: (z, x, 1 - c)))


def shift_x(v, by):
    return lax.ppermute(v, "ctx", ctx_pairs(lambda z, x, c: (z, (x + by) % X, c)))


def shift_z(v, by):
    return lax.ppermute(v, "ctx", ctx_pairs(lambda z, x, c: ((z + by) % ZL, x, c)))


def ahead_z(v, by):
    return lax.ppermute(v, "ctx", ctx_pairs(lambda z, x, c: (z + by, x, c) if z + by < ZL else None))


def swap_zh(v):
    return lax.ppermute(v, "ch", ch_pairs(lambda h, y: (1 - h, y)))


def shift_y(v, by):
    return lax.ppermute(v, "ch", ch_pairs(lambda h, y: (h, (y + by) % Y)))


def drive_kernel(proj, halo, taps, rates, drive, queries, ends, wide):
    def lane_block(j, carry):
        lanes = pl.ds(pl.multiple_of(j * 128, 128), 128)
        base = pl.multiple_of(j * PITCH, 8)
        for s in range(3):
            wide[s, 6:8, :] = halo[s, :, lanes]
            wide[s, 8:, :] = proj[s, :, lanes].astype(F32)
        step = 64
        for start in range(0, ROWS, step):
            filtered = []
            for s in range(3):
                total = taps[s : s + 1, lanes] * wide[s, 8 + start : 8 + start + step, :]
                total += taps[3 + s : 4 + s, lanes] * wide[s, 7 + start : 7 + start + step, :]
                total += taps[6 + s : 7 + s, lanes] * wide[s, 6 + start : 6 + start + step, :]
                filtered.append(total)
            queries[start : start + step, lanes] = filtered[0]
            drive[pl.ds(base + start, step), :] = filtered[1] * filtered[2]
        lam = [jnp.broadcast_to(rates[n : n + 1, lanes], (8, 128)) for n in range(MODES)]
        decay = [jnp.exp(-8.0 * lam[n]) for n in range(MODES)]

        def rows_block(b, states):
            u = drive[pl.ds(base + b * 8, 8), :]
            return tuple(states[n] * decay[n] + u for n in range(MODES))

        zero = jnp.zeros((8, 128), F32)
        states = lax.fori_loop(0, ROWS // 8, rows_block, (zero,) * MODES, unroll=4)
        left = 7.0 - lax.broadcasted_iota(jnp.int32, (8, 128), 0).astype(F32)
        for n in range(MODES):
            end = jnp.sum(states[n] * jnp.exp(-lam[n] * left), axis=0, keepdims=True)
            ends[n, pl.ds(j, 1), :] = end
        return carry

    lax.fori_loop(0, LANES, lane_block, 0)


def drive_call(proj, halo, taps, rates):
    return pl.pallas_call(
        drive_kernel,
        out_shape=(
            jax.ShapeDtypeStruct((LANES * PITCH, 128), F32),
            jax.ShapeDtypeStruct((ROWS, CHANS), F32),
            jax.ShapeDtypeStruct((MODES, LANES, 128), F32),
        ),
        scratch_shapes=[pltpu.VMEM((3, ROWS + 8, 128), F32)],
        compiler_params=pltpu.CompilerParams(vmem_limit_bytes=VMEM_LIMIT),
        cost_estimate=pl.CostEstimate(flops=30_000_000, bytes_accessed=4_000_000, transcendentals=0),
        name="drive_and_ends",
    )(proj, halo, taps, rates)


def response_kernel(place, drive, queries, rates, weights, carried, keep, send, response):
    decay = [jnp.exp(-rates[n]) for n in range(MODES)]
    gain = [weights[n] for n in range(MODES)]

    def step(t, states):
        u = drive[pl.ds(t, LANES, stride=PITCH), :]
        states = tuple(states[n] * decay[n] + u for n in range(MODES))
        terms = [states[n] * gain[n] for n in range(MODES)]
        while len(terms) > 1:
            terms = [terms[i] + terms[i + 1] for i in range(0, len(terms), 2)]
        response[pl.ds(t, LANES, stride=PITCH), :] = terms[0]
        return states

    lax.fori_loop(0, ROWS, step, tuple(carried[n] for n in range(MODES)), unroll=4)
    core = place[0]
    for out, parity in ((keep, core), (send, 1 - core)):
        for k in range(HALF // 128):
            j = (k // 2) * 4 + parity * 2 + k % 2
            lanes = pl.ds(pl.multiple_of(j * 128, 128), 128)
            rows = pl.ds(pl.multiple_of(j * PITCH, 8), ROWS)
            out[:, k * 128 : (k + 1) * 128] = (queries[:, lanes] * response[rows, :]).astype(BF16)


def response_call(place, drive, queries, rates, weights, carried):
    whole = pl.BlockSpec(memory_space=pltpu.VMEM)
    return pl.pallas_call(
        response_kernel,
        in_specs=[pl.BlockSpec(memory_space=pltpu.SMEM)] + [whole] * 5,
        out_shape=(jax.ShapeDtypeStruct((ROWS, HALF), BF16), jax.ShapeDtypeStruct((ROWS, HALF), BF16)),
        scratch_shapes=[pltpu.VMEM((LANES * PITCH, 128), F32)],
        compiler_params=pltpu.CompilerParams(vmem_limit_bytes=VMEM_LIMIT),
        cost_estimate=pl.CostEstimate(flops=30_000_000, bytes_accessed=3_000_000, transcendentals=0),
        name="response_and_gate",
    )(place, drive, queries, rates, weights, carried)


def project_kernel(place, *refs):
    weights, gated = refs[: ZL * X], refs[ZL * X : ZL * X + ZH * Y * 2]
    mine, other, left, right, total, w_sem, g_sem = refs[ZL * X + ZH * Y * 2 :]
    z, x, h, y = place[1], place[2], place[3], place[4]
    copies_w, copies_g = [], []
    for i in range(ZH):
        for j in range(Y):
            q = lax.rem(h + i, ZH) * Y + lax.rem(y + Y - j, Y)
            columns = pl.ds(pl.multiple_of(q * HALF, HALF), HALF)
            for part in range(2):
                n = (i * Y + j) * 2 + part
                copy = pltpu.make_async_copy(
                    gated[n], left.at[pl.ds(part * ROWS, ROWS), columns], g_sem.at[n]
                )
                copy.start()
                copies_g.append(copy)
    for s in range(ZL):
        for r in range(X):
            n = s * X + r
            m = lax.rem(z + ZL - s, ZL) * X + lax.rem(x + X - r, X)
            rows = pl.ds(pl.multiple_of(m * ROWS, ROWS), ROWS)
            copy = pltpu.make_async_copy(weights[n], right.at[rows, :], w_sem.at[n])
            copy.start()
            copies_w.append(copy)
    for copy in copies_g:
        copy.wait()
    depth = X * ROWS
    for s in range(ZL):
        for r in range(X):
            copies_w[s * X + r].wait()
        start = pl.multiple_of(lax.rem(z + ZL - s, ZL) * depth, depth)
        for col in range(0, CHANS, 256):
            product = jnp.dot(
                left[:, pl.ds(start, depth)],
                right[pl.ds(start, depth), col : col + 256],
                preferred_element_type=F32,
            )
            if s > 0:
                product += total[:, col : col + 256]
            if s < ZL - 1:
                total[:, col : col + 256] = product
            else:
                mine[:, col : col + 256] = product[:ROWS]
                other[:, col : col + 256] = product[ROWS:].astype(BF16)


def project_call(place, weights, gated):
    count = len(weights) + len(gated)
    whole = pl.BlockSpec(memory_space=pltpu.VMEM)
    return pl.pallas_call(
        project_kernel,
        in_specs=[pl.BlockSpec(memory_space=pltpu.SMEM)] + [pl.BlockSpec(memory_space=pl.ANY)] * count,
        out_specs=(whole, whole),
        out_shape=(jax.ShapeDtypeStruct((ROWS, CHANS), F32), jax.ShapeDtypeStruct((ROWS, CHANS), BF16)),
        scratch_shapes=[
            pltpu.VMEM((2 * ROWS, ZH * Y * HALF), BF16),
            pltpu.VMEM((ZL * X * ROWS, CHANS), BF16),
            pltpu.VMEM((2 * ROWS, CHANS), F32),
            pltpu.SemaphoreType.DMA((len(weights),)),
            pltpu.SemaphoreType.DMA((len(gated),)),
        ],
        compiler_params=pltpu.CompilerParams(vmem_limit_bytes=VMEM_LIMIT),
        cost_estimate=pl.CostEstimate(flops=4_300_000_000, bytes_accessed=14_000_000, transcendentals=0),
        name="projection",
    )(place, *weights, *gated)


def carried_states(ends, rates, z, x, core):
    def decays(steps):
        return jnp.exp(-rates * (ROWS * steps).astype(F32))

    one = jnp.int32(1)
    sibling = swap_core(ends)
    first = jnp.where(core == 0, ends, sibling)
    second = jnp.where(core == 0, sibling, ends)
    chip = decays(one) * first + second
    arrived = [shift_x(chip, r) for r in range(1, X)]
    group = decays(2 * (X - 1 - x)) * chip
    before = jnp.zeros_like(chip)
    for r in range(1, X):
        origin = lax.rem(x + X - r, X)
        group += decays(2 * (X - 1 - origin)) * arrived[r - 1]
        before += jnp.where(r <= x, 1.0, 0.0) * decays(one * 2 * (r - 1)) * arrived[r - 1]
    groups = [ahead_z(group, s) for s in range(1, ZL)]
    far = groups[0]
    for s in range(2, ZL):
        far += decays(one * 2 * X * (s - 1)) * groups[s - 1]
    into_chip = before + decays(2 * x) * far
    return jnp.where(core == 0, into_chip, decays(one) * into_chip + first)


def body(stream, projected, short_taps, decay_rates, residues, out_weight):
    p, q = lax.axis_index("ctx"), lax.axis_index("ch")
    core, x, z = p % CORE, (p // CORE) % X, p // (CORE * X)
    y, h = q % Y, q // Y
    place = jnp.stack([core, z, x, h, y]).astype(jnp.int32)

    proj = projected.transpose(1, 0, 2)
    halo = lax.ppermute(projected[ROWS - 2 :], "ctx", [(i, i + 1) for i in range(ZL * X * CORE - 1)])
    halo = halo.transpose(1, 0, 2).astype(F32)
    drive, queries, ends = drive_call(proj, halo, short_taps.reshape(9, CHANS), decay_rates)

    shards = [out_weight] + [shift_z(out_weight, s) for s in range(1, ZL)]
    weights = []
    for s in range(ZL):
        weights.append(shards[s])
        weights += [shift_x(shards[s], r) for r in range(1, X)]

    rates3 = decay_rates.reshape(MODES, LANES, 128)
    weights3 = residues.reshape(MODES, LANES, 128)
    carried = carried_states(ends, rates3, z, x, core)
    keep, send = response_call(place, drive, queries, rates3, weights3, carried)
    theirs = swap_core(send)

    gated = []
    for part in (keep, theirs):
        across = swap_zh(part)
        gated.append([[v] + [shift_y(v, j) for j in range(1, Y)] for v in (part, across)])
    pieces = [gated[part][i][j] for i in range(ZH) for j in range(Y) for part in range(2)]

    mine, other = project_call(place, weights, pieces)
    summed = stream.astype(F32) + mine + swap_core(other).astype(F32)
    return summed.astype(BF16)


def solution(mesh):
    in_specs = (
        P("ctx", "ch"),
        P("ctx", None, "ch"),
        P(None, None, "ch"),
        P(None, "ch"),
        P(None, "ch"),
        P("ctx", "ch"),
    )
    return jax.shard_map(body, mesh=mesh, in_specs=in_specs, out_specs=P("ctx", "ch"), check_vma=False)
```

time: 616 us -> 208 us (0.34)
  the two profiles are of different devices: /device:TPU:35 before, /device:TPU:81 now
where the time goes in v1:
time: 208 us
  waiting for transfers between devices  121 us (58%)
  starting transfers between devices  65.4 us (31%)
  Pallas kernels  14.2 us (7%)
  local copies, waits for them, and re-layouts  4.88 us (2%)
  other arithmetic  2.46 us (1%)
    ppermute x15, waiting for transfers between devices, shift_x(): lax.ppermute(v, 'ctx', ctx_pairs(lambda z, x, c: (z, (x + by) % X, c)))  57.1 us
    ppermute x2, waiting for transfers between devices, swap_zh(): return lax.ppermute(v, 'ch', ch_pairs(lambda h, y: (1 - h, y)))  23.1 us
    ppermute x12, waiting for transfers between devices, shift_y(): return lax.ppermute(v, 'ch', ch_pairs(lambda h, y: (h, (y + by) % Y)))  16.5 us
    ppermute x3, waiting for transfers between devices, shift_z(): lax.ppermute(v, 'ctx', ctx_pairs(lambda z, x, c: ((z + by) % ZL, x, c)))  16.3 us
    ppermute x3, starting transfers between devices, shift_z(): lax.ppermute(v, 'ctx', ctx_pairs(lambda z, x, c: ((z + by) % ZL, x, c)))  16.3 us
    ppermute x12, starting transfers between devices, shift_y(): return lax.ppermute(v, 'ch', ch_pairs(lambda h, y: (h, (y + by) % Y)))  13.7 us
    ppermute x15, starting transfers between devices, shift_x(): lax.ppermute(v, 'ctx', ctx_pairs(lambda z, x, c: (z, (x + by) % X, c)))  11.7 us
    ppermute x2, starting transfers between devices, swap_zh(): return lax.ppermute(v, 'ch', ch_pairs(lambda h, y: (1 - h, y)))  8.51 us
  transfers between devices with their start and end apart: 39, of which 23 were waited for; matrix products, arithmetic and copies ran while one was open for 0% of the time, Pallas kernels for 0%

profile of v1, /device:TPU:81, one launch (start us, length us, event | category | flops | bytes accessed | tf_op | source)
XLA Modules:
  0.0 207.8 jit_solution(7710590907622206306)
XLA Ops:
  0.9 3.7 %collective-permute-start.15 = (bf16[2,3,1024]{2,0,1:T(2,128)(2,1)S(1)}, bf16[2,3,1024]{2,0,1:T(2,128)(2,1)S(1)}, u32[]{:S(2)}, u32[]{:S(2)}) collective-permute-start(bf16[2,3,1024]{2,0,1:T(2,128)(2,1)S(1)} %slice.3), channel_id=1, source_target_pairs={{0,8},{8,16},{16,24},{24,32},{32,40},{40,48},{48,56},{56,64},{64,7... | collective-permute-start | bytes 36872 | tf_op jit(solution)/shard_map/ppermute | solution.py:245
  7.6 2.8 %drive_and_ends.1 = (f32[2112,128]{1,0:T(8,128)S(1)}, f32[256,1024]{1,0:T(8,128)S(1)}, f32[16,8,128]{2,1,0:T(8,128)S(1)}) custom-call(bf16[3,256,1024]{2,1,0:T(8,128)(2,1)S(1)} %bitcast.16, f32[3,2,1024]{2,1,0:T(2,128)S(1)} %convert_bitcast_fusion.halo, f32[9,1024]{1,0:T(8,128)S(1)} %reshape.9.taps, f32[16,1024]{1,0:T(8,128)S(1)} %copy-done.1), custom_call_target="tpu_custom_call" | custom-call | flops 30000000 | bytes 4000000 | tf_op jit(solution)/shard_map/drive_and_ends/pallas_call | solution.py:97
  10.5 3.4 %collective-permute-start.16 = (f32[16,8,128]{2,1,0:T(8,128)S(1)}, f32[16,8,128]{2,1,0:T(8,128)S(1)}, u32[]{:S(2)}, u32[]{:S(2)}) collective-permute-start(f32[16,8,128]{2,1,0:T(8,128)S(1)} %get-tuple-element.14), channel_id=1, source_target_pairs={{0,8},{8,0},{16,24},{24,16},{32,40},{40,32},{48,56},{56,48},{64,72... | collective-permute-start | bytes 196616 | tf_op jit(solution)/shard_map/ppermute | solution.py:38
  19.8 1.9 collective-permute-done.17
  23.8 4.2 %collective-permute-start.20 = (f32[16,8,128]{2,1,0:T(8,128)S(1)}, f32[16,8,128]{2,1,0:T(8,128)S(1)}, u32[]{:S(2)}, u32[]{:S(2)}) collective-permute-start(f32[16,8,128]{2,1,0:T(8,128)S(1)} %multiply_add_fusion), channel_id=1, source_target_pairs={{0,64},{8,72},{16,80},{24,88},{32,96},{40,104},{48,112},{56,120},{... | collective-permute-start | bytes 196616 | tf_op jit(solution)/shard_map/ppermute | solution.py:50
  28.2 3.0 %collective-permute-done.21 = f32[16,8,128]{2,1,0:T(8,128)S(1)} collective-permute-done((f32[16,8,128]{2,1,0:T(8,128)S(1)}, f32[16,8,128]{2,1,0:T(8,128)S(1)}, u32[]{:S(2)}, u32[]{:S(2)}) %collective-permute-start.21) | collective-permute-done | bytes 65568 | tf_op jit(solution)/shard_map/ppermute | solution.py:50
  31.2 2.1 %collective-permute-done.20 = f32[16,8,128]{2,1,0:T(8,128)S(1)} collective-permute-done((f32[16,8,128]{2,1,0:T(8,128)S(1)}, f32[16,8,128]{2,1,0:T(8,128)S(1)}, u32[]{:S(2)}, u32[]{:S(2)}) %collective-permute-start.20) | collective-permute-done | bytes 65568 | tf_op jit(solution)/shard_map/ppermute | solution.py:50
  33.4 3.3 %response_and_gate.1 = (bf16[256,512]{1,0:T(8,128)(2,1)S(1)}, bf16[256,512]{1,0:T(8,128)(2,1)S(1)}) custom-call(s32[5]{0:T(128)S(1)} %stack.23.place, f32[2112,128]{1,0:T(8,128)S(1)} %get-tuple-element.12.drive, f32[256,1024]{1,0:T(8,128)S(1)} %get-tuple-element.13.queries, f32[16,8,128]{2,1,0:T(8,128)S(1)} %bitcast.15, f32[16,8,128]{2,1,0:T(8,128)S(1)} %bitcast.17, ...), custom_call_target="tpu_custom_call" | custom-call | flops 30000000 | bytes 3000000 | tf_op jit(solution)/shard_map/response_and_gate/pallas_call | solution.py:136
  38.2 4.3 %collective-permute-start.30 = (bf16[256,512]{1,0:T(8,128)(2,1)S(1)}, bf16[256,512]{1,0:T(8,128)(2,1)S(1)}, u32[]{:S(2)}, u32[]{:S(2)}) collective-permute-start(bf16[256,512]{1,0:T(8,128)(2,1)S(1)} %get-tuple-element.15.refs_16_), channel_id=1, source_target_pairs={{0,4},{1,5},{2,6},{3,7},{4,0},{5,1},{6,2},{7,3},{8,12},{9,13},{10,... | collective-permute-start | bytes 786440 | tf_op jit(solution)/shard_map/ppermute | solution.py:54
  42.6 2.6 %collective-permute-start.26 = (bf16[256,512]{1,0:T(8,128)(2,1)S(1)}, bf16[256,512]{1,0:T(8,128)(2,1)S(1)}, u32[]{:S(2)}, u32[]{:S(2)}) collective-permute-start(bf16[256,512]{1,0:T(8,128)(2,1)S(1)} %get-tuple-element.15.refs_16_), channel_id=1, source_target_pairs={{0,2},{1,3},{2,0},{3,1},{4,6},{5,7},{6,4},{7,5},{8,10},{9,11},{10,... | collective-permute-start | bytes 786440 | tf_op jit(solution)/shard_map/ppermute | solution.py:58
  45.3 5.8 %collective-permute-done.30.refs_24_ = bf16[256,512]{1,0:T(8,128)(2,1)S(1)} collective-permute-done((bf16[256,512]{1,0:T(8,128)(2,1)S(1)}, bf16[256,512]{1,0:T(8,128)(2,1)S(1)}, u32[]{:S(2)}, u32[]{:S(2)}) %collective-permute-start.30) | collective-permute-done | bytes 262176 | tf_op jit(solution)/shard_map/ppermute | solution.py:54
  51.0 16.3 %collective-permute-start.3 = (bf16[256,1024]{1,0:T(8,128)(2,1)S(1)}, bf16[256,1024]{1,0:T(8,128)(2,1)S(1)}, u32[]{:S(2)}, u32[]{:S(2)}) collective-permute-start(bf16[256,1024]{1,0:T(8,128)(2,1)S(1)} %copy-done.2), channel_id=1, source_target_pairs={{0,64},{8,72},{16,80},{24,88},{32,96},{40,104},{48,112},{56,120},{... | collective-permute-start | bytes 1572872 | tf_op jit(solution)/shard_map/ppermute | solution.py:46
  69.3 14.1 %collective-permute-done.7.refs_8_ = bf16[256,1024]{1,0:T(8,128)(2,1)S(1)} collective-permute-done((bf16[256,1024]{1,0:T(8,128)(2,1)S(1)}, bf16[256,1024]{1,0:T(8,128)(2,1)S(1)}, u32[]{:S(2)}, u32[]{:S(2)}) %collective-permute-start.7) | collective-permute-done | bytes 524320 | tf_op jit(solution)/shard_map/ppermute | solution.py:46
  83.3 2.3 %collective-permute-done.3.refs_4_ = bf16[256,1024]{1,0:T(8,128)(2,1)S(1)} collective-permute-done((bf16[256,1024]{1,0:T(8,128)(2,1)S(1)}, bf16[256,1024]{1,0:T(8,128)(2,1)S(1)}, u32[]{:S(2)}, u32[]{:S(2)}) %collective-permute-start.3) | collective-permute-done | bytes 524320 | tf_op jit(solution)/shard_map/ppermute | solution.py:46
  85.6 4.2 %collective-permute-start.31 = (bf16[256,512]{1,0:T(8,128)(2,1)S(1)}, bf16[256,512]{1,0:T(8,128)(2,1)S(1)}, u32[]{:S(2)}, u32[]{:S(2)}) collective-permute-start(bf16[256,512]{1,0:T(8,128)(2,1)S(1)} %collective-permute-done.23.refs_17_), channel_id=1, source_target_pairs={{0,4},{1,5},{2,6},{3,7},{4,0},{5,1},{6,2},{7,3},{8,12},{9,13},{10,... | collective-permute-start | bytes 786440 | tf_op jit(solution)/shard_map/ppermute | solution.py:54
  90.0 2.6 %collective-permute-start.27 = (bf16[256,512]{1,0:T(8,128)(2,1)S(1)}, bf16[256,512]{1,0:T(8,128)(2,1)S(1)}, u32[]{:S(2)}, u32[]{:S(2)}) collective-permute-start(bf16[256,512]{1,0:T(8,128)(2,1)S(1)} %collective-permute-done.23.refs_17_), channel_id=1, source_target_pairs={{0,2},{1,3},{2,0},{3,1},{4,6},{5,7},{6,4},{7,5},{8,10},{9,11},{10,... | collective-permute-start | bytes 786440 | tf_op jit(solution)/shard_map/ppermute | solution.py:58
  92.6 2.6 %collective-permute-done.refs_1_ = bf16[256,1024]{1,0:T(8,128)(2,1)S(1)} collective-permute-done((bf16[256,1024]{1,0:T(8,128)(2,1)S(1)}, bf16[256,1024]{1,0:T(8,128)(2,1)S(1)}, u32[]{:S(2)}, u32[]{:S(2)}) %collective-permute-start) | collective-permute-done | bytes 524320 | tf_op jit(solution)/shard_map/ppermute | solution.py:42
  96.6 17.3 %collective-permute-done.31.refs_25_ = bf16[256,512]{1,0:T(8,128)(2,1)S(1)} collective-permute-done((bf16[256,512]{1,0:T(8,128)(2,1)S(1)}, bf16[256,512]{1,0:T(8,128)(2,1)S(1)}, u32[]{:S(2)}, u32[]{:S(2)}) %collective-permute-start.31) | collective-permute-done | bytes 262176 | tf_op jit(solution)/shard_map/ppermute | solution.py:54
  116.2 3.4 %collective-permute-start.35 = (bf16[256,512]{1,0:T(8,128)(2,1)S(1)}, bf16[256,512]{1,0:T(8,128)(2,1)S(1)}, u32[]{:S(2)}, u32[]{:S(2)}) collective-permute-start(bf16[256,512]{1,0:T(8,128)(2,1)S(1)} %collective-permute-done.31.refs_25_), channel_id=1, source_target_pairs={{0,2},{1,3},{2,0},{3,1},{4,6},{5,7},{6,4},{7,5},{8,10},{9,11},{10,... | collective-permute-start | bytes 786440 | tf_op jit(solution)/shard_map/ppermute | solution.py:58
  120.3 2.6 %collective-permute-done.34.refs_28_ = bf16[256,512]{1,0:T(8,128)(2,1)S(1)} collective-permute-done((bf16[256,512]{1,0:T(8,128)(2,1)S(1)}, bf16[256,512]{1,0:T(8,128)(2,1)S(1)}, u32[]{:S(2)}, u32[]{:S(2)}) %collective-permute-start.34) | collective-permute-done | bytes 262176 | tf_op jit(solution)/shard_map/ppermute | solution.py:58
  123.1 4.7 %collective-permute-done.32.refs_26_ = bf16[256,512]{1,0:T(8,128)(2,1)S(1)} collective-permute-done((bf16[256,512]{1,0:T(8,128)(2,1)S(1)}, bf16[256,512]{1,0:T(8,128)(2,1)S(1)}, u32[]{:S(2)}, u32[]{:S(2)}) %collective-permute-start.32) | collective-permute-done | bytes 262176 | tf_op jit(solution)/shard_map/ppermute | solution.py:58
  127.8 2.7 %collective-permute-start.6 = (bf16[256,1024]{1,0:T(8,128)(2,1)S(1)}, bf16[256,1024]{1,0:T(8,128)(2,1)S(1)}, u32[]{:S(2)}, u32[]{:S(2)}) collective-permute-start(bf16[256,1024]{1,0:T(8,128)(2,1)S(1)} %collective-permute-done.3.refs_4_), channel_id=1, source_target_pairs={{0,48},{8,56},{16,0},{24,8},{32,16},{40,24},{48,32},{56,40},{64,11... | collective-permute-start | bytes 1572872 | tf_op jit(solution)/shard_map/ppermute | solution.py:42
  130.5 3.7 %collective-permute-done.35.refs_29_ = bf16[256,512]{1,0:T(8,128)(2,1)S(1)} collective-permute-done((bf16[256,512]{1,0:T(8,128)(2,1)S(1)}, bf16[256,512]{1,0:T(8,128)(2,1)S(1)}, u32[]{:S(2)}, u32[]{:S(2)}) %collective-permute-start.35) | collective-permute-done | bytes 262176 | tf_op jit(solution)/shard_map/ppermute | solution.py:58
  135.1 5.5 %collective-permute-done.33.refs_27_ = bf16[256,512]{1,0:T(8,128)(2,1)S(1)} collective-permute-done((bf16[256,512]{1,0:T(8,128)(2,1)S(1)}, bf16[256,512]{1,0:T(8,128)(2,1)S(1)}, u32[]{:S(2)}, u32[]{:S(2)}) %collective-permute-start.33) | collective-permute-done | bytes 262176 | tf_op jit(solution)/shard_map/ppermute | solution.py:58
  141.8 3.3 %collective-permute-start.14 = (bf16[256,1024]{1,0:T(8,128)(2,1)S(1)}, bf16[256,1024]{1,0:T(8,128)(2,1)S(1)}, u32[]{:S(2)}, u32[]{:S(2)}) collective-permute-start(bf16[256,1024]{1,0:T(8,128)(2,1)S(1)} %collective-permute-done.11.refs_12_), channel_id=1, source_target_pairs={{0,48},{8,56},{16,0},{24,8},{32,16},{40,24},{48,32},{56,40},{64,11... | collective-permute-start | bytes 1572872 | tf_op jit(solution)/shard_map/ppermute | solution.py:42
  145.1 7.0 %collective-permute-done.8.refs_9_ = bf16[256,1024]{1,0:T(8,128)(2,1)S(1)} collective-permute-done((bf16[256,1024]{1,0:T(8,128)(2,1)S(1)}, bf16[256,1024]{1,0:T(8,128)(2,1)S(1)}, u32[]{:S(2)}, u32[]{:S(2)}) %collective-permute-start.8) | collective-permute-done | bytes 524320 | tf_op jit(solution)/shard_map/ppermute | solution.py:42
  154.0 4.1 %collective-permute-done.5.refs_6_ = bf16[256,1024]{1,0:T(8,128)(2,1)S(1)} collective-permute-done((bf16[256,1024]{1,0:T(8,128)(2,1)S(1)}, bf16[256,1024]{1,0:T(8,128)(2,1)S(1)}, u32[]{:S(2)}, u32[]{:S(2)}) %collective-permute-start.5) | collective-permute-done | bytes 524320 | tf_op jit(solution)/shard_map/ppermute | solution.py:42
  158.1 16.5 %collective-permute-done.4.refs_5_ = bf16[256,1024]{1,0:T(8,128)(2,1)S(1)} collective-permute-done((bf16[256,1024]{1,0:T(8,128)(2,1)S(1)}, bf16[256,1024]{1,0:T(8,128)(2,1)S(1)}, u32[]{:S(2)}, u32[]{:S(2)}) %collective-permute-start.4) | collective-permute-done | bytes 524320 | tf_op jit(solution)/shard_map/ppermute | solution.py:42
  176.5 4.1 %collective-permute-done.13.refs_14_ = bf16[256,1024]{1,0:T(8,128)(2,1)S(1)} collective-permute-done((bf16[256,1024]{1,0:T(8,128)(2,1)S(1)}, bf16[256,1024]{1,0:T(8,128)(2,1)S(1)}, u32[]{:S(2)}, u32[]{:S(2)}) %collective-permute-start.13) | collective-permute-done | bytes 524320 | tf_op jit(solution)/shard_map/ppermute | solution.py:42
  180.6 13.8 %collective-permute-done.12.refs_13_ = bf16[256,1024]{1,0:T(8,128)(2,1)S(1)} collective-permute-done((bf16[256,1024]{1,0:T(8,128)(2,1)S(1)}, bf16[256,1024]{1,0:T(8,128)(2,1)S(1)}, u32[]{:S(2)}, u32[]{:S(2)}) %collective-permute-start.12) | collective-permute-done | bytes 524320 | tf_op jit(solution)/shard_map/ppermute | solution.py:42
  195.3 8.1 %projection.1 = (f32[256,1024]{1,0:T(8,128)}, bf16[256,1024]{1,0:T(8,128)(2,1)S(1)}) custom-call(s32[5]{0:T(128)S(1)} %stack.23.place, bf16[256,1024]{1,0:T(8,128)(2,1)S(1)} %copy-done.2, bf16[256,1024]{1,0:T(8,128)(2,1)S(1)} %collective-permute-done.refs_1_, bf16[256,1024]{1,0:T(8,128)(2,1)} %copy-done.8, bf16[256,1024]{1,0:T(8,128)(2,1)} %copy-done.7, ...), custom_call_target="tpu_custom_call" | custom-call | flops 4300000256 | bytes 14000000 | tf_op jit(solution)/shard_map/projection/pallas_call | solution.py:196
  205.5 2.3 %add_convert_fusion = bf16[256,1024]{1,0:T(8,128)(2,1)} fusion(bf16[256,1024]{1,0:T(8,128)(2,1)S(1)} %collective-permute-done.38, f32[256,1024]{1,0:T(8,128)} %get-tuple-element.17, bf16[256,1024]{1,0:T(8,128)(2,1)S(1)} %copy-done.3), kind=kLoop, calls=%fused_computation | loop fusion | flops 1310720 | bytes 2621440 | tf_op jit(solution)/shard_map/convert_element_type | solution.py:269
  (97 shorter events, 29.4 us)
Async XLA Ops:
  22.5 8.7 %collective-permute-start.21 = (f32[16,8,128]{2,1,0:T(8,128)S(1)}, f32[16,8,128]{2,1,0:T(8,128)S(1)}, u32[]{:S(2)}, u32[]{:S(2)}) collective-permute-start(f32[16,8,128]{2,1,0:T(8,128)S(1)} %multiply_add_fusion), channel_id=1, source_target_pairs={{0,128},{8,136},{16,144},{24,152},{32,160},{40,168},{48,176},{56,1... | collective-permute-start | bytes 196616 | tf_op jit(solution)/shard_map/ppermute | solution.py:50
  23.8 9.5 %collective-permute-start.20 = (f32[16,8,128]{2,1,0:T(8,128)S(1)}, f32[16,8,128]{2,1,0:T(8,128)S(1)}, u32[]{:S(2)}, u32[]{:S(2)}) collective-permute-start(f32[16,8,128]{2,1,0:T(8,128)S(1)} %multiply_add_fusion), channel_id=1, source_target_pairs={{0,64},{8,72},{16,80},{24,88},{32,96},{40,104},{48,112},{56,120},{... | collective-permute-start | bytes 196616 | tf_op jit(solution)/shard_map/ppermute | solution.py:50
  36.7 8.6 %collective-permute-start.23 = (bf16[256,512]{1,0:T(8,128)(2,1)S(1)}, bf16[256,512]{1,0:T(8,128)(2,1)S(1)}, u32[]{:S(2)}, u32[]{:S(2)}) collective-permute-start(bf16[256,512]{1,0:T(8,128)(2,1)S(1)} %get-tuple-element.16), channel_id=1, source_target_pairs={{0,8},{8,0},{16,24},{24,16},{32,40},{40,32},{48,56},{56,48},{64,72... | collective-permute-start | bytes 786440 | tf_op jit(solution)/shard_map/ppermute | solution.py:38
  38.2 45.2 %collective-permute-start.7 = (bf16[256,1024]{1,0:T(8,128)(2,1)S(1)}, bf16[256,1024]{1,0:T(8,128)(2,1)S(1)}, u32[]{:S(2)}, u32[]{:S(2)}) collective-permute-start(bf16[256,1024]{1,0:T(8,128)(2,1)S(1)} %copy-done.2), channel_id=1, source_target_pairs={{0,128},{8,136},{16,144},{24,152},{32,160},{40,168},{48,176},{56,1... | collective-permute-start | bytes 1572872 | tf_op jit(solution)/shard_map/ppermute | solution.py:46
  38.2 12.9 %collective-permute-start.30 = (bf16[256,512]{1,0:T(8,128)(2,1)S(1)}, bf16[256,512]{1,0:T(8,128)(2,1)S(1)}, u32[]{:S(2)}, u32[]{:S(2)}) collective-permute-start(bf16[256,512]{1,0:T(8,128)(2,1)S(1)} %get-tuple-element.15.refs_16_), channel_id=1, source_target_pairs={{0,4},{1,5},{2,6},{3,7},{4,0},{5,1},{6,2},{7,3},{8,12},{9,13},{10,... | collective-permute-start | bytes 786440 | tf_op jit(solution)/shard_map/ppermute | solution.py:54
  42.5 24.9 %collective-permute-start.28 = (bf16[256,512]{1,0:T(8,128)(2,1)S(1)}, bf16[256,512]{1,0:T(8,128)(2,1)S(1)}, u32[]{:S(2)}, u32[]{:S(2)}) collective-permute-start(bf16[256,512]{1,0:T(8,128)(2,1)S(1)} %get-tuple-element.15.refs_16_), channel_id=1, source_target_pairs={{0,3},{1,0},{2,1},{3,2},{4,7},{5,4},{6,5},{7,6},{8,11},{9,8},{10,9... | collective-permute-start | bytes 786440 | tf_op jit(solution)/shard_map/ppermute | solution.py:58
  42.6 26.0 %collective-permute-start.26 = (bf16[256,512]{1,0:T(8,128)(2,1)S(1)}, bf16[256,512]{1,0:T(8,128)(2,1)S(1)}, u32[]{:S(2)}, u32[]{:S(2)}) collective-permute-start(bf16[256,512]{1,0:T(8,128)(2,1)S(1)} %get-tuple-element.15.refs_16_), channel_id=1, source_target_pairs={{0,2},{1,3},{2,0},{3,1},{4,6},{5,7},{6,4},{7,5},{8,10},{9,11},{10,... | collective-permute-start | bytes 786440 | tf_op jit(solution)/shard_map/ppermute | solution.py:58
  45.3 24.0 %collective-permute-start.24 = (bf16[256,512]{1,0:T(8,128)(2,1)S(1)}, bf16[256,512]{1,0:T(8,128)(2,1)S(1)}, u32[]{:S(2)}, u32[]{:S(2)}) collective-permute-start(bf16[256,512]{1,0:T(8,128)(2,1)S(1)} %get-tuple-element.15.refs_16_), channel_id=1, source_target_pairs={{0,1},{1,2},{2,3},{3,0},{4,5},{5,6},{6,7},{7,4},{8,9},{9,10},{10,1... | collective-permute-start | bytes 786440 | tf_op jit(solution)/shard_map/ppermute | solution.py:58
  51.0 34.6 %collective-permute-start.3 = (bf16[256,1024]{1,0:T(8,128)(2,1)S(1)}, bf16[256,1024]{1,0:T(8,128)(2,1)S(1)}, u32[]{:S(2)}, u32[]{:S(2)}) collective-permute-start(bf16[256,1024]{1,0:T(8,128)(2,1)S(1)} %copy-done.2), channel_id=1, source_target_pairs={{0,64},{8,72},{16,80},{24,88},{32,96},{40,104},{48,112},{56,120},{... | collective-permute-start | bytes 1572872 | tf_op jit(solution)/shard_map/ppermute | solution.py:46
  67.3 22.5 %collective-permute-start.2 = (bf16[256,1024]{1,0:T(8,128)(2,1)S(1)}, bf16[256,1024]{1,0:T(8,128)(2,1)S(1)}, u32[]{:S(2)}, u32[]{:S(2)}) collective-permute-start(bf16[256,1024]{1,0:T(8,128)(2,1)S(1)} %copy-done.2), channel_id=1, source_target_pairs={{0,48},{8,56},{16,0},{24,8},{32,16},{40,24},{48,32},{56,40},{64,11... | collective-permute-start | bytes 1572872 | tf_op jit(solution)/shard_map/ppermute | solution.py:42
  68.6 21.4 %collective-permute-start.1 = (bf16[256,1024]{1,0:T(8,128)(2,1)S(1)}, bf16[256,1024]{1,0:T(8,128)(2,1)S(1)}, u32[]{:S(2)}, u32[]{:S(2)}) collective-permute-start(bf16[256,1024]{1,0:T(8,128)(2,1)S(1)} %copy-done.2), channel_id=1, source_target_pairs={{0,32},{8,40},{16,48},{24,56},{32,0},{40,8},{48,16},{56,24},{64,96... | collective-permute-start | bytes 1572872 | tf_op jit(solution)/shard_map/ppermute | solution.py:42
  69.2 26.0 %collective-permute-start = (bf16[256,1024]{1,0:T(8,128)(2,1)S(1)}, bf16[256,1024]{1,0:T(8,128)(2,1)S(1)}, u32[]{:S(2)}, u32[]{:S(2)}) collective-permute-start(bf16[256,1024]{1,0:T(8,128)(2,1)S(1)} %copy-done.2), channel_id=1, source_target_pairs={{0,16},{8,24},{16,32},{24,40},{32,48},{40,56},{48,0},{56,8},{64,80... | collective-permute-start | bytes 1572872 | tf_op jit(solution)/shard_map/ppermute | solution.py:42
  83.3 12.8 %collective-permute-start.11 = (bf16[256,1024]{1,0:T(8,128)(2,1)S(1)}, bf16[256,1024]{1,0:T(8,128)(2,1)S(1)}, u32[]{:S(2)}, u32[]{:S(2)}) collective-permute-start(bf16[256,1024]{1,0:T(8,128)(2,1)S(1)} %copy-done.2), channel_id=1, source_target_pairs={{0,192},{8,200},{16,208},{24,216},{32,224},{40,232},{48,240},{56,2... | collective-permute-start | bytes 1572872 | tf_op jit(solution)/shard_map/ppermute | solution.py:46
  85.6 28.4 %collective-permute-start.31 = (bf16[256,512]{1,0:T(8,128)(2,1)S(1)}, bf16[256,512]{1,0:T(8,128)(2,1)S(1)}, u32[]{:S(2)}, u32[]{:S(2)}) collective-permute-start(bf16[256,512]{1,0:T(8,128)(2,1)S(1)} %collective-permute-done.23.refs_17_), channel_id=1, source_target_pairs={{0,4},{1,5},{2,6},{3,7},{4,0},{5,1},{6,2},{7,3},{8,12},{9,13},{10,... | collective-permute-start | bytes 786440 | tf_op jit(solution)/shard_map/ppermute | solution.py:54
  89.8 24.2 %collective-permute-start.29 = (bf16[256,512]{1,0:T(8,128)(2,1)S(1)}, bf16[256,512]{1,0:T(8,128)(2,1)S(1)}, u32[]{:S(2)}, u32[]{:S(2)}) collective-permute-start(bf16[256,512]{1,0:T(8,128)(2,1)S(1)} %collective-permute-done.23.refs_17_), channel_id=1, source_target_pairs={{0,3},{1,0},{2,1},{3,2},{4,7},{5,4},{6,5},{7,6},{8,11},{9,8},{10,9... | collective-permute-start | bytes 786440 | tf_op jit(solution)/shard_map/ppermute | solution.py:58
  90.0 25.9 %collective-permute-start.27 = (bf16[256,512]{1,0:T(8,128)(2,1)S(1)}, bf16[256,512]{1,0:T(8,128)(2,1)S(1)}, u32[]{:S(2)}, u32[]{:S(2)}) collective-permute-start(bf16[256,512]{1,0:T(8,128)(2,1)S(1)} %collective-permute-done.23.refs_17_), channel_id=1, source_target_pairs={{0,2},{1,3},{2,0},{3,1},{4,6},{5,7},{6,4},{7,5},{8,10},{9,11},{10,... | collective-permute-start | bytes 786440 | tf_op jit(solution)/shard_map/ppermute | solution.py:58
  95.2 21.1 %collective-permute-start.25 = (bf16[256,512]{1,0:T(8,128)(2,1)S(1)}, bf16[256,512]{1,0:T(8,128)(2,1)S(1)}, u32[]{:S(2)}, u32[]{:S(2)}) collective-permute-start(bf16[256,512]{1,0:T(8,128)(2,1)S(1)} %collective-permute-done.23.refs_17_), channel_id=1, source_target_pairs={{0,1},{1,2},{2,3},{3,0},{4,5},{5,6},{6,7},{7,4},{8,9},{9,10},{10,1... | collective-permute-start | bytes 786440 | tf_op jit(solution)/shard_map/ppermute | solution.py:58
  96.2 23.5 %collective-permute-start.36 = (bf16[256,512]{1,0:T(8,128)(2,1)S(1)}, bf16[256,512]{1,0:T(8,128)(2,1)S(1)}, u32[]{:S(2)}, u32[]{:S(2)}) collective-permute-start(bf16[256,512]{1,0:T(8,128)(2,1)S(1)} %collective-permute-done.30.refs_24_), channel_id=1, source_target_pairs={{0,3},{1,0},{2,1},{3,2},{4,7},{5,4},{6,5},{7,6},{8,11},{9,8},{10,9... | collective-permute-start | bytes 786440 | tf_op jit(solution)/shard_map/ppermute | solution.py:58
  114.0 8.9 %collective-permute-start.34 = (bf16[256,512]{1,0:T(8,128)(2,1)S(1)}, bf16[256,512]{1,0:T(8,128)(2,1)S(1)}, u32[]{:S(2)}, u32[]{:S(2)}) collective-permute-start(bf16[256,512]{1,0:T(8,128)(2,1)S(1)} %collective-permute-done.30.refs_24_), channel_id=1, source_target_pairs={{0,2},{1,3},{2,0},{3,1},{4,6},{5,7},{6,4},{7,5},{8,10},{9,11},{10,... | collective-permute-start | bytes 786440 | tf_op jit(solution)/shard_map/ppermute | solution.py:58
  114.0 13.7 %collective-permute-start.32 = (bf16[256,512]{1,0:T(8,128)(2,1)S(1)}, bf16[256,512]{1,0:T(8,128)(2,1)S(1)}, u32[]{:S(2)}, u32[]{:S(2)}) collective-permute-start(bf16[256,512]{1,0:T(8,128)(2,1)S(1)} %collective-permute-done.30.refs_24_), channel_id=1, source_target_pairs={{0,1},{1,2},{2,3},{3,0},{4,5},{5,6},{6,7},{7,4},{8,9},{9,10},{10,1... | collective-permute-start | bytes 786440 | tf_op jit(solution)/shard_map/ppermute | solution.py:58
  115.9 11.8 %collective-permute-start.37 = (bf16[256,512]{1,0:T(8,128)(2,1)S(1)}, bf16[256,512]{1,0:T(8,128)(2,1)S(1)}, u32[]{:S(2)}, u32[]{:S(2)}) collective-permute-start(bf16[256,512]{1,0:T(8,128)(2,1)S(1)} %collective-permute-done.31.refs_25_), channel_id=1, source_target_pairs={{0,3},{1,0},{2,1},{3,2},{4,7},{5,4},{6,5},{7,6},{8,11},{9,8},{10,9... | collective-permute-start | bytes 786440 | tf_op jit(solution)/shard_map/ppermute | solution.py:58
  116.2 17.9 %collective-permute-start.35 = (bf16[256,512]{1,0:T(8,128)(2,1)S(1)}, bf16[256,512]{1,0:T(8,128)(2,1)S(1)}, u32[]{:S(2)}, u32[]{:S(2)}) collective-permute-start(bf16[256,512]{1,0:T(8,128)(2,1)S(1)} %collective-permute-done.31.refs_25_), channel_id=1, source_target_pairs={{0,2},{1,3},{2,0},{3,1},{4,6},{5,7},{6,4},{7,5},{8,10},{9,11},{10,... | collective-permute-start | bytes 786440 | tf_op jit(solution)/shard_map/ppermute | solution.py:58
  119.6 21.1 %collective-permute-start.10 = (bf16[256,1024]{1,0:T(8,128)(2,1)S(1)}, bf16[256,1024]{1,0:T(8,128)(2,1)S(1)}, u32[]{:S(2)}, u32[]{:S(2)}) collective-permute-start(bf16[256,1024]{1,0:T(8,128)(2,1)S(1)} %collective-permute-done.7.refs_8_), channel_id=1, source_target_pairs={{0,48},{8,56},{16,0},{24,8},{32,16},{40,24},{48,32},{56,40},{64,11... | collective-permute-start | bytes 1572872 | tf_op jit(solution)/shard_map/ppermute | solution.py:42
  122.9 18.9 %collective-permute-start.9 = (bf16[256,1024]{1,0:T(8,128)(2,1)S(1)}, bf16[256,1024]{1,0:T(8,128)(2,1)S(1)}, u32[]{:S(2)}, u32[]{:S(2)}) collective-permute-start(bf16[256,1024]{1,0:T(8,128)(2,1)S(1)} %collective-permute-done.7.refs_8_), channel_id=1, source_target_pairs={{0,32},{8,40},{16,48},{24,56},{32,0},{40,8},{48,16},{56,24},{64,96... | collective-permute-start | bytes 1572872 | tf_op jit(solution)/shard_map/ppermute | solution.py:42
  127.8 24.4 %collective-permute-start.8 = (bf16[256,1024]{1,0:T(8,128)(2,1)S(1)}, bf16[256,1024]{1,0:T(8,128)(2,1)S(1)}, u32[]{:S(2)}, u32[]{:S(2)}) collective-permute-start(bf16[256,1024]{1,0:T(8,128)(2,1)S(1)} %collective-permute-done.7.refs_8_), channel_id=1, source_target_pairs={{0,16},{8,24},{16,32},{24,40},{32,48},{40,56},{48,0},{56,8},{64,80... | collective-permute-start | bytes 1572872 | tf_op jit(solution)/shard_map/ppermute | solution.py:42
  127.8 26.2 %collective-permute-start.6 = (bf16[256,1024]{1,0:T(8,128)(2,1)S(1)}, bf16[256,1024]{1,0:T(8,128)(2,1)S(1)}, u32[]{:S(2)}, u32[]{:S(2)}) collective-permute-start(bf16[256,1024]{1,0:T(8,128)(2,1)S(1)} %collective-permute-done.3.refs_4_), channel_id=1, source_target_pairs={{0,48},{8,56},{16,0},{24,8},{32,16},{40,24},{48,32},{56,40},{64,11... | collective-permute-start | bytes 1572872 | tf_op jit(solution)/shard_map/ppermute | solution.py:42
  134.1 6.5 %collective-permute-start.33 = (bf16[256,512]{1,0:T(8,128)(2,1)S(1)}, bf16[256,512]{1,0:T(8,128)(2,1)S(1)}, u32[]{:S(2)}, u32[]{:S(2)}) collective-permute-start(bf16[256,512]{1,0:T(8,128)(2,1)S(1)} %collective-permute-done.31.refs_25_), channel_id=1, source_target_pairs={{0,1},{1,2},{2,3},{3,0},{4,5},{5,6},{6,7},{7,4},{8,9},{9,10},{10,1... | collective-permute-start | bytes 786440 | tf_op jit(solution)/shard_map/ppermute | solution.py:58
  140.6 17.5 %collective-permute-start.5 = (bf16[256,1024]{1,0:T(8,128)(2,1)S(1)}, bf16[256,1024]{1,0:T(8,128)(2,1)S(1)}, u32[]{:S(2)}, u32[]{:S(2)}) collective-permute-start(bf16[256,1024]{1,0:T(8,128)(2,1)S(1)} %collective-permute-done.3.refs_4_), channel_id=1, source_target_pairs={{0,32},{8,40},{16,48},{24,56},{32,0},{40,8},{48,16},{56,24},{64,96... | collective-permute-start | bytes 1572872 | tf_op jit(solution)/shard_map/ppermute | solution.py:42
  140.8 33.8 %collective-permute-start.4 = (bf16[256,1024]{1,0:T(8,128)(2,1)S(1)}, bf16[256,1024]{1,0:T(8,128)(2,1)S(1)}, u32[]{:S(2)}, u32[]{:S(2)}) collective-permute-start(bf16[256,1024]{1,0:T(8,128)(2,1)S(1)} %collective-permute-done.3.refs_4_), channel_id=1, source_target_pairs={{0,16},{8,24},{16,32},{24,40},{32,48},{40,56},{48,0},{56,8},{64,80... | collective-permute-start | bytes 1572872 | tf_op jit(solution)/shard_map/ppermute | solution.py:42
  141.8 34.6 %collective-permute-start.14 = (bf16[256,1024]{1,0:T(8,128)(2,1)S(1)}, bf16[256,1024]{1,0:T(8,128)(2,1)S(1)}, u32[]{:S(2)}, u32[]{:S(2)}) collective-permute-start(bf16[256,1024]{1,0:T(8,128)(2,1)S(1)} %collective-permute-done.11.refs_12_), channel_id=1, source_target_pairs={{0,48},{8,56},{16,0},{24,8},{32,16},{40,24},{48,32},{56,40},{64,11... | collective-permute-start | bytes 1572872 | tf_op jit(solution)/shard_map/ppermute | solution.py:42
  152.1 28.5 %collective-permute-start.13 = (bf16[256,1024]{1,0:T(8,128)(2,1)S(1)}, bf16[256,1024]{1,0:T(8,128)(2,1)S(1)}, u32[]{:S(2)}, u32[]{:S(2)}) collective-permute-start(bf16[256,1024]{1,0:T(8,128)(2,1)S(1)} %collective-permute-done.11.refs_12_), channel_id=1, source_target_pairs={{0,32},{8,40},{16,48},{24,56},{32,0},{40,8},{48,16},{56,24},{64,96... | collective-permute-start | bytes 1572872 | tf_op jit(solution)/shard_map/ppermute | solution.py:42
  154.0 40.5 %collective-permute-start.12 = (bf16[256,1024]{1,0:T(8,128)(2,1)S(1)}, bf16[256,1024]{1,0:T(8,128)(2,1)S(1)}, u32[]{:S(2)}, u32[]{:S(2)}) collective-permute-start(bf16[256,1024]{1,0:T(8,128)(2,1)S(1)} %collective-permute-done.11.refs_12_), channel_id=1, source_target_pairs={{0,16},{8,24},{16,32},{24,40},{32,48},{40,56},{48,0},{56,8},{64,80... | collective-permute-start | bytes 1572872 | tf_op jit(solution)/shard_map/ppermute | solution.py:42
  (26 other events, 1044.5 us)

commit v2 on v1

--- a/solution.py
+++ b/solution.py
@@ -13,7 +13,7 @@
 LANES = CHANS // 128
 PITCH = ROWS + 8
 HALF = CHANS // 2
-VMEM_LIMIT = 48 * 1024 * 1024
+VMEM_LIMIT = 16 * 1024 * 1024
 
 
 def ctx_pairs(move):
@@ -38,24 +38,51 @@
     return lax.ppermute(v, "ctx", ctx_pairs(lambda z, x, c: (z, x, 1 - c)))
 
 
-def shift_x(v, by):
-    return lax.ppermute(v, "ctx", ctx_pairs(lambda z, x, c: (z, (x + by) % X, c)))
-
-
-def shift_z(v, by):
-    return lax.ppermute(v, "ctx", ctx_pairs(lambda z, x, c: ((z + by) % ZL, x, c)))
-
-
-def ahead_z(v, by):
-    return lax.ppermute(v, "ctx", ctx_pairs(lambda z, x, c: (z + by, x, c) if z + by < ZL else None))
+def around_x(v, by):
+    return lax.ppermute(v, "ctx", ctx_pairs(lambda z, x, c: (z, (x + by * (1 - 2 * c)) % X, c)))
+
+
+def around_z(v, by):
+    return lax.ppermute(v, "ctx", ctx_pairs(lambda z, x, c: ((z + by * (1 - 2 * c)) % ZL, x, c)))
+
+
+def flip_x(v, bit):
+    return lax.ppermute(v, "ctx", ctx_pairs(lambda z, x, c: (z, x ^ bit, c)))
+
+
+def flip_z(v, bit):
+    return lax.ppermute(v, "ctx", ctx_pairs(lambda z, x, c: (z ^ bit, x, c)))
+
+
+def ahead_z(v, bit):
+    return lax.ppermute(v, "ctx", ctx_pairs(lambda z, x, c: None if z & bit else (z | bit, x, c)))
 
 
 def swap_zh(v):
     return lax.ppermute(v, "ch", ch_pairs(lambda h, y: (1 - h, y)))
 
 
-def shift_y(v, by):
-    return lax.ppermute(v, "ch", ch_pairs(lambda h, y: (h, (y + by) % Y)))
+def around_y(v, by):
+    pairs = []
+    for p in range(ZL * X * CORE):
+        step = by * (1 - 2 * (p % CORE))
+        for q, target in ch_pairs(lambda h, y: (h, (y + step) % Y)):
+            pairs.append((p * ZH * Y + q, p * ZH * Y + target))
+    return lax.ppermute(v, ("ctx", "ch"), pairs)
+
+
+def after(v, *earlier):
+    return lax.optimization_barrier((v,) + earlier)[0]
+
+
+class Lane:
+    def __init__(self, *earlier):
+        self.earlier = earlier
+
+    def send(self, op, v, *rest):
+        result = op(after(v, *self.earlier), *rest)
+        self.earlier = (result,)
+        return result
 
 
 def drive_kernel(proj, halo, taps, rates, drive, queries, ends, wide):
@@ -103,7 +130,7 @@
         ),
         scratch_shapes=[pltpu.VMEM((3, ROWS + 8, 128), F32)],
         compiler_params=pltpu.CompilerParams(vmem_limit_bytes=VMEM_LIMIT),
-        cost_estimate=pl.CostEstimate(flops=30_000_000, bytes_accessed=4_000_000, transcendentals=0),
+        cost_estimate=pl.CostEstimate(flops=1, bytes_accessed=1, transcendentals=0),
         name="drive_and_ends",
     )(proj, halo, taps, rates)
 
@@ -139,48 +166,42 @@
         out_shape=(jax.ShapeDtypeStruct((ROWS, HALF), BF16), jax.ShapeDtypeStruct((ROWS, HALF), BF16)),
         scratch_shapes=[pltpu.VMEM((LANES * PITCH, 128), F32)],
         compiler_params=pltpu.CompilerParams(vmem_limit_bytes=VMEM_LIMIT),
-        cost_estimate=pl.CostEstimate(flops=30_000_000, bytes_accessed=3_000_000, transcendentals=0),
+        cost_estimate=pl.CostEstimate(flops=1, bytes_accessed=1, transcendentals=0),
         name="response_and_gate",
     )(place, drive, queries, rates, weights, carried)
 
 
 def project_kernel(place, *refs):
-    weights, gated = refs[: ZL * X], refs[ZL * X : ZL * X + ZH * Y * 2]
-    mine, other, left, right, total, w_sem, g_sem = refs[ZL * X + ZH * Y * 2 :]
+    count_w, count_g = ZL * X, Y * 3
+    weights, gated = refs[:count_w], refs[count_w : count_w + count_g]
+    mine, other, left, total, sem = refs[count_w + count_g :]
     z, x, h, y = place[1], place[2], place[3], place[4]
-    copies_w, copies_g = [], []
-    for i in range(ZH):
-        for j in range(Y):
-            q = lax.rem(h + i, ZH) * Y + lax.rem(y + Y - j, Y)
-            columns = pl.ds(pl.multiple_of(q * HALF, HALF), HALF)
-            for part in range(2):
-                n = (i * Y + j) * 2 + part
-                copy = pltpu.make_async_copy(
-                    gated[n], left.at[pl.ds(part * ROWS, ROWS), columns], g_sem.at[n]
-                )
-                copy.start()
-                copies_g.append(copy)
+    sign = 1 - 2 * place[0]
+
+    def origin(at, slot, count):
+        return lax.rem(at + count + (0, -1, 1, 2)[slot] * sign, count)
+
+    copies = []
+
+    def put(n, q, first, rows):
+        columns = pl.ds(pl.multiple_of(q * HALF, HALF), HALF)
+        copy = pltpu.make_async_copy(gated[n], left.at[pl.ds(first, rows), columns], sem.at[n])
+        copy.start()
+        copies.append(copy)
+
+    for j in range(Y):
+        at = origin(y, j, Y)
+        put(3 * j, h * Y + at, 0, 2 * ROWS)
+        put(3 * j + 1, (1 - h) * Y + at, 0, ROWS)
+        put(3 * j + 2, (1 - h) * Y + at, ROWS, ROWS)
+    for copy in copies:
+        copy.wait()
     for s in range(ZL):
-        for r in range(X):
-            n = s * X + r
-            m = lax.rem(z + ZL - s, ZL) * X + lax.rem(x + X - r, X)
-            rows = pl.ds(pl.multiple_of(m * ROWS, ROWS), ROWS)
-            copy = pltpu.make_async_copy(weights[n], right.at[rows, :], w_sem.at[n])
-            copy.start()
-            copies_w.append(copy)
-    for copy in copies_g:
-        copy.wait()
-    depth = X * ROWS
-    for s in range(ZL):
-        for r in range(X):
-            copies_w[s * X + r].wait()
-        start = pl.multiple_of(lax.rem(z + ZL - s, ZL) * depth, depth)
+        blocks = [origin(z, s, ZL) * X + origin(x, r, X) for r in range(X)]
+        rows = jnp.concatenate([left[:, pl.ds(pl.multiple_of(m * ROWS, ROWS), ROWS)] for m in blocks], axis=1)
         for col in range(0, CHANS, 256):
-            product = jnp.dot(
-                left[:, pl.ds(start, depth)],
-                right[pl.ds(start, depth), col : col + 256],
-                preferred_element_type=F32,
-            )
+            shards = [weights[s * X + r][:, col : col + 256] for r in range(X)]
+            product = jnp.dot(rows, jnp.concatenate(shards, axis=0), preferred_element_type=F32)
             if s > 0:
                 product += total[:, col : col + 256]
             if s < ZL - 1:
@@ -191,48 +212,57 @@
 
 
 def project_call(place, weights, gated):
-    count = len(weights) + len(gated)
     whole = pl.BlockSpec(memory_space=pltpu.VMEM)
     return pl.pallas_call(
         project_kernel,
-        in_specs=[pl.BlockSpec(memory_space=pltpu.SMEM)] + [pl.BlockSpec(memory_space=pl.ANY)] * count,
+        in_specs=[pl.BlockSpec(memory_space=pltpu.SMEM)]
+        + [whole] * len(weights)
+        + [pl.BlockSpec(memory_space=pl.ANY)] * len(gated),
         out_specs=(whole, whole),
         out_shape=(jax.ShapeDtypeStruct((ROWS, CHANS), F32), jax.ShapeDtypeStruct((ROWS, CHANS), BF16)),
         scratch_shapes=[
             pltpu.VMEM((2 * ROWS, ZH * Y * HALF), BF16),
-            pltpu.VMEM((ZL * X * ROWS, CHANS), BF16),
             pltpu.VMEM((2 * ROWS, CHANS), F32),
-            pltpu.SemaphoreType.DMA((len(weights),)),
-            pltpu.SemaphoreType.DMA((len(gated),)),
+            pltpu.SemaphoreType.DMA((Y * 3,)),
         ],
-        compiler_params=pltpu.CompilerParams(vmem_limit_bytes=VMEM_LIMIT),
+        compiler_params=pltpu.CompilerParams(vmem_limit_bytes=28 * 1024 * 1024),
         cost_estimate=pl.CostEstimate(flops=4_300_000_000, bytes_accessed=14_000_000, transcendentals=0),
         name="projection",
     )(place, *weights, *gated)
 
 
-def carried_states(ends, rates, z, x, core):
-    def decays(steps):
-        return jnp.exp(-rates * (ROWS * steps).astype(F32))
-
-    one = jnp.int32(1)
-    sibling = swap_core(ends)
-    first = jnp.where(core == 0, ends, sibling)
-    second = jnp.where(core == 0, sibling, ends)
-    chip = decays(one) * first + second
-    arrived = [shift_x(chip, r) for r in range(1, X)]
-    group = decays(2 * (X - 1 - x)) * chip
-    before = jnp.zeros_like(chip)
-    for r in range(1, X):
-        origin = lax.rem(x + X - r, X)
-        group += decays(2 * (X - 1 - origin)) * arrived[r - 1]
-        before += jnp.where(r <= x, 1.0, 0.0) * decays(one * 2 * (r - 1)) * arrived[r - 1]
-    groups = [ahead_z(group, s) for s in range(1, ZL)]
-    far = groups[0]
-    for s in range(2, ZL):
-        far += decays(one * 2 * X * (s - 1)) * groups[s - 1]
-    into_chip = before + decays(2 * x) * far
-    return jnp.where(core == 0, into_chip, decays(one) * into_chip + first)
+def carried_states(ends, rates, z, x, core, before_x, before_z):
+    def decays(rows):
+        return jnp.exp(-rates * jnp.asarray(rows).astype(F32))
+
+    total, prefix, size, offset = ends, jnp.zeros_like(ends), ROWS, jnp.int32(0)
+    steps = (
+        (swap_core, core),
+        (functools.partial(flip_x, bit=1), x % 2),
+        (functools.partial(flip_x, bit=2), x // 2),
+        (functools.partial(flip_z, bit=1), z % 2),
+        (functools.partial(ahead_z, bit=2), z // 2),
+    )
+    arrived = []
+    for k, (exchange, upper) in enumerate(steps):
+        if k == 1:
+            total = after(total, *before_x)
+        if k == 3:
+            total = after(total, *before_z)
+        theirs = exchange(total)
+        arrived.append(theirs)
+        is_upper = upper == 1
+        prefix = prefix + jnp.where(is_upper, decays(offset) * theirs, 0.0)
+        total = decays(size) * jnp.where(is_upper, theirs, total) + jnp.where(is_upper, total, theirs)
+        offset = offset + size * upper
+        size = size * 2
+    return prefix, arrived[2], arrived[4]
+
+
+def around(lanes, op, v):
+    behind = lanes[0].send(op, v, 1)
+    ahead = lanes[1].send(op, v, -1)
+    return [v, behind, ahead, lanes[0].send(op, behind, 1)]
 
 
 def body(stream, projected, short_taps, decay_rates, residues, out_weight):
@@ -243,26 +273,40 @@
 
     proj = projected.transpose(1, 0, 2)
     halo = lax.ppermute(projected[ROWS - 2 :], "ctx", [(i, i + 1) for i in range(ZL * X * CORE - 1)])
+    z_behind = around_z(out_weight, 1)
+    own_behind, own_ahead = around_x(out_weight, 1), around_x(out_weight, -1)
     halo = halo.transpose(1, 0, 2).astype(F32)
     drive, queries, ends = drive_call(proj, halo, short_taps.reshape(9, CHANS), decay_rates)
 
-    shards = [out_weight] + [shift_z(out_weight, s) for s in range(1, ZL)]
-    weights = []
-    for s in range(ZL):
-        weights.append(shards[s])
-        weights += [shift_x(shards[s], r) for r in range(1, X)]
-
     rates3 = decay_rates.reshape(MODES, LANES, 128)
     weights3 = residues.reshape(MODES, LANES, 128)
-    carried = carried_states(ends, rates3, z, x, core)
+    z_ahead = around_z(after(out_weight, z_behind), -1)
+    carried, x_done, z_done = carried_states(ends, rates3, z, x, core, (own_behind, own_ahead), (z_ahead,))
+    z_far = around_z(after(z_behind, z_done), 1)
+
+    shards = (out_weight, z_behind, z_ahead, z_far)
+    first, second = Lane(x_done), Lane(x_done)
+    behind, ahead, far = [own_behind] + [None] * (ZL - 1), [own_ahead] + [None] * (ZL - 1), [None] * ZL
+    far[0] = first.send(around_x, behind[0], 1)
+    behind[1] = second.send(around_x, shards[1], 1)
+    carried = after(carried, far[0], behind[1])
+    ahead[1] = first.send(around_x, shards[1], -1)
+    far[1] = second.send(around_x, behind[1], 1)
+    behind[2] = first.send(around_x, shards[2], 1)
+    ahead[2] = second.send(around_x, shards[2], -1)
+    far[2] = first.send(around_x, behind[2], 1)
+    behind[3] = second.send(around_x, shards[3], 1)
+    ahead[3] = first.send(around_x, shards[3], -1)
+    far[3] = second.send(around_x, behind[3], 1)
+    weights = [v for s in range(ZL) for v in (shards[s], behind[s], ahead[s], far[s])]
+
     keep, send = response_call(place, drive, queries, rates3, weights3, carried)
     theirs = swap_core(send)
-
-    gated = []
-    for part in (keep, theirs):
-        across = swap_zh(part)
-        gated.append([[v] + [shift_y(v, j) for j in range(1, Y)] for v in (part, across)])
-    pieces = [gated[part][i][j] for i in range(ZH) for j in range(Y) for part in range(2)]
+    lane_h, lanes_y = Lane(), (Lane(), Lane())
+    across = [lane_h.send(swap_zh, part) for part in (keep, theirs)]
+    own = around((Lane(), Lane()), around_y, jnp.concatenate([keep, theirs], axis=0))
+    parts = [around(lanes_y if part == 0 else lanes_y[::-1], around_y, across[part]) for part in range(2)]
+    pieces = [v for j in range(Y) for v in (own[j], parts[0][j], parts[1][j])]
 
     mine, other = project_call(place, weights, pieces)
     summed = stream.astype(F32) + mine + swap_core(other).astype(F32)

time: 208 us -> 142 us (0.68)
  the two profiles are of different devices: /device:TPU:81 before, /device:TPU:35 now
where the time goes in v2:
time: 142 us; the launch traced here: 141 us
  waiting for transfers between devices  63.1 us (44%)
  starting transfers between devices  55.7 us (39%)
  Pallas kernels  13.3 us (9%)
  local copies, waits for them, and re-layouts  4.91 us (3%)
  other arithmetic  4.19 us (3%)
    ppermute x2, waiting for transfers between devices, swap_zh(): return lax.ppermute(v, 'ch', ch_pairs(lambda h, y: (1 - h, y)))  26.8 us
    ppermute x9, waiting for transfers between devices, around_y(): return lax.ppermute(v, ('ctx', 'ch'), pairs)  17.8 us
    ppermute x12, starting transfers between devices, around_x(): lax.ppermute(v, 'ctx', ctx_pairs(lambda z, x, c: (z, (x + by * (1 - 2 * c...  17.6 us
    ppermute x2, starting transfers between devices, swap_zh(): return lax.ppermute(v, 'ch', ch_pairs(lambda h, y: (1 - h, y)))  8.19 us
    ppermute x9, starting transfers between devices, around_y(): return lax.ppermute(v, ('ctx', 'ch'), pairs)  7.72 us
    ppermute x3, waiting for transfers between devices, around_z(): lax.ppermute(v, 'ctx', ctx_pairs(lambda z, x, c: ((z + by * (1 - 2 * c))...  7.53 us
    pallas_call x1, Pallas kernels, project_call(): pl.pallas_call(project_kernel, in_specs=[pl.BlockSpec(memory_space=pltpu....  7.19 us
    ppermute x1, starting transfers between devices, ahead_z(): lax.ppermute(v, 'ctx', ctx_pairs(lambda z, x, c: None if z & bit else (z...  5.43 us
  transfers between devices with their start and end apart: 34, of which 12 were waited for; matrix products, arithmetic and copies ran while one was open for 4% of the time, Pallas kernels for 4%

profile of v2, /device:TPU:35, one launch (start us, length us, event | category | flops | bytes accessed | tf_op | source)
XLA Modules:
  0.0 141.4 jit_solution(13058428003602598610)
XLA Ops:
  0.9 3.7 %collective-permute-start.2 = (bf16[2,3,1024]{2,0,1:T(2,128)(2,1)S(1)}, bf16[2,3,1024]{2,0,1:T(2,128)(2,1)S(1)}, u32[]{:S(2)}, u32[]{:S(2)}) collective-permute-start(bf16[2,3,1024]{2,0,1:T(2,128)(2,1)S(1)} %slice.3), channel_id=1, source_target_pairs={{0,8},{8,16},{16,24},{24,32},{32,40},{40,48},{48,56},{56,64},{64,7... | collective-permute-start | bytes 36872 | tf_op jit(solution)/shard_map/ppermute | solution.py:275
  6.9 1.4 copy-done
  9.2 2.8 %drive_and_ends.1 = (f32[2112,128]{1,0:T(8,128)S(1)}, f32[256,1024]{1,0:T(8,128)S(1)}, f32[16,8,128]{2,1,0:T(8,128)S(1)}) custom-call(bf16[3,256,1024]{2,1,0:T(8,128)(2,1)S(1)} %bitcast.18, f32[3,2,1024]{2,1,0:T(2,128)S(1)} %convert_bitcast_fusion.halo, f32[9,1024]{1,0:T(8,128)S(1)} %reshape.10.taps, f32[16,1024]{1,0:T(8,128)S(1)} %copy-done.1), custom_call_target="tpu_custom_call" | custom-call | flops 1 | bytes 1 | tf_op jit(solution)/shard_map/drive_and_ends/pallas_call | solution.py:124
  12.3 1.1 collective-permute-done.3
  13.4 4.9 %collective-permute-done.1.refs_2_ = bf16[256,1024]{1,0:T(8,128)(2,1)S(1)} collective-permute-done((bf16[256,1024]{1,0:T(8,128)(2,1)}, bf16[256,1024]{1,0:T(8,128)(2,1)S(1)}, u32[]{:S(2)}, u32[]{:S(2)}) %collective-permute-start.1) | collective-permute-done | bytes 524320 | tf_op jit(solution)/shard_map/ppermute | solution.py:42
  18.8 3.0 %collective-permute-done.4 = f32[16,8,128]{2,1,0:T(8,128)S(1)} collective-permute-done((f32[16,8,128]{2,1,0:T(8,128)S(1)}, f32[16,8,128]{2,1,0:T(8,128)S(1)}, u32[]{:S(2)}, u32[]{:S(2)}) %collective-permute-start.4) | collective-permute-done | bytes 65568 | tf_op jit(solution)/shard_map/ppermute | solution.py:50
  21.8 3.0 %collective-permute-start.5 = (f32[16,8,128]{2,1,0:T(8,128)S(1)}, f32[16,8,128]{2,1,0:T(8,128)S(1)}, u32[]{:S(2)}, u32[]{:S(2)}) collective-permute-start(f32[16,8,128]{2,1,0:T(8,128)S(1)} %select_add_fusion.3), channel_id=1, source_target_pairs={{0,32},{8,40},{16,48},{24,56},{32,0},{40,8},{48,16},{56,24},{64,96... | collective-permute-start | bytes 196616 | tf_op jit(solution)/shard_map/ppermute | solution.py:50
  24.8 2.8 %collective-permute-start.11 = (bf16[256,1024]{1,0:T(8,128)(2,1)S(1)}, bf16[256,1024]{1,0:T(8,128)(2,1)}, u32[]{:S(2)}, u32[]{:S(2)}) collective-permute-start(bf16[256,1024]{1,0:T(8,128)(2,1)S(1)} %copy-done.3), channel_id=1, source_target_pairs={{0,192},{8,72},{16,208},{24,88},{32,224},{40,104},{48,240},{56,120... | collective-permute-start | bytes 1572872 | tf_op jit(solution)/shard_map/ppermute | solution.py:46
  27.5 2.1 %collective-permute-start.6 = (bf16[256,1024]{1,0:T(8,128)(2,1)}, bf16[256,1024]{1,0:T(8,128)(2,1)}, u32[]{:S(2)}, u32[]{:S(2)}) collective-permute-start(bf16[256,1024]{1,0:T(8,128)(2,1)} %collective-permute-done.refs_1_), channel_id=1, source_target_pairs={{0,16},{8,56},{16,32},{24,8},{32,48},{40,24},{48,0},{56,40},{64,80... | collective-permute-start | bytes 1572872 | tf_op jit(solution)/shard_map/ppermute | solution.py:42
  29.7 1.4 %collective-permute-start.8 = (bf16[256,1024]{1,0:T(8,128)(2,1)}, bf16[256,1024]{1,0:T(8,128)(2,1)}, u32[]{:S(2)}, u32[]{:S(2)}) collective-permute-start(bf16[256,1024]{1,0:T(8,128)(2,1)} %collective-permute-done.7.refs_4_), channel_id=1, source_target_pairs={{0,16},{8,56},{16,32},{24,8},{32,48},{40,24},{48,0},{56,40},{64,80... | collective-permute-start | bytes 1572872 | tf_op jit(solution)/shard_map/ppermute | solution.py:42
  31.8 7.5 %collective-permute-done.11.refs_8_ = bf16[256,1024]{1,0:T(8,128)(2,1)} collective-permute-done((bf16[256,1024]{1,0:T(8,128)(2,1)S(1)}, bf16[256,1024]{1,0:T(8,128)(2,1)}, u32[]{:S(2)}, u32[]{:S(2)}) %collective-permute-start.11) | collective-permute-done | bytes 524320 | tf_op jit(solution)/shard_map/ppermute | solution.py:46
  39.3 1.5 %collective-permute-start.15 = (f32[16,8,128]{2,1,0:T(8,128)}, f32[16,8,128]{2,1,0:T(8,128)S(1)}, u32[]{:S(2)}, u32[]{:S(2)}) collective-permute-start(f32[16,8,128]{2,1,0:T(8,128)} %select_add_fusion.2), channel_id=1, source_target_pairs={{0,64},{8,72},{16,80},{24,88},{32,96},{40,104},{48,112},{56,120},{... | collective-permute-start | bytes 196616 | tf_op jit(solution)/shard_map/ppermute | solution.py:54
  41.8 2.1 %collective-permute-start.10 = (bf16[256,1024]{1,0:T(8,128)(2,1)}, bf16[256,1024]{1,0:T(8,128)(2,1)}, u32[]{:S(2)}, u32[]{:S(2)}) collective-permute-start(bf16[256,1024]{1,0:T(8,128)(2,1)} %collective-permute-done.8.refs_5_), channel_id=1, source_target_pairs={{0,16},{8,56},{16,32},{24,8},{32,48},{40,24},{48,0},{56,40},{64,80... | collective-permute-start | bytes 1572872 | tf_op jit(solution)/shard_map/ppermute | solution.py:42
  43.9 1.5 %select_add_fusion.1 = f32[16,8,128]{2,1,0:T(8,128)} fusion(f32[16,8,128]{2,1,0:T(8,128)} %select_add_fusion.2, f32[16,8,128]{2,1,0:T(8,128)S(1)} %collective-permute-done.15, pred[]{:T(512)S(6)} %eq.23, f32[2,8,8,128]{3,2,1,0:T(8,128)S(1)} %copy.7), kind=kLoop, calls=%fused_computation.2 | loop fusion | flops 98304 | bytes 262145 | tf_op jit(solution)/shard_map/add | solution.py:256
  45.5 5.4 %collective-permute-start.16 = (f32[16,8,128]{2,1,0:T(8,128)}, f32[16,8,128]{2,1,0:T(8,128)}, u32[]{:S(2)}, u32[]{:S(2)}) collective-permute-start(f32[16,8,128]{2,1,0:T(8,128)} %select_add_fusion.1), channel_id=1, source_target_pairs={{0,128},{8,136},{16,144},{24,152},{32,160},{40,168},{48,176},{56,1... | collective-permute-start | bytes 196616 | tf_op jit(solution)/shard_map/ppermute | solution.py:58
  53.2 2.2 %collective-permute-start.12 = (bf16[256,1024]{1,0:T(8,128)(2,1)}, bf16[256,1024]{1,0:T(8,128)(2,1)S(1)}, u32[]{:S(2)}, u32[]{:S(2)}) collective-permute-start(bf16[256,1024]{1,0:T(8,128)(2,1)} %collective-permute-done.11.refs_8_), channel_id=1, source_target_pairs={{0,16},{8,56},{16,32},{24,8},{32,48},{40,24},{48,0},{56,40},{64,80... | collective-permute-start | bytes 1572872 | tf_op jit(solution)/shard_map/ppermute | solution.py:42
  55.4 2.3 %collective-permute-start.13 = (bf16[256,1024]{1,0:T(8,128)(2,1)}, bf16[256,1024]{1,0:T(8,128)(2,1)S(1)}, u32[]{:S(2)}, u32[]{:S(2)}) collective-permute-start(bf16[256,1024]{1,0:T(8,128)(2,1)} %collective-permute-done.11.refs_8_), channel_id=1, source_target_pairs={{0,48},{8,24},{16,0},{24,40},{32,16},{40,56},{48,32},{56,8},{64,11... | collective-permute-start | bytes 1572872 | tf_op jit(solution)/shard_map/ppermute | solution.py:42
  57.7 3.3 %response_and_gate.1 = (bf16[256,512]{1,0:T(8,128)(2,1)S(1)}, bf16[256,512]{1,0:T(8,128)(2,1)S(1)}) custom-call(s32[5]{0:T(128)S(1)} %stack.23.place, f32[2112,128]{1,0:T(8,128)S(1)} %get-tuple-element.48.drive, f32[256,1024]{1,0:T(8,128)S(1)} %get-tuple-element.49.queries, f32[16,8,128]{2,1,0:T(8,128)S(1)} %bitcast.17, f32[16,8,128]{2,1,0:T(8,128)S(1)} %bitcast.19, ...), custom_call_target="tpu_custom_call" | custom-call | flops 1 | bytes 1 | tf_op jit(solution)/shard_map/response_and_gate/pallas_call | solution.py:163
  60.9 7.1 %collective-permute-start.22 = (bf16[256,512]{1,0:T(8,128)(2,1)S(1)}, bf16[256,512]{1,0:T(8,128)(2,1)S(1)}, u32[]{:S(2)}, u32[]{:S(2)}) collective-permute-start(bf16[256,512]{1,0:T(8,128)(2,1)S(1)} %get-tuple-element.51), channel_id=1, source_target_pairs={{0,4},{1,5},{2,6},{3,7},{4,0},{5,1},{6,2},{7,3},{8,12},{9,13},{10,... | collective-permute-start | bytes 786440 | tf_op jit(solution)/shard_map/ppermute | solution.py:62
  68.0 2.3 %collective-permute-start.21 = (bf16[256,512]{1,0:T(8,128)(2,1)S(1)}, bf16[256,512]{1,0:T(8,128)(2,1)S(1)}, u32[]{:S(2)}, u32[]{:S(2)}) collective-permute-start(bf16[256,512]{1,0:T(8,128)(2,1)S(1)} %get-tuple-element.52), channel_id=1, source_target_pairs={{0,8},{8,0},{16,24},{24,16},{32,40},{40,32},{48,56},{56,48},{64,72... | collective-permute-start | bytes 786440 | tf_op jit(solution)/shard_map/ppermute | solution.py:38
  70.3 11.6 %collective-permute-done.22.refs_17_ = bf16[256,512]{1,0:T(8,128)(2,1)S(1)} collective-permute-done((bf16[256,512]{1,0:T(8,128)(2,1)S(1)}, bf16[256,512]{1,0:T(8,128)(2,1)S(1)}, u32[]{:S(2)}, u32[]{:S(2)}) %collective-permute-start.22) | collective-permute-done | bytes 262176 | tf_op jit(solution)/shard_map/ppermute | solution.py:62
  81.9 2.7 %collective-permute-start.25 = (bf16[256,512]{1,0:T(8,128)(2,1)S(1)}, bf16[256,512]{1,0:T(8,128)(2,1)S(1)}, u32[]{:S(2)}, u32[]{:S(2)}) collective-permute-start(bf16[256,512]{1,0:T(8,128)(2,1)S(1)} %collective-permute-done.22.refs_17_), channel_id=1, source_target_pairs={{0,1},{1,2},{2,3},{3,0},{4,5},{5,6},{6,7},{7,4},{8,11},{9,8},{10,9... | collective-permute-start | bytes 786440 | tf_op jit(solution)/shard_map/ppermute | solution.py:71
  84.8 2.7 %collective-permute-start.24 = (bf16[512,512]{1,0:T(8,128)(2,1)S(1)}, bf16[512,512]{1,0:T(8,128)(2,1)S(1)}, u32[]{:S(2)}, u32[]{:S(2)}) collective-permute-start(bf16[512,512]{1,0:T(8,128)(2,1)S(1)} %constant_dynamic-update-slice_fusion.refs_16_), channel_id=1, source_target_pairs={{0,1},{1,2},{2,3},{3,0},{4,5},{5,6},{6,7},{7,4},{8,11},{9,8},{10,9... | collective-permute-start | bytes 1572872 | tf_op jit(solution)/shard_map/ppermute | solution.py:71
  87.5 4.8 %collective-permute-start.18 = (bf16[256,1024]{1,0:T(8,128)(2,1)S(1)}, bf16[256,1024]{1,0:T(8,128)(2,1)S(1)}, u32[]{:S(2)}, u32[]{:S(2)}) collective-permute-start(bf16[256,1024]{1,0:T(8,128)(2,1)S(1)} %collective-permute-done.17.refs_12_), channel_id=1, source_target_pairs={{0,16},{8,56},{16,32},{24,8},{32,48},{40,24},{48,0},{56,40},{64,80... | collective-permute-start | bytes 1572872 | tf_op jit(solution)/shard_map/ppermute | solution.py:42
  92.3 1.1 collective-permute-start.23
  94.2 15.2 %collective-permute-done.23.refs_18_ = bf16[256,512]{1,0:T(8,128)(2,1)S(1)} collective-permute-done((bf16[256,512]{1,0:T(8,128)(2,1)S(1)}, bf16[256,512]{1,0:T(8,128)(2,1)S(1)}, u32[]{:S(2)}, u32[]{:S(2)}) %collective-permute-start.23) | collective-permute-done | bytes 262176 | tf_op jit(solution)/shard_map/ppermute | solution.py:62
  110.3 4.7 %collective-permute-done.29.refs_26_ = bf16[256,512]{1,0:T(8,128)(2,1)S(1)} collective-permute-done((bf16[256,512]{1,0:T(8,128)(2,1)S(1)}, bf16[256,512]{1,0:T(8,128)(2,1)S(1)}, u32[]{:S(2)}, u32[]{:S(2)}) %collective-permute-start.29) | collective-permute-done | bytes 262176 | tf_op jit(solution)/shard_map/ppermute | solution.py:71
  115.0 2.8 %collective-permute-done.27.refs_21_ = bf16[256,512]{1,0:T(8,128)(2,1)S(1)} collective-permute-done((bf16[256,512]{1,0:T(8,128)(2,1)S(1)}, bf16[256,512]{1,0:T(8,128)(2,1)S(1)}, u32[]{:S(2)}, u32[]{:S(2)}) %collective-permute-start.27) | collective-permute-done | bytes 262176 | tf_op jit(solution)/shard_map/ppermute | solution.py:71
  119.2 9.6 %collective-permute-done.32.refs_27_ = bf16[256,512]{1,0:T(8,128)(2,1)S(1)} collective-permute-done((bf16[256,512]{1,0:T(8,128)(2,1)S(1)}, bf16[256,512]{1,0:T(8,128)(2,1)S(1)}, u32[]{:S(2)}, u32[]{:S(2)}) %collective-permute-start.32) | collective-permute-done | bytes 262176 | tf_op jit(solution)/shard_map/ppermute | solution.py:71
  128.8 7.2 %projection.1 = (f32[256,1024]{1,0:T(8,128)S(1)}, bf16[256,1024]{1,0:T(8,128)(2,1)S(1)}) custom-call(s32[5]{0:T(128)S(1)} %stack.23.place, bf16[256,1024]{1,0:T(8,128)(2,1)S(1)} %copy-done.3, bf16[256,1024]{1,0:T(8,128)(2,1)} %collective-permute-done.refs_1_, bf16[256,1024]{1,0:T(8,128)(2,1)S(1)} %collective-permute-done.1.refs_2_, ...), custom_call_target="tpu_custom_call" | custom-call | flops 4300000256 | bytes 14000000 | tf_op jit(solution)/shard_map/projection/pallas_call | solution.py:216
  136.0 2.8 %collective-permute-start.33 = (bf16[256,1024]{1,0:T(8,128)(2,1)S(1)}, bf16[256,1024]{1,0:T(8,128)(2,1)S(1)}, u32[]{:S(2)}, u32[]{:S(2)}) collective-permute-start(bf16[256,1024]{1,0:T(8,128)(2,1)S(1)} %get-tuple-element.60), channel_id=1, source_target_pairs={{0,8},{8,0},{16,24},{24,16},{32,40},{40,32},{48,56},{56,48},{64,72... | collective-permute-start | bytes 1572872 | tf_op jit(solution)/shard_map/ppermute | solution.py:38
  138.9 1.5 %collective-permute-done.33 = bf16[256,1024]{1,0:T(8,128)(2,1)S(1)} collective-permute-done((bf16[256,1024]{1,0:T(8,128)(2,1)S(1)}, bf16[256,1024]{1,0:T(8,128)(2,1)S(1)}, u32[]{:S(2)}, u32[]{:S(2)}) %collective-permute-start.33) | collective-permute-done | bytes 524320 | tf_op jit(solution)/shard_map/ppermute | solution.py:38
  (65 shorter events, 13.0 us)
Async XLA Ops:
  0.9 6.1 %collective-permute-start.2 = (bf16[2,3,1024]{2,0,1:T(2,128)(2,1)S(1)}, bf16[2,3,1024]{2,0,1:T(2,128)(2,1)S(1)}, u32[]{:S(2)}, u32[]{:S(2)}) collective-permute-start(bf16[2,3,1024]{2,0,1:T(2,128)(2,1)S(1)} %slice.3), channel_id=1, source_target_pairs={{0,8},{8,16},{16,24},{24,32},{32,40},{40,48},{48,56},{56,64},{64,7... | collective-permute-start | bytes 36872 | tf_op jit(solution)/shard_map/ppermute | solution.py:275
  4.5 13.7 %collective-permute-start.1 = (bf16[256,1024]{1,0:T(8,128)(2,1)}, bf16[256,1024]{1,0:T(8,128)(2,1)S(1)}, u32[]{:S(2)}, u32[]{:S(2)}) collective-permute-start(bf16[256,1024]{1,0:T(8,128)(2,1)} %refs_0_.1), channel_id=1, source_target_pairs={{0,48},{8,24},{16,0},{24,40},{32,16},{40,56},{48,32},{56,8},{64,11... | collective-permute-start | bytes 1572872 | tf_op jit(solution)/shard_map/ppermute | solution.py:42
  5.5 12.7 %collective-permute-start = (bf16[256,1024]{1,0:T(8,128)(2,1)}, bf16[256,1024]{1,0:T(8,128)(2,1)}, u32[]{:S(2)}, u32[]{:S(2)}) collective-permute-start(bf16[256,1024]{1,0:T(8,128)(2,1)} %refs_0_.1), channel_id=1, source_target_pairs={{0,16},{8,56},{16,32},{24,8},{32,48},{40,24},{48,0},{56,40},{64,80... | collective-permute-start | bytes 1572872 | tf_op jit(solution)/shard_map/ppermute | solution.py:42
  12.1 12.6 %collective-permute-start.7 = (bf16[256,1024]{1,0:T(8,128)(2,1)S(1)}, bf16[256,1024]{1,0:T(8,128)(2,1)}, u32[]{:S(2)}, u32[]{:S(2)}) collective-permute-start(bf16[256,1024]{1,0:T(8,128)(2,1)S(1)} %copy-done.3), channel_id=1, source_target_pairs={{0,64},{8,200},{16,80},{24,216},{32,96},{40,232},{48,112},{56,248}... | collective-permute-start | bytes 1572872 | tf_op jit(solution)/shard_map/ppermute | solution.py:46
  21.8 5.7 %collective-permute-start.5 = (f32[16,8,128]{2,1,0:T(8,128)S(1)}, f32[16,8,128]{2,1,0:T(8,128)S(1)}, u32[]{:S(2)}, u32[]{:S(2)}) collective-permute-start(f32[16,8,128]{2,1,0:T(8,128)S(1)} %select_add_fusion.3), channel_id=1, source_target_pairs={{0,32},{8,40},{16,48},{24,56},{32,0},{40,8},{48,16},{56,24},{64,96... | collective-permute-start | bytes 196616 | tf_op jit(solution)/shard_map/ppermute | solution.py:50
  24.8 14.5 %collective-permute-start.11 = (bf16[256,1024]{1,0:T(8,128)(2,1)S(1)}, bf16[256,1024]{1,0:T(8,128)(2,1)}, u32[]{:S(2)}, u32[]{:S(2)}) collective-permute-start(bf16[256,1024]{1,0:T(8,128)(2,1)S(1)} %copy-done.3), channel_id=1, source_target_pairs={{0,192},{8,72},{16,208},{24,88},{32,224},{40,104},{48,240},{56,120... | collective-permute-start | bytes 1572872 | tf_op jit(solution)/shard_map/ppermute | solution.py:46
  27.5 13.2 %collective-permute-start.6 = (bf16[256,1024]{1,0:T(8,128)(2,1)}, bf16[256,1024]{1,0:T(8,128)(2,1)}, u32[]{:S(2)}, u32[]{:S(2)}) collective-permute-start(bf16[256,1024]{1,0:T(8,128)(2,1)} %collective-permute-done.refs_1_), channel_id=1, source_target_pairs={{0,16},{8,56},{16,32},{24,8},{32,48},{40,24},{48,0},{56,40},{64,80... | collective-permute-start | bytes 1572872 | tf_op jit(solution)/shard_map/ppermute | solution.py:42
  29.7 12.1 %collective-permute-start.8 = (bf16[256,1024]{1,0:T(8,128)(2,1)}, bf16[256,1024]{1,0:T(8,128)(2,1)}, u32[]{:S(2)}, u32[]{:S(2)}) collective-permute-start(bf16[256,1024]{1,0:T(8,128)(2,1)} %collective-permute-done.7.refs_4_), channel_id=1, source_target_pairs={{0,16},{8,56},{16,32},{24,8},{32,48},{40,24},{48,0},{56,40},{64,80... | collective-permute-start | bytes 1572872 | tf_op jit(solution)/shard_map/ppermute | solution.py:42
  39.3 4.7 %collective-permute-start.15 = (f32[16,8,128]{2,1,0:T(8,128)}, f32[16,8,128]{2,1,0:T(8,128)S(1)}, u32[]{:S(2)}, u32[]{:S(2)}) collective-permute-start(f32[16,8,128]{2,1,0:T(8,128)} %select_add_fusion.2), channel_id=1, source_target_pairs={{0,64},{8,72},{16,80},{24,88},{32,96},{40,104},{48,112},{56,120},{... | collective-permute-start | bytes 196616 | tf_op jit(solution)/shard_map/ppermute | solution.py:54
  40.8 12.4 %collective-permute-start.9 = (bf16[256,1024]{1,0:T(8,128)(2,1)}, bf16[256,1024]{1,0:T(8,128)(2,1)}, u32[]{:S(2)}, u32[]{:S(2)}) collective-permute-start(bf16[256,1024]{1,0:T(8,128)(2,1)} %collective-permute-done.7.refs_4_), channel_id=1, source_target_pairs={{0,48},{8,24},{16,0},{24,40},{32,16},{40,56},{48,32},{56,8},{64,11... | collective-permute-start | bytes 1572872 | tf_op jit(solution)/shard_map/ppermute | solution.py:42
  41.8 13.6 %collective-permute-start.10 = (bf16[256,1024]{1,0:T(8,128)(2,1)}, bf16[256,1024]{1,0:T(8,128)(2,1)}, u32[]{:S(2)}, u32[]{:S(2)}) collective-permute-start(bf16[256,1024]{1,0:T(8,128)(2,1)} %collective-permute-done.8.refs_5_), channel_id=1, source_target_pairs={{0,16},{8,56},{16,32},{24,8},{32,48},{40,24},{48,0},{56,40},{64,80... | collective-permute-start | bytes 1572872 | tf_op jit(solution)/shard_map/ppermute | solution.py:42
  45.5 6.7 %collective-permute-start.16 = (f32[16,8,128]{2,1,0:T(8,128)}, f32[16,8,128]{2,1,0:T(8,128)}, u32[]{:S(2)}, u32[]{:S(2)}) collective-permute-start(f32[16,8,128]{2,1,0:T(8,128)} %select_add_fusion.1), channel_id=1, source_target_pairs={{0,128},{8,136},{16,144},{24,152},{32,160},{40,168},{48,176},{56,1... | collective-permute-start | bytes 196616 | tf_op jit(solution)/shard_map/ppermute | solution.py:58
  52.2 35.3 %collective-permute-start.17 = (bf16[256,1024]{1,0:T(8,128)(2,1)}, bf16[256,1024]{1,0:T(8,128)(2,1)S(1)}, u32[]{:S(2)}, u32[]{:S(2)}) collective-permute-start(bf16[256,1024]{1,0:T(8,128)(2,1)} %collective-permute-done.7.refs_4_), channel_id=1, source_target_pairs={{0,64},{8,200},{16,80},{24,216},{32,96},{40,232},{48,112},{56,248}... | collective-permute-start | bytes 1572872 | tf_op jit(solution)/shard_map/ppermute | solution.py:46
  53.2 31.6 %collective-permute-start.12 = (bf16[256,1024]{1,0:T(8,128)(2,1)}, bf16[256,1024]{1,0:T(8,128)(2,1)S(1)}, u32[]{:S(2)}, u32[]{:S(2)}) collective-permute-start(bf16[256,1024]{1,0:T(8,128)(2,1)} %collective-permute-done.11.refs_8_), channel_id=1, source_target_pairs={{0,16},{8,56},{16,32},{24,8},{32,48},{40,24},{48,0},{56,40},{64,80... | collective-permute-start | bytes 1572872 | tf_op jit(solution)/shard_map/ppermute | solution.py:42
  55.4 32.2 %collective-permute-start.13 = (bf16[256,1024]{1,0:T(8,128)(2,1)}, bf16[256,1024]{1,0:T(8,128)(2,1)S(1)}, u32[]{:S(2)}, u32[]{:S(2)}) collective-permute-start(bf16[256,1024]{1,0:T(8,128)(2,1)} %collective-permute-done.11.refs_8_), channel_id=1, source_target_pairs={{0,48},{8,24},{16,0},{24,40},{32,16},{40,56},{48,32},{56,8},{64,11... | collective-permute-start | bytes 1572872 | tf_op jit(solution)/shard_map/ppermute | solution.py:42
  60.9 21.0 %collective-permute-start.22 = (bf16[256,512]{1,0:T(8,128)(2,1)S(1)}, bf16[256,512]{1,0:T(8,128)(2,1)S(1)}, u32[]{:S(2)}, u32[]{:S(2)}) collective-permute-start(bf16[256,512]{1,0:T(8,128)(2,1)S(1)} %get-tuple-element.51), channel_id=1, source_target_pairs={{0,4},{1,5},{2,6},{3,7},{4,0},{5,1},{6,2},{7,3},{8,12},{9,13},{10,... | collective-permute-start | bytes 786440 | tf_op jit(solution)/shard_map/ppermute | solution.py:62
  68.0 16.7 %collective-permute-start.21 = (bf16[256,512]{1,0:T(8,128)(2,1)S(1)}, bf16[256,512]{1,0:T(8,128)(2,1)S(1)}, u32[]{:S(2)}, u32[]{:S(2)}) collective-permute-start(bf16[256,512]{1,0:T(8,128)(2,1)S(1)} %get-tuple-element.52), channel_id=1, source_target_pairs={{0,8},{8,0},{16,24},{24,16},{32,40},{40,32},{48,56},{56,48},{64,72... | collective-permute-start | bytes 786440 | tf_op jit(solution)/shard_map/ppermute | solution.py:38
  81.9 10.4 %collective-permute-start.25 = (bf16[256,512]{1,0:T(8,128)(2,1)S(1)}, bf16[256,512]{1,0:T(8,128)(2,1)S(1)}, u32[]{:S(2)}, u32[]{:S(2)}) collective-permute-start(bf16[256,512]{1,0:T(8,128)(2,1)S(1)} %collective-permute-done.22.refs_17_), channel_id=1, source_target_pairs={{0,1},{1,2},{2,3},{3,0},{4,5},{5,6},{6,7},{7,4},{8,11},{9,8},{10,9... | collective-permute-start | bytes 786440 | tf_op jit(solution)/shard_map/ppermute | solution.py:71
  84.7 9.6 %collective-permute-start.26 = (bf16[256,512]{1,0:T(8,128)(2,1)S(1)}, bf16[256,512]{1,0:T(8,128)(2,1)S(1)}, u32[]{:S(2)}, u32[]{:S(2)}) collective-permute-start(bf16[256,512]{1,0:T(8,128)(2,1)S(1)} %collective-permute-done.22.refs_17_), channel_id=1, source_target_pairs={{0,3},{1,0},{2,1},{3,2},{4,7},{5,4},{6,5},{7,6},{8,9},{9,10},{10,1... | collective-permute-start | bytes 786440 | tf_op jit(solution)/shard_map/ppermute | solution.py:71
  84.8 24.6 %collective-permute-start.24 = (bf16[512,512]{1,0:T(8,128)(2,1)S(1)}, bf16[512,512]{1,0:T(8,128)(2,1)S(1)}, u32[]{:S(2)}, u32[]{:S(2)}) collective-permute-start(bf16[512,512]{1,0:T(8,128)(2,1)S(1)} %constant_dynamic-update-slice_fusion.refs_16_), channel_id=1, source_target_pairs={{0,1},{1,2},{2,3},{3,0},{4,5},{5,6},{6,7},{7,4},{8,11},{9,8},{10,9... | collective-permute-start | bytes 1572872 | tf_op jit(solution)/shard_map/ppermute | solution.py:71
  87.5 21.9 %collective-permute-start.14 = (bf16[256,1024]{1,0:T(8,128)(2,1)S(1)}, bf16[256,1024]{1,0:T(8,128)(2,1)S(1)}, u32[]{:S(2)}, u32[]{:S(2)}) collective-permute-start(bf16[256,1024]{1,0:T(8,128)(2,1)S(1)} %collective-permute-done.12.refs_9_), channel_id=1, source_target_pairs={{0,16},{8,56},{16,32},{24,8},{32,48},{40,24},{48,0},{56,40},{64,80... | collective-permute-start | bytes 1572872 | tf_op jit(solution)/shard_map/ppermute | solution.py:42
  87.5 22.6 %collective-permute-start.18 = (bf16[256,1024]{1,0:T(8,128)(2,1)S(1)}, bf16[256,1024]{1,0:T(8,128)(2,1)S(1)}, u32[]{:S(2)}, u32[]{:S(2)}) collective-permute-start(bf16[256,1024]{1,0:T(8,128)(2,1)S(1)} %collective-permute-done.17.refs_12_), channel_id=1, source_target_pairs={{0,16},{8,56},{16,32},{24,8},{32,48},{40,24},{48,0},{56,40},{64,80... | collective-permute-start | bytes 1572872 | tf_op jit(solution)/shard_map/ppermute | solution.py:42
  92.3 17.1 %collective-permute-start.23 = (bf16[256,512]{1,0:T(8,128)(2,1)S(1)}, bf16[256,512]{1,0:T(8,128)(2,1)S(1)}, u32[]{:S(2)}, u32[]{:S(2)}) collective-permute-start(bf16[256,512]{1,0:T(8,128)(2,1)S(1)} %collective-permute-done.21), channel_id=1, source_target_pairs={{0,4},{1,5},{2,6},{3,7},{4,0},{5,1},{6,2},{7,3},{8,12},{9,13},{10,... | collective-permute-start | bytes 786440 | tf_op jit(solution)/shard_map/ppermute | solution.py:62
  94.2 24.5 %collective-permute-start.28 = (bf16[512,512]{1,0:T(8,128)(2,1)S(1)}, bf16[512,512]{1,0:T(8,128)(2,1)S(1)}, u32[]{:S(2)}, u32[]{:S(2)}) collective-permute-start(bf16[512,512]{1,0:T(8,128)(2,1)S(1)} %constant_dynamic-update-slice_fusion.refs_16_), channel_id=1, source_target_pairs={{0,3},{1,0},{2,1},{3,2},{4,7},{5,4},{6,5},{7,6},{8,9},{9,10},{10,1... | collective-permute-start | bytes 1572872 | tf_op jit(solution)/shard_map/ppermute | solution.py:71
  109.4 5.5 %collective-permute-start.29 = (bf16[256,512]{1,0:T(8,128)(2,1)S(1)}, bf16[256,512]{1,0:T(8,128)(2,1)S(1)}, u32[]{:S(2)}, u32[]{:S(2)}) collective-permute-start(bf16[256,512]{1,0:T(8,128)(2,1)S(1)} %collective-permute-done.25.refs_20_), channel_id=1, source_target_pairs={{0,1},{1,2},{2,3},{3,0},{4,5},{5,6},{6,7},{7,4},{8,11},{9,8},{10,9... | collective-permute-start | bytes 786440 | tf_op jit(solution)/shard_map/ppermute | solution.py:71
  109.4 8.3 %collective-permute-start.27 = (bf16[256,512]{1,0:T(8,128)(2,1)S(1)}, bf16[256,512]{1,0:T(8,128)(2,1)S(1)}, u32[]{:S(2)}, u32[]{:S(2)}) collective-permute-start(bf16[256,512]{1,0:T(8,128)(2,1)S(1)} %collective-permute-done.23.refs_18_), channel_id=1, source_target_pairs={{0,1},{1,2},{2,3},{3,0},{4,5},{5,6},{6,7},{7,4},{8,11},{9,8},{10,9... | collective-permute-start | bytes 786440 | tf_op jit(solution)/shard_map/ppermute | solution.py:71
  109.5 19.4 %collective-permute-start.31 = (bf16[512,512]{1,0:T(8,128)(2,1)S(1)}, bf16[512,512]{1,0:T(8,128)(2,1)S(1)}, u32[]{:S(2)}, u32[]{:S(2)}) collective-permute-start(bf16[512,512]{1,0:T(8,128)(2,1)S(1)} %collective-permute-done.24.refs_19_), channel_id=1, source_target_pairs={{0,1},{1,2},{2,3},{3,0},{4,5},{5,6},{6,7},{7,4},{8,11},{9,8},{10,9... | collective-permute-start | bytes 1572872 | tf_op jit(solution)/shard_map/ppermute | solution.py:71
  110.2 18.7 %collective-permute-start.19 = (bf16[256,1024]{1,0:T(8,128)(2,1)S(1)}, bf16[256,1024]{1,0:T(8,128)(2,1)S(1)}, u32[]{:S(2)}, u32[]{:S(2)}) collective-permute-start(bf16[256,1024]{1,0:T(8,128)(2,1)S(1)} %collective-permute-done.17.refs_12_), channel_id=1, source_target_pairs={{0,48},{8,24},{16,0},{24,40},{32,16},{40,56},{48,32},{56,8},{64,11... | collective-permute-start | bytes 1572872 | tf_op jit(solution)/shard_map/ppermute | solution.py:42
  114.9 13.9 %collective-permute-start.20 = (bf16[256,1024]{1,0:T(8,128)(2,1)S(1)}, bf16[256,1024]{1,0:T(8,128)(2,1)S(1)}, u32[]{:S(2)}, u32[]{:S(2)}) collective-permute-start(bf16[256,1024]{1,0:T(8,128)(2,1)S(1)} %collective-permute-done.18.refs_13_), channel_id=1, source_target_pairs={{0,16},{8,56},{16,32},{24,8},{32,48},{40,24},{48,0},{56,40},{64,80... | collective-permute-start | bytes 1572872 | tf_op jit(solution)/shard_map/ppermute | solution.py:42
  117.8 11.0 %collective-permute-start.32 = (bf16[256,512]{1,0:T(8,128)(2,1)S(1)}, bf16[256,512]{1,0:T(8,128)(2,1)S(1)}, u32[]{:S(2)}, u32[]{:S(2)}) collective-permute-start(bf16[256,512]{1,0:T(8,128)(2,1)S(1)} %collective-permute-done.27.refs_21_), channel_id=1, source_target_pairs={{0,1},{1,2},{2,3},{3,0},{4,5},{5,6},{6,7},{7,4},{8,11},{9,8},{10,9... | collective-permute-start | bytes 786440 | tf_op jit(solution)/shard_map/ppermute | solution.py:71
  118.7 10.1 %collective-permute-start.30 = (bf16[256,512]{1,0:T(8,128)(2,1)S(1)}, bf16[256,512]{1,0:T(8,128)(2,1)S(1)}, u32[]{:S(2)}, u32[]{:S(2)}) collective-permute-start(bf16[256,512]{1,0:T(8,128)(2,1)S(1)} %collective-permute-done.23.refs_18_), channel_id=1, source_target_pairs={{0,3},{1,0},{2,1},{3,2},{4,7},{5,4},{6,5},{7,6},{8,9},{9,10},{10,1... | collective-permute-start | bytes 786440 | tf_op jit(solution)/shard_map/ppermute | solution.py:71
  136.0 4.4 %collective-permute-start.33 = (bf16[256,1024]{1,0:T(8,128)(2,1)S(1)}, bf16[256,1024]{1,0:T(8,128)(2,1)S(1)}, u32[]{:S(2)}, u32[]{:S(2)}) collective-permute-start(bf16[256,1024]{1,0:T(8,128)(2,1)S(1)} %get-tuple-element.60), channel_id=1, source_target_pairs={{0,8},{8,0},{16,24},{24,16},{32,40},{40,32},{48,56},{56,48},{64,72... | collective-permute-start | bytes 1572872 | tf_op jit(solution)/shard_map/ppermute | solution.py:38
  (8 other events, 84.9 us)

commit v3 on v2

--- a/solution.py
+++ b/solution.py
@@ -50,12 +50,8 @@
     return lax.ppermute(v, "ctx", ctx_pairs(lambda z, x, c: (z, x ^ bit, c)))
 
 
-def flip_z(v, bit):
-    return lax.ppermute(v, "ctx", ctx_pairs(lambda z, x, c: (z ^ bit, x, c)))
-
-
-def ahead_z(v, bit):
-    return lax.ppermute(v, "ctx", ctx_pairs(lambda z, x, c: None if z & bit else (z | bit, x, c)))
+def ahead_z(v, by):
+    return lax.ppermute(v, "ctx", ctx_pairs(lambda z, x, c: (z + by, x, c) if z + by < ZL else None))
 
 
 def swap_zh(v):
@@ -71,18 +67,13 @@
     return lax.ppermute(v, ("ctx", "ch"), pairs)
 
 
-def after(v, *earlier):
-    return lax.optimization_barrier((v,) + earlier)[0]
-
-
-class Lane:
-    def __init__(self, *earlier):
-        self.earlier = earlier
-
-    def send(self, op, v, *rest):
-        result = op(after(v, *self.earlier), *rest)
-        self.earlier = (result,)
-        return result
+def around(op, v):
+    behind, ahead = op(v, 1), op(v, -1)
+    return [v, behind, ahead, op(behind, 1)]
+
+
+def fence(*arrays):
+    return lax.optimization_barrier(arrays)
 
 
 def drive_kernel(proj, halo, taps, rates, drive, queries, ends, wide):
@@ -172,9 +163,14 @@
 
 
 def project_kernel(place, *refs):
-    count_w, count_g = ZL * X, Y * 3
+    count_w, count_g = 2 * X, Y * 2
     weights, gated = refs[:count_w], refs[count_w : count_w + count_g]
     mine, other, left, total, sem = refs[count_w + count_g :]
+
+    def shard(s, r, columns):
+        first, others = weights[2 * r], weights[2 * r + 1]
+        return first[:, columns] if s == 0 else others[(s - 1) * ROWS : s * ROWS, columns]
+
     z, x, h, y = place[1], place[2], place[3], place[4]
     sign = 1 - 2 * place[0]
 
@@ -183,24 +179,21 @@
 
     copies = []
 
-    def put(n, q, first, rows):
-        columns = pl.ds(pl.multiple_of(q * HALF, HALF), HALF)
-        copy = pltpu.make_async_copy(gated[n], left.at[pl.ds(first, rows), columns], sem.at[n])
-        copy.start()
-        copies.append(copy)
-
     for j in range(Y):
-        at = origin(y, j, Y)
-        put(3 * j, h * Y + at, 0, 2 * ROWS)
-        put(3 * j + 1, (1 - h) * Y + at, 0, ROWS)
-        put(3 * j + 2, (1 - h) * Y + at, ROWS, ROWS)
+        for i in range(ZH):
+            n = 2 * j + i
+            q = lax.rem(h + i, ZH) * Y + origin(y, j, Y)
+            columns = pl.ds(pl.multiple_of(q * HALF, HALF), HALF)
+            copy = pltpu.make_async_copy(gated[n], left.at[:, columns], sem.at[n])
+            copy.start()
+            copies.append(copy)
     for copy in copies:
         copy.wait()
     for s in range(ZL):
         blocks = [origin(z, s, ZL) * X + origin(x, r, X) for r in range(X)]
         rows = jnp.concatenate([left[:, pl.ds(pl.multiple_of(m * ROWS, ROWS), ROWS)] for m in blocks], axis=1)
         for col in range(0, CHANS, 256):
-            shards = [weights[s * X + r][:, col : col + 256] for r in range(X)]
+            shards = [shard(s, r, slice(col, col + 256)) for r in range(X)]
             product = jnp.dot(rows, jnp.concatenate(shards, axis=0), preferred_element_type=F32)
             if s > 0:
                 product += total[:, col : col + 256]
@@ -223,7 +216,7 @@
         scratch_shapes=[
             pltpu.VMEM((2 * ROWS, ZH * Y * HALF), BF16),
             pltpu.VMEM((2 * ROWS, CHANS), F32),
-            pltpu.SemaphoreType.DMA((Y * 3,)),
+            pltpu.SemaphoreType.DMA((Y * 2,)),
         ],
         compiler_params=pltpu.CompilerParams(vmem_limit_bytes=28 * 1024 * 1024),
         cost_estimate=pl.CostEstimate(flops=4_300_000_000, bytes_accessed=14_000_000, transcendentals=0),
@@ -231,38 +224,24 @@
     )(place, *weights, *gated)
 
 
-def carried_states(ends, rates, z, x, core, before_x, before_z):
-    def decays(rows):
-        return jnp.exp(-rates * jnp.asarray(rows).astype(F32))
-
-    total, prefix, size, offset = ends, jnp.zeros_like(ends), ROWS, jnp.int32(0)
-    steps = (
-        (swap_core, core),
-        (functools.partial(flip_x, bit=1), x % 2),
-        (functools.partial(flip_x, bit=2), x // 2),
-        (functools.partial(flip_z, bit=1), z % 2),
-        (functools.partial(ahead_z, bit=2), z // 2),
-    )
-    arrived = []
-    for k, (exchange, upper) in enumerate(steps):
-        if k == 1:
-            total = after(total, *before_x)
-        if k == 3:
-            total = after(total, *before_z)
-        theirs = exchange(total)
-        arrived.append(theirs)
-        is_upper = upper == 1
-        prefix = prefix + jnp.where(is_upper, decays(offset) * theirs, 0.0)
-        total = decays(size) * jnp.where(is_upper, theirs, total) + jnp.where(is_upper, total, theirs)
-        offset = offset + size * upper
-        size = size * 2
-    return prefix, arrived[2], arrived[4]
-
-
-def around(lanes, op, v):
-    behind = lanes[0].send(op, v, 1)
-    ahead = lanes[1].send(op, v, -1)
-    return [v, behind, ahead, lanes[0].send(op, behind, 1)]
+def decays(rates, rows):
+    return jnp.exp(-rates * jnp.asarray(rows).astype(F32))
+
+
+def chip_states(ends, rates, core):
+    theirs = swap_core(ends)
+    first, second = jnp.where(core == 0, ends, theirs), jnp.where(core == 0, theirs, ends)
+    return decays(rates, ROWS) * first + second, jnp.where(core == 0, 0.0, theirs)
+
+
+def ring_states(chip, others, rates, x):
+    size = CORE * ROWS
+    group, before = decays(rates, size * (X - 1 - x)) * chip, jnp.zeros_like(chip)
+    for bits, theirs in zip((1, 2, 3), others):
+        at = x ^ bits
+        group += decays(rates, size * (X - 1 - at)) * theirs
+        before += jnp.where(at < x, decays(rates, size * jnp.maximum(x - 1 - at, 0)) * theirs, 0.0)
+    return group, before
 
 
 def body(stream, projected, short_taps, decay_rates, residues, out_weight):
@@ -273,41 +252,43 @@
 
     proj = projected.transpose(1, 0, 2)
     halo = lax.ppermute(projected[ROWS - 2 :], "ctx", [(i, i + 1) for i in range(ZL * X * CORE - 1)])
-    z_behind = around_z(out_weight, 1)
-    own_behind, own_ahead = around_x(out_weight, 1), around_x(out_weight, -1)
+    z_behind, z_ahead = around_z(out_weight, 1), around_z(out_weight, -1)
+    behind0, ahead0 = around_x(out_weight, 1), around_x(out_weight, -1)
     halo = halo.transpose(1, 0, 2).astype(F32)
     drive, queries, ends = drive_call(proj, halo, short_taps.reshape(9, CHANS), decay_rates)
 
     rates3 = decay_rates.reshape(MODES, LANES, 128)
     weights3 = residues.reshape(MODES, LANES, 128)
-    z_ahead = around_z(after(out_weight, z_behind), -1)
-    carried, x_done, z_done = carried_states(ends, rates3, z, x, core, (own_behind, own_ahead), (z_ahead,))
-    z_far = around_z(after(z_behind, z_done), 1)
-
-    shards = (out_weight, z_behind, z_ahead, z_far)
-    first, second = Lane(x_done), Lane(x_done)
-    behind, ahead, far = [own_behind] + [None] * (ZL - 1), [own_ahead] + [None] * (ZL - 1), [None] * ZL
-    far[0] = first.send(around_x, behind[0], 1)
-    behind[1] = second.send(around_x, shards[1], 1)
-    carried = after(carried, far[0], behind[1])
-    ahead[1] = first.send(around_x, shards[1], -1)
-    far[1] = second.send(around_x, behind[1], 1)
-    behind[2] = first.send(around_x, shards[2], 1)
-    ahead[2] = second.send(around_x, shards[2], -1)
-    far[2] = first.send(around_x, behind[2], 1)
-    behind[3] = second.send(around_x, shards[3], 1)
-    ahead[3] = first.send(around_x, shards[3], -1)
-    far[3] = second.send(around_x, behind[3], 1)
-    weights = [v for s in range(ZL) for v in (shards[s], behind[s], ahead[s], far[s])]
-
+    chip, in_chip = chip_states(ends, rates3, core)
+    chip, z_behind, behind0, ahead0 = fence(chip, z_behind, behind0, ahead0)
+    others = [flip_x(chip, bits) for bits in (1, 2, 3)]
+    z_far = around_z(z_behind, 1)
+    group, before = ring_states(chip, others, rates3, x)
+    group, z_ahead = fence(group, z_ahead)
+    groups = [ahead_z(group, by) for by in (1, 2, 3)]
+    column = jnp.concatenate([z_behind, z_ahead, z_far], axis=0)
+    far1, far2, far3, column, behind0 = fence(*groups, column, behind0)
+    behind, ahead = around_x(column, 1), around_x(column, -1)
+    groups = [far1, far2, far3]
+    later = groups[0]
+    for k in (1, 2):
+        later += decays(rates3, CORE * X * ROWS * k) * groups[k]
+    into_chip = before + decays(rates3, CORE * ROWS * x) * later
+    carried = jnp.where(core == 0, into_chip, decays(rates3, ROWS) * into_chip + in_chip)
     keep, send = response_call(place, drive, queries, rates3, weights3, carried)
-    theirs = swap_core(send)
-    lane_h, lanes_y = Lane(), (Lane(), Lane())
-    across = [lane_h.send(swap_zh, part) for part in (keep, theirs)]
-    own = around((Lane(), Lane()), around_y, jnp.concatenate([keep, theirs], axis=0))
-    parts = [around(lanes_y if part == 0 else lanes_y[::-1], around_y, across[part]) for part in range(2)]
-    pieces = [v for j in range(Y) for v in (own[j], parts[0][j], parts[1][j])]
-
+    both = jnp.concatenate([keep, swap_core(send)], axis=0)
+    across = swap_zh(both)
+    own = around(around_y, both)
+    _, a = fence(own[1], behind)
+    far = around_x(a, 1)
+
+    across, _, _ = fence(across, own[1], own[2])
+    _, a = fence(ahead, behind0)
+    far0 = around_x(a, 1)
+    across = around(around_y, across)
+
+    weights = (out_weight, column, behind0, behind, ahead0, ahead, far0, far)
+    pieces = [v for j in range(Y) for v in (own[j], across[j])]
     mine, other = project_call(place, weights, pieces)
     summed = stream.astype(F32) + mine + swap_core(other).astype(F32)
     return summed.astype(BF16)

time: 142 us -> 129 us (0.908)
  starting transfers between devices: 55.7 us -> 47 us
  waiting for transfers between devices: 63.1 us -> 55.5 us
  local copies, waits for them, and re-layouts: 4.91 us -> 9.16 us
    ppermute x2 -> x1, waiting for transfers between devices: 26.8 us -> 12.3 us  [swap_zh(): return lax.ppermute(v, 'ch', ch_pairs(lambda h, y: (1 - h, y)))]
    ppermute x12 -> x6, starting transfers between devices: 17.6 us -> 10.5 us  [around_x(): lax.ppermute(v, 'ctx', ctx_pairs(lambda z, x, c: (z, (x + by * (1 - 2 * c...]
    ppermute x9 -> x6, waiting for transfers between devices: 17.8 us -> 24.6 us  [around_y(): return lax.ppermute(v, ('ctx', 'ch'), pairs)]
    unnamed x15 -> x33, local copies, waits for them, and re-layouts: 3.15 us -> 7.39 us
    add x5 -> x2, other arithmetic: 3.15 us -> 0.07 us  [the longest x1 0.05 us: ring_states(): group += decays(rates, size * (X - 1 - at)) * theirs]
    ppermute x2 -> x1, starting transfers between devices: 8.19 us -> 5.54 us  [swap_zh(): return lax.ppermute(v, 'ch', ch_pairs(lambda h, y: (1 - h, y)))]
    ppermute x2 -> x3, starting transfers between devices: 6.92 us -> 9.1 us  [ahead_z(): lax.ppermute(v, 'ctx', ctx_pairs(lambda z, x, c: (z + by, x, c) if z + by...]
    ppermute x2 -> x3, starting transfers between devices: 3.51 us -> 5.23 us  [flip_x(): return lax.ppermute(v, 'ctx', ctx_pairs(lambda z, x, c: (z, x ^ bit, c)))]
  transfers between devices with their start and end apart: 34 -> 26, of which waited for: 12 -> 14; matrix products, arithmetic and copies ran while one was open for 4% -> 3% of each run, Pallas kernels for 4% -> 5%
where the time goes in v3:
time: 129 us; the launch traced here: 128 us
  waiting for transfers between devices  55.5 us (43%)
  starting transfers between devices  47 us (36%)
  Pallas kernels  12.8 us (10%)
  local copies, waits for them, and re-layouts  9.16 us (7%)
  other arithmetic  3.63 us (3%)
    ppermute x6, waiting for transfers between devices, around_y(): return lax.ppermute(v, ('ctx', 'ch'), pairs)  24.6 us
    ppermute x1, waiting for transfers between devices, swap_zh(): return lax.ppermute(v, 'ch', ch_pairs(lambda h, y: (1 - h, y)))  12.3 us
    ppermute x6, starting transfers between devices, around_x(): lax.ppermute(v, 'ctx', ctx_pairs(lambda z, x, c: (z, (x + by * (1 - 2 * c...  10.5 us
    ppermute x3, starting transfers between devices, ahead_z(): lax.ppermute(v, 'ctx', ctx_pairs(lambda z, x, c: (z + by, x, c) if z + by...  9.1 us
    ppermute x3, waiting for transfers between devices, around_z(): lax.ppermute(v, 'ctx', ctx_pairs(lambda z, x, c: ((z + by * (1 - 2 * c))...  7.59 us
    unnamed x33, local copies, waits for them, and re-layouts  7.39 us
    ppermute x6, starting transfers between devices, around_y(): return lax.ppermute(v, ('ctx', 'ch'), pairs)  7.07 us
    pallas_call x1, Pallas kernels, project_call(): pl.pallas_call(project_kernel, in_specs=[pl.BlockSpec(memory_space=pltpu....  6.68 us
  transfers between devices with their start and end apart: 26, of which 14 were waited for; matrix products, arithmetic and copies ran while one was open for 3% of the time, Pallas kernels for 5%

profile of v3, /device:TPU:35, one launch (start us, length us, event | category | flops | bytes accessed | tf_op | source)
XLA Modules:
  0.0 128.3 jit_solution(12186716596469785238)
XLA Ops:
  0.9 3.7 %collective-permute-start = (bf16[2,3,1024]{2,0,1:T(2,128)(2,1)S(1)}, bf16[2,3,1024]{2,0,1:T(2,128)(2,1)S(1)}, u32[]{:S(2)}, u32[]{:S(2)}) collective-permute-start(bf16[2,3,1024]{2,0,1:T(2,128)(2,1)S(1)} %slice.3), channel_id=1, source_target_pairs={{0,8},{8,16},{16,24},{24,32},{32,40},{40,48},{48,56},{56,64},{64,7... | collective-permute-start | bytes 36872 | tf_op jit(solution)/shard_map/ppermute | solution.py:254
  6.9 1.4 %copy-done = bf16[256,3,1024]{2,0,1:T(8,128)(2,1)S(1)} copy-done((bf16[256,3,1024]{2,0,1:T(8,128)(2,1)S(1)}, bf16[256,3,1024]{2,0,1:T(8,128)(2,1)}, u32[]{:S(2)}) %copy-start) | copy-done | bytes 1572888
  9.2 2.8 %drive_and_ends.1 = (f32[2112,128]{1,0:T(8,128)S(1)}, f32[256,1024]{1,0:T(8,128)S(1)}, f32[16,8,128]{2,1,0:T(8,128)S(1)}) custom-call(bf16[3,256,1024]{2,1,0:T(8,128)(2,1)S(1)} %bitcast.16, f32[3,2,1024]{2,1,0:T(2,128)S(1)} %convert_bitcast_fusion.halo, f32[9,1024]{1,0:T(8,128)S(1)} %reshape.10.taps, f32[16,1024]{1,0:T(8,128)S(1)} %copy-done.3), custom_call_target="tpu_custom_call" | custom-call | flops 1 | bytes 1 | tf_op jit(solution)/shard_map/drive_and_ends/pallas_call | solution.py:115
  13.0 1.4 %collective-permute-start.1 = (f32[16,8,128]{2,1,0:T(8,128)S(1)}, f32[16,8,128]{2,1,0:T(8,128)S(1)}, u32[]{:S(2)}, u32[]{:S(2)}) collective-permute-start(f32[16,8,128]{2,1,0:T(8,128)S(1)} %get-tuple-element.26), channel_id=1, source_target_pairs={{0,8},{8,0},{16,24},{24,16},{32,40},{40,32},{48,56},{56,48},{64,72... | collective-permute-start | bytes 196616 | tf_op jit(solution)/shard_map/ppermute | solution.py:38
  14.4 1.6 %collective-permute-start.8 = (bf16[256,1024]{1,0:T(8,128)(2,1)S(1)}, bf16[256,1024]{1,0:T(8,128)(2,1)}, u32[]{:S(2)}, u32[]{:S(2)}) collective-permute-start(bf16[256,1024]{1,0:T(8,128)(2,1)S(1)} %copy-done.5), channel_id=1, source_target_pairs={{0,192},{8,72},{16,208},{24,88},{32,224},{40,104},{48,240},{56,120... | collective-permute-start | bytes 1572872 | tf_op jit(solution)/shard_map/ppermute | solution.py:46
  16.1 2.1 %collective-permute-done.4.refs_4_ = bf16[256,1024]{1,0:T(8,128)(2,1)S(1)} collective-permute-done((bf16[256,1024]{1,0:T(8,128)(2,1)}, bf16[256,1024]{1,0:T(8,128)(2,1)S(1)}, u32[]{:S(2)}, u32[]{:S(2)}) %collective-permute-start.4) | collective-permute-done | bytes 524320 | tf_op jit(solution)/shard_map/ppermute | solution.py:42
  19.1 2.5 %collective-permute-done.2 = bf16[256,1024]{1,0:T(8,128)(2,1)} collective-permute-done((bf16[256,1024]{1,0:T(8,128)(2,1)}, bf16[256,1024]{1,0:T(8,128)(2,1)}, u32[]{:S(2)}, u32[]{:S(2)}) %collective-permute-start.2) | collective-permute-done | bytes 524320 | tf_op jit(solution)/shard_map/ppermute | solution.py:46
  21.9 4.9 %collective-permute-start.6 = (f32[16,8,128]{2,1,0:T(8,128)S(1)}, f32[16,8,128]{2,1,0:T(8,128)S(1)}, u32[]{:S(2)}, u32[]{:S(2)}) collective-permute-start(f32[16,8,128]{2,1,0:T(8,128)S(1)} %select_add_fusion), channel_id=1, source_target_pairs={{0,32},{8,40},{16,48},{24,56},{32,0},{40,8},{48,16},{56,24},{64,96... | collective-permute-start | bytes 196616 | tf_op jit(solution)/shard_map/ppermute | solution.py:50
  26.8 1.6 %collective-permute-done.6 = f32[16,8,128]{2,1,0:T(8,128)S(1)} collective-permute-done((f32[16,8,128]{2,1,0:T(8,128)S(1)}, f32[16,8,128]{2,1,0:T(8,128)S(1)}, u32[]{:S(2)}, u32[]{:S(2)}) %collective-permute-start.6) | collective-permute-done | bytes 65568 | tf_op jit(solution)/shard_map/ppermute | solution.py:50
  28.5 1.9 %collective-permute-done.5 = f32[16,8,128]{2,1,0:T(8,128)S(1)} collective-permute-done((f32[16,8,128]{2,1,0:T(8,128)S(1)}, f32[16,8,128]{2,1,0:T(8,128)S(1)}, u32[]{:S(2)}, u32[]{:S(2)}) %collective-permute-start.5) | collective-permute-done | bytes 65568 | tf_op jit(solution)/shard_map/ppermute | solution.py:50
  30.4 5.1 %collective-permute-done.8 = bf16[256,1024]{1,0:T(8,128)(2,1)} collective-permute-done((bf16[256,1024]{1,0:T(8,128)(2,1)S(1)}, bf16[256,1024]{1,0:T(8,128)(2,1)}, u32[]{:S(2)}, u32[]{:S(2)}) %collective-permute-start.8) | collective-permute-done | bytes 524320 | tf_op jit(solution)/shard_map/ppermute | solution.py:46
  36.1 6.5 %collective-permute-start.10 = (f32[16,8,128]{2,1,0:T(8,128)S(1)}, f32[16,8,128]{2,1,0:T(8,128)S(1)}, u32[]{:S(2)}, u32[]{:S(2)}) collective-permute-start(f32[16,8,128]{2,1,0:T(8,128)S(1)} %multiply_add_fusion), channel_id=1, source_target_pairs={{0,128},{8,136},{16,144},{24,152},{32,160},{40,168},{48,176},{56,1... | collective-permute-start | bytes 196616 | tf_op jit(solution)/shard_map/ppermute | solution.py:54
  42.7 1.9 %collective-permute-start.9 = (f32[16,8,128]{2,1,0:T(8,128)S(1)}, f32[16,8,128]{2,1,0:T(8,128)S(1)}, u32[]{:S(2)}, u32[]{:S(2)}) collective-permute-start(f32[16,8,128]{2,1,0:T(8,128)S(1)} %multiply_add_fusion), channel_id=1, source_target_pairs={{0,64},{8,72},{16,80},{24,88},{32,96},{40,104},{48,112},{56,120},{... | collective-permute-start | bytes 196616 | tf_op jit(solution)/shard_map/ppermute | solution.py:54
  44.6 1.5 %pad_maximum_fusion.refs_1_ = bf16[768,1024]{1,0:T(8,128)(2,1)S(1)} fusion(bf16[256,1024]{1,0:T(8,128)(2,1)} %collective-permute-done.12, bf16[256,1024]{1,0:T(8,128)(2,1)} %collective-permute-done.8, bf16[256,1024]{1,0:T(8,128)(2,1)} %collective-permute-done.2), kind=kLoop, calls=%fused_computation | loop fusion | flops 4718592 | bytes 3145728 | tf_op jit(solution)/shard_map/concatenate | solution.py:269
  48.3 2.5 %collective-permute-start.13 = (bf16[768,1024]{1,0:T(8,128)(2,1)S(1)}, bf16[768,1024]{1,0:T(8,128)(2,1)}, u32[]{:S(2)}, u32[]{:S(2)}) collective-permute-start(bf16[768,1024]{1,0:T(8,128)(2,1)S(1)} %pad_maximum_fusion.refs_1_), channel_id=1, source_target_pairs={{0,16},{8,56},{16,32},{24,8},{32,48},{40,24},{48,0},{56,40},{64,80... | collective-permute-start | bytes 4718600 | tf_op jit(solution)/shard_map/ppermute | solution.py:42
  52.8 1.2 copy-done.2
  54.0 3.3 %response_and_gate.1 = (bf16[256,512]{1,0:T(8,128)(2,1)S(1)}, bf16[256,512]{1,0:T(8,128)(2,1)S(1)}) custom-call(s32[5]{0:T(128)S(1)} %stack.23.place, f32[2112,128]{1,0:T(8,128)S(1)} %get-tuple-element.36.drive, f32[256,1024]{1,0:T(8,128)S(1)} %copy-done.2, f32[16,8,128]{2,1,0:T(8,128)S(1)} %bitcast.15, f32[16,8,128]{2,1,0:T(8,128)S(1)} %bitcast.17, ...), custom_call_target="tpu_custom_call" | custom-call | flops 1 | bytes 1 | tf_op jit(solution)/shard_map/response_and_gate/pallas_call | solution.py:154
  57.4 2.0 %collective-permute-start.14 = (bf16[768,1024]{1,0:T(8,128)(2,1)S(1)}, bf16[768,1024]{1,0:T(8,128)(2,1)S(1)}, u32[]{:S(2)}, u32[]{:S(2)}) collective-permute-start(bf16[768,1024]{1,0:T(8,128)(2,1)S(1)} %pad_maximum_fusion.refs_1_), channel_id=1, source_target_pairs={{0,48},{8,24},{16,0},{24,40},{32,16},{40,56},{48,32},{56,8},{64,11... | collective-permute-start | bytes 4718600 | tf_op jit(solution)/shard_map/ppermute | solution.py:42
  59.4 2.8 %collective-permute-start.17 = (bf16[512,512]{1,0:T(8,128)(2,1)S(1)}, bf16[512,512]{1,0:T(8,128)(2,1)S(1)}, u32[]{:S(2)}, u32[]{:S(2)}) collective-permute-start(bf16[512,512]{1,0:T(8,128)(2,1)S(1)} %constant_dynamic-update-slice_fusion.refs_8_), channel_id=1, source_target_pairs={{0,1},{1,2},{2,3},{3,0},{4,5},{5,6},{6,7},{7,4},{8,11},{9,8},{10,9... | collective-permute-start | bytes 1572872 | tf_op jit(solution)/shard_map/ppermute | solution.py:67
  62.2 5.5 %collective-permute-start.19 = (bf16[512,512]{1,0:T(8,128)(2,1)S(1)}, bf16[512,512]{1,0:T(8,128)(2,1)S(1)}, u32[]{:S(2)}, u32[]{:S(2)}) collective-permute-start(bf16[512,512]{1,0:T(8,128)(2,1)S(1)} %constant_dynamic-update-slice_fusion.refs_8_), channel_id=1, source_target_pairs={{0,4},{1,5},{2,6},{3,7},{4,0},{5,1},{6,2},{7,3},{8,12},{9,13},{10,... | collective-permute-start | bytes 1572872 | tf_op jit(solution)/shard_map/ppermute | solution.py:58
  67.8 5.9 %collective-permute-done.17.refs_10_ = bf16[512,512]{1,0:T(8,128)(2,1)S(1)} collective-permute-done((bf16[512,512]{1,0:T(8,128)(2,1)S(1)}, bf16[512,512]{1,0:T(8,128)(2,1)S(1)}, u32[]{:S(2)}, u32[]{:S(2)}) %collective-permute-start.17) | collective-permute-done | bytes 524320 | tf_op jit(solution)/shard_map/ppermute | solution.py:67
  73.7 2.9 %collective-permute-done.13.refs_3_ = bf16[768,1024]{1,0:T(8,128)(2,1)} collective-permute-done((bf16[768,1024]{1,0:T(8,128)(2,1)S(1)}, bf16[768,1024]{1,0:T(8,128)(2,1)}, u32[]{:S(2)}, u32[]{:S(2)}) %collective-permute-start.13) | collective-permute-done | bytes 1572896 | tf_op jit(solution)/shard_map/ppermute | solution.py:42
  76.6 2.3 %collective-permute-start.18 = (bf16[768,1024]{1,0:T(8,128)(2,1)}, bf16[768,1024]{1,0:T(8,128)(2,1)S(1)}, u32[]{:S(2)}, u32[]{:S(2)}) collective-permute-start(bf16[768,1024]{1,0:T(8,128)(2,1)} %collective-permute-done.13.refs_3_), channel_id=1, source_target_pairs={{0,16},{8,56},{16,32},{24,8},{32,48},{40,24},{48,0},{56,40},{64,80... | collective-permute-start | bytes 4718600 | tf_op jit(solution)/shard_map/ppermute | solution.py:42
  78.9 12.3 %collective-permute-done.19.refs_9_ = bf16[512,512]{1,0:T(8,128)(2,1)S(1)} collective-permute-done((bf16[512,512]{1,0:T(8,128)(2,1)S(1)}, bf16[512,512]{1,0:T(8,128)(2,1)S(1)}, u32[]{:S(2)}, u32[]{:S(2)}) %collective-permute-start.19) | collective-permute-done | bytes 524320 | tf_op jit(solution)/shard_map/ppermute | solution.py:58
  92.6 2.2 %collective-permute-start.23 = (bf16[512,512]{1,0:T(8,128)(2,1)S(1)}, bf16[512,512]{1,0:T(8,128)(2,1)S(1)}, u32[]{:S(2)}, u32[]{:S(2)}) collective-permute-start(bf16[512,512]{1,0:T(8,128)(2,1)S(1)} %collective-permute-done.17.refs_10_), channel_id=1, source_target_pairs={{0,1},{1,2},{2,3},{3,0},{4,5},{5,6},{6,7},{7,4},{8,11},{9,8},{10,9... | collective-permute-start | bytes 1572872 | tf_op jit(solution)/shard_map/ppermute | solution.py:67
  94.8 8.5 %collective-permute-done.21.refs_11_ = bf16[512,512]{1,0:T(8,128)(2,1)S(1)} collective-permute-done((bf16[512,512]{1,0:T(8,128)(2,1)S(1)}, bf16[512,512]{1,0:T(8,128)(2,1)S(1)}, u32[]{:S(2)}, u32[]{:S(2)}) %collective-permute-start.21) | collective-permute-done | bytes 524320 | tf_op jit(solution)/shard_map/ppermute | solution.py:67
  103.9 2.2 %collective-permute-start.15 = (bf16[256,1024]{1,0:T(8,128)(2,1)S(1)}, bf16[256,1024]{1,0:T(8,128)(2,1)S(1)}, u32[]{:S(2)}, u32[]{:S(2)}) collective-permute-start(bf16[256,1024]{1,0:T(8,128)(2,1)S(1)} %copy-done.9), channel_id=1, source_target_pairs={{0,16},{8,56},{16,32},{24,8},{32,48},{40,24},{48,0},{56,40},{64,80... | collective-permute-start | bytes 1572872 | tf_op jit(solution)/shard_map/ppermute | solution.py:42
  107.0 3.7 %collective-permute-done.23.refs_14_ = bf16[512,512]{1,0:T(8,128)(2,1)S(1)} collective-permute-done((bf16[512,512]{1,0:T(8,128)(2,1)S(1)}, bf16[512,512]{1,0:T(8,128)(2,1)S(1)}, u32[]{:S(2)}, u32[]{:S(2)}) %collective-permute-start.23) | collective-permute-done | bytes 524320 | tf_op jit(solution)/shard_map/ppermute | solution.py:67
  110.7 5.6 %collective-permute-done.24.refs_15_ = bf16[512,512]{1,0:T(8,128)(2,1)S(1)} collective-permute-done((bf16[512,512]{1,0:T(8,128)(2,1)S(1)}, bf16[512,512]{1,0:T(8,128)(2,1)S(1)}, u32[]{:S(2)}, u32[]{:S(2)}) %collective-permute-start.24) | collective-permute-done | bytes 524320 | tf_op jit(solution)/shard_map/ppermute | solution.py:67
  116.3 6.7 %projection.1 = (f32[256,1024]{1,0:T(8,128)S(1)}, bf16[256,1024]{1,0:T(8,128)(2,1)S(1)}) custom-call(s32[5]{0:T(128)S(1)} %stack.23.place, bf16[256,1024]{1,0:T(8,128)(2,1)S(1)} %copy-done.5, bf16[768,1024]{1,0:T(8,128)(2,1)S(1)} %pad_maximum_fusion.refs_1_, bf16[256,1024]{1,0:T(8,128)(2,1)S(1)} %copy-done.9, ...), custom_call_target="tpu_custom_call" | custom-call | flops 4300000256 | bytes 14000000 | tf_op jit(solution)/shard_map/projection/pallas_call | solution.py:209
  123.0 2.7 %collective-permute-start.25 = (bf16[256,1024]{1,0:T(8,128)(2,1)S(1)}, bf16[256,1024]{1,0:T(8,128)(2,1)S(1)}, u32[]{:S(2)}, u32[]{:S(2)}) collective-permute-start(bf16[256,1024]{1,0:T(8,128)(2,1)S(1)} %get-tuple-element.46), channel_id=1, source_target_pairs={{0,8},{8,0},{16,24},{24,16},{32,40},{40,32},{48,56},{56,48},{64,72... | collective-permute-start | bytes 1572872 | tf_op jit(solution)/shard_map/ppermute | solution.py:38
  125.7 1.5 %collective-permute-done.25 = bf16[256,1024]{1,0:T(8,128)(2,1)S(1)} collective-permute-done((bf16[256,1024]{1,0:T(8,128)(2,1)S(1)}, bf16[256,1024]{1,0:T(8,128)(2,1)S(1)}, u32[]{:S(2)}, u32[]{:S(2)}) %collective-permute-start.25) | collective-permute-done | bytes 524320 | tf_op jit(solution)/shard_map/ppermute | solution.py:38
  (66 shorter events, 15.2 us)
Async XLA Ops:
  0.0 16.0 %copy-start.4 = (f32[16,1024]{1,0:T(8,128)S(1)}, f32[16,1024]{1,0:T(8,128)}, u32[]{:S(2)}) copy-start(f32[16,1024]{1,0:T(8,128)} %rates.1) | copy-start | bytes 196612
  0.9 6.1 %collective-permute-start = (bf16[2,3,1024]{2,0,1:T(2,128)(2,1)S(1)}, bf16[2,3,1024]{2,0,1:T(2,128)(2,1)S(1)}, u32[]{:S(2)}, u32[]{:S(2)}) collective-permute-start(bf16[2,3,1024]{2,0,1:T(2,128)(2,1)S(1)} %slice.3), channel_id=1, source_target_pairs={{0,8},{8,16},{16,24},{24,32},{32,40},{40,48},{48,56},{56,64},{64,7... | collective-permute-start | bytes 36872 | tf_op jit(solution)/shard_map/ppermute | solution.py:254
  4.5 13.7 %collective-permute-start.4 = (bf16[256,1024]{1,0:T(8,128)(2,1)}, bf16[256,1024]{1,0:T(8,128)(2,1)S(1)}, u32[]{:S(2)}, u32[]{:S(2)}) collective-permute-start(bf16[256,1024]{1,0:T(8,128)(2,1)} %refs_0_.1), channel_id=1, source_target_pairs={{0,48},{8,24},{16,0},{24,40},{32,16},{40,56},{48,32},{56,8},{64,11... | collective-permute-start | bytes 1572872 | tf_op jit(solution)/shard_map/ppermute | solution.py:42
  5.5 13.5 %collective-permute-start.3 = (bf16[256,1024]{1,0:T(8,128)(2,1)}, bf16[256,1024]{1,0:T(8,128)(2,1)S(1)}, u32[]{:S(2)}, u32[]{:S(2)}) collective-permute-start(bf16[256,1024]{1,0:T(8,128)(2,1)} %refs_0_.1), channel_id=1, source_target_pairs={{0,16},{8,56},{16,32},{24,8},{32,48},{40,24},{48,0},{56,40},{64,80... | collective-permute-start | bytes 1572872 | tf_op jit(solution)/shard_map/ppermute | solution.py:42
  6.1 15.5 %collective-permute-start.2 = (bf16[256,1024]{1,0:T(8,128)(2,1)}, bf16[256,1024]{1,0:T(8,128)(2,1)}, u32[]{:S(2)}, u32[]{:S(2)}) collective-permute-start(bf16[256,1024]{1,0:T(8,128)(2,1)} %refs_0_.1), channel_id=1, source_target_pairs={{0,64},{8,200},{16,80},{24,216},{32,96},{40,232},{48,112},{56,248}... | collective-permute-start | bytes 1572872 | tf_op jit(solution)/shard_map/ppermute | solution.py:46
  13.0 3.1 %collective-permute-start.1 = (f32[16,8,128]{2,1,0:T(8,128)S(1)}, f32[16,8,128]{2,1,0:T(8,128)S(1)}, u32[]{:S(2)}, u32[]{:S(2)}) collective-permute-start(f32[16,8,128]{2,1,0:T(8,128)S(1)} %get-tuple-element.26), channel_id=1, source_target_pairs={{0,8},{8,0},{16,24},{24,16},{32,40},{40,32},{48,56},{56,48},{64,72... | collective-permute-start | bytes 196616 | tf_op jit(solution)/shard_map/ppermute | solution.py:38
  14.4 21.1 %collective-permute-start.8 = (bf16[256,1024]{1,0:T(8,128)(2,1)S(1)}, bf16[256,1024]{1,0:T(8,128)(2,1)}, u32[]{:S(2)}, u32[]{:S(2)}) collective-permute-start(bf16[256,1024]{1,0:T(8,128)(2,1)S(1)} %copy-done.5), channel_id=1, source_target_pairs={{0,192},{8,72},{16,208},{24,88},{32,224},{40,104},{48,240},{56,120... | collective-permute-start | bytes 1572872 | tf_op jit(solution)/shard_map/ppermute | solution.py:46
  19.1 25.5 %copy-start.8 = (bf16[256,1024]{1,0:T(8,128)(2,1)}, bf16[256,1024]{1,0:T(8,128)(2,1)S(1)}, u32[]{:S(2)}) copy-start(bf16[256,1024]{1,0:T(8,128)(2,1)S(1)} %collective-permute-done.3.refs_2_) | copy-start | bytes 1572868
  21.6 23.0 %collective-permute-start.12 = (bf16[256,1024]{1,0:T(8,128)(2,1)}, bf16[256,1024]{1,0:T(8,128)(2,1)}, u32[]{:S(2)}, u32[]{:S(2)}) collective-permute-start(bf16[256,1024]{1,0:T(8,128)(2,1)} %collective-permute-done.2), channel_id=1, source_target_pairs={{0,64},{8,200},{16,80},{24,216},{32,96},{40,232},{48,112},{56,248}... | collective-permute-start | bytes 1572872 | tf_op jit(solution)/shard_map/ppermute | solution.py:46
  21.6 5.2 %collective-permute-start.7 = (f32[16,8,128]{2,1,0:T(8,128)S(1)}, f32[16,8,128]{2,1,0:T(8,128)S(1)}, u32[]{:S(2)}, u32[]{:S(2)}) collective-permute-start(f32[16,8,128]{2,1,0:T(8,128)S(1)} %select_add_fusion), channel_id=1, source_target_pairs={{0,48},{8,56},{16,32},{24,40},{32,16},{40,24},{48,0},{56,8},{64,11... | collective-permute-start | bytes 196616 | tf_op jit(solution)/shard_map/ppermute | solution.py:50
  21.9 6.6 %collective-permute-start.6 = (f32[16,8,128]{2,1,0:T(8,128)S(1)}, f32[16,8,128]{2,1,0:T(8,128)S(1)}, u32[]{:S(2)}, u32[]{:S(2)}) collective-permute-start(f32[16,8,128]{2,1,0:T(8,128)S(1)} %select_add_fusion), channel_id=1, source_target_pairs={{0,32},{8,40},{16,48},{24,56},{32,0},{40,8},{48,16},{56,24},{64,96... | collective-permute-start | bytes 196616 | tf_op jit(solution)/shard_map/ppermute | solution.py:50
  26.8 3.5 %collective-permute-start.5 = (f32[16,8,128]{2,1,0:T(8,128)S(1)}, f32[16,8,128]{2,1,0:T(8,128)S(1)}, u32[]{:S(2)}, u32[]{:S(2)}) collective-permute-start(f32[16,8,128]{2,1,0:T(8,128)S(1)} %select_add_fusion), channel_id=1, source_target_pairs={{0,16},{8,24},{16,0},{24,8},{32,48},{40,56},{48,32},{56,40},{64,80... | collective-permute-start | bytes 196616 | tf_op jit(solution)/shard_map/ppermute | solution.py:50
  30.3 14.3 %copy-start.11 = (f32[16,8,128]{2,1,0:T(8,128)}, f32[16,8,128]{2,1,0:T(8,128)S(1)}, u32[]{:S(2)}) copy-start(f32[16,8,128]{2,1,0:T(8,128)S(1)} %collective-permute-done.5) | copy-start | bytes 196612
  35.5 10.6 %collective-permute-start.11 = (f32[16,8,128]{2,1,0:T(8,128)S(1)}, f32[16,8,128]{2,1,0:T(8,128)S(1)}, u32[]{:S(2)}, u32[]{:S(2)}) collective-permute-start(f32[16,8,128]{2,1,0:T(8,128)S(1)} %multiply_add_fusion), channel_id=1, source_target_pairs={{0,192},{8,200},{16,208},{24,216},{32,224},{40,232},{48,240},{56,2... | collective-permute-start | bytes 196616 | tf_op jit(solution)/shard_map/ppermute | solution.py:54
  36.1 10.0 %collective-permute-start.10 = (f32[16,8,128]{2,1,0:T(8,128)S(1)}, f32[16,8,128]{2,1,0:T(8,128)S(1)}, u32[]{:S(2)}, u32[]{:S(2)}) collective-permute-start(f32[16,8,128]{2,1,0:T(8,128)S(1)} %multiply_add_fusion), channel_id=1, source_target_pairs={{0,128},{8,136},{16,144},{24,152},{32,160},{40,168},{48,176},{56,1... | collective-permute-start | bytes 196616 | tf_op jit(solution)/shard_map/ppermute | solution.py:54
  42.7 5.0 %collective-permute-start.9 = (f32[16,8,128]{2,1,0:T(8,128)S(1)}, f32[16,8,128]{2,1,0:T(8,128)S(1)}, u32[]{:S(2)}, u32[]{:S(2)}) collective-permute-start(f32[16,8,128]{2,1,0:T(8,128)S(1)} %multiply_add_fusion), channel_id=1, source_target_pairs={{0,64},{8,72},{16,80},{24,88},{32,96},{40,104},{48,112},{56,120},{... | collective-permute-start | bytes 196616 | tf_op jit(solution)/shard_map/ppermute | solution.py:54
  48.3 28.3 %collective-permute-start.13 = (bf16[768,1024]{1,0:T(8,128)(2,1)S(1)}, bf16[768,1024]{1,0:T(8,128)(2,1)}, u32[]{:S(2)}, u32[]{:S(2)}) collective-permute-start(bf16[768,1024]{1,0:T(8,128)(2,1)S(1)} %pad_maximum_fusion.refs_1_), channel_id=1, source_target_pairs={{0,16},{8,56},{16,32},{24,8},{32,48},{40,24},{48,0},{56,40},{64,80... | collective-permute-start | bytes 4718600 | tf_op jit(solution)/shard_map/ppermute | solution.py:42
  54.0 49.9 %copy-start.9 = (bf16[256,1024]{1,0:T(8,128)(2,1)S(1)}, bf16[256,1024]{1,0:T(8,128)(2,1)}, u32[]{:S(2)}) copy-start(bf16[256,1024]{1,0:T(8,128)(2,1)} %copy-done.8) | copy-start | bytes 1572868
  54.0 62.3 %copy-start.7 = (bf16[256,1024]{1,0:T(8,128)(2,1)S(1)}, bf16[256,1024]{1,0:T(8,128)(2,1)}, u32[]{:S(2)}) copy-start(bf16[256,1024]{1,0:T(8,128)(2,1)} %copy-done.6) | copy-start | bytes 1572868
  57.3 2.1 %collective-permute-start.16 = (bf16[256,512]{1,0:T(8,128)(2,1)S(1)}, bf16[256,512]{1,0:T(8,128)(2,1)S(1)}, u32[]{:S(2)}, u32[]{:S(2)}) collective-permute-start(bf16[256,512]{1,0:T(8,128)(2,1)S(1)} %get-tuple-element.42), channel_id=1, source_target_pairs={{0,8},{8,0},{16,24},{24,16},{32,40},{40,32},{48,56},{56,48},{64,72... | collective-permute-start | bytes 786440 | tf_op jit(solution)/shard_map/ppermute | solution.py:38
  57.4 46.5 %collective-permute-start.14 = (bf16[768,1024]{1,0:T(8,128)(2,1)S(1)}, bf16[768,1024]{1,0:T(8,128)(2,1)S(1)}, u32[]{:S(2)}, u32[]{:S(2)}) collective-permute-start(bf16[768,1024]{1,0:T(8,128)(2,1)S(1)} %pad_maximum_fusion.refs_1_), channel_id=1, source_target_pairs={{0,48},{8,24},{16,0},{24,40},{32,16},{40,56},{48,32},{56,8},{64,11... | collective-permute-start | bytes 4718600 | tf_op jit(solution)/shard_map/ppermute | solution.py:42
  59.4 67.9 %copy-start.10 = (bf16[256,1024]{1,0:T(8,128)(2,1)S(1)}, bf16[256,1024]{1,0:T(8,128)(2,1)}, u32[]{:S(2)}) copy-start(bf16[256,1024]{1,0:T(8,128)(2,1)} %param.6) | copy-start | bytes 1572868
  59.4 14.3 %collective-permute-start.17 = (bf16[512,512]{1,0:T(8,128)(2,1)S(1)}, bf16[512,512]{1,0:T(8,128)(2,1)S(1)}, u32[]{:S(2)}, u32[]{:S(2)}) collective-permute-start(bf16[512,512]{1,0:T(8,128)(2,1)S(1)} %constant_dynamic-update-slice_fusion.refs_8_), channel_id=1, source_target_pairs={{0,1},{1,2},{2,3},{3,0},{4,5},{5,6},{6,7},{7,4},{8,11},{9,8},{10,9... | collective-permute-start | bytes 1572872 | tf_op jit(solution)/shard_map/ppermute | solution.py:67
  62.2 16.6 %collective-permute-start.20 = (bf16[512,512]{1,0:T(8,128)(2,1)S(1)}, bf16[512,512]{1,0:T(8,128)(2,1)S(1)}, u32[]{:S(2)}, u32[]{:S(2)}) collective-permute-start(bf16[512,512]{1,0:T(8,128)(2,1)S(1)} %constant_dynamic-update-slice_fusion.refs_8_), channel_id=1, source_target_pairs={{0,3},{1,0},{2,1},{3,2},{4,7},{5,4},{6,5},{7,6},{8,9},{9,10},{10,1... | collective-permute-start | bytes 1572872 | tf_op jit(solution)/shard_map/ppermute | solution.py:67
  62.2 28.9 %collective-permute-start.19 = (bf16[512,512]{1,0:T(8,128)(2,1)S(1)}, bf16[512,512]{1,0:T(8,128)(2,1)S(1)}, u32[]{:S(2)}, u32[]{:S(2)}) collective-permute-start(bf16[512,512]{1,0:T(8,128)(2,1)S(1)} %constant_dynamic-update-slice_fusion.refs_8_), channel_id=1, source_target_pairs={{0,4},{1,5},{2,6},{3,7},{4,0},{5,1},{6,2},{7,3},{8,12},{9,13},{10,... | collective-permute-start | bytes 1572872 | tf_op jit(solution)/shard_map/ppermute | solution.py:58
  76.6 39.8 %collective-permute-start.18 = (bf16[768,1024]{1,0:T(8,128)(2,1)}, bf16[768,1024]{1,0:T(8,128)(2,1)S(1)}, u32[]{:S(2)}, u32[]{:S(2)}) collective-permute-start(bf16[768,1024]{1,0:T(8,128)(2,1)} %collective-permute-done.13.refs_3_), channel_id=1, source_target_pairs={{0,16},{8,56},{16,32},{24,8},{32,48},{40,24},{48,0},{56,40},{64,80... | collective-permute-start | bytes 4718600 | tf_op jit(solution)/shard_map/ppermute | solution.py:42
  91.2 12.2 %collective-permute-start.21 = (bf16[512,512]{1,0:T(8,128)(2,1)S(1)}, bf16[512,512]{1,0:T(8,128)(2,1)S(1)}, u32[]{:S(2)}, u32[]{:S(2)}) collective-permute-start(bf16[512,512]{1,0:T(8,128)(2,1)S(1)} %collective-permute-done.19.refs_9_), channel_id=1, source_target_pairs={{0,1},{1,2},{2,3},{3,0},{4,5},{5,6},{6,7},{7,4},{8,11},{9,8},{10,9... | collective-permute-start | bytes 1572872 | tf_op jit(solution)/shard_map/ppermute | solution.py:67
  92.2 14.9 %collective-permute-start.22 = (bf16[512,512]{1,0:T(8,128)(2,1)S(1)}, bf16[512,512]{1,0:T(8,128)(2,1)S(1)}, u32[]{:S(2)}, u32[]{:S(2)}) collective-permute-start(bf16[512,512]{1,0:T(8,128)(2,1)S(1)} %collective-permute-done.19.refs_9_), channel_id=1, source_target_pairs={{0,3},{1,0},{2,1},{3,2},{4,7},{5,4},{6,5},{7,6},{8,9},{9,10},{10,1... | collective-permute-start | bytes 1572872 | tf_op jit(solution)/shard_map/ppermute | solution.py:67
  92.6 18.1 %collective-permute-start.23 = (bf16[512,512]{1,0:T(8,128)(2,1)S(1)}, bf16[512,512]{1,0:T(8,128)(2,1)S(1)}, u32[]{:S(2)}, u32[]{:S(2)}) collective-permute-start(bf16[512,512]{1,0:T(8,128)(2,1)S(1)} %collective-permute-done.17.refs_10_), channel_id=1, source_target_pairs={{0,1},{1,2},{2,3},{3,0},{4,5},{5,6},{6,7},{7,4},{8,11},{9,8},{10,9... | collective-permute-start | bytes 1572872 | tf_op jit(solution)/shard_map/ppermute | solution.py:67
  103.4 13.0 %collective-permute-start.24 = (bf16[512,512]{1,0:T(8,128)(2,1)S(1)}, bf16[512,512]{1,0:T(8,128)(2,1)S(1)}, u32[]{:S(2)}, u32[]{:S(2)}) collective-permute-start(bf16[512,512]{1,0:T(8,128)(2,1)S(1)} %collective-permute-done.21.refs_11_), channel_id=1, source_target_pairs={{0,1},{1,2},{2,3},{3,0},{4,5},{5,6},{6,7},{7,4},{8,11},{9,8},{10,9... | collective-permute-start | bytes 1572872 | tf_op jit(solution)/shard_map/ppermute | solution.py:67
  103.9 12.4 %collective-permute-start.15 = (bf16[256,1024]{1,0:T(8,128)(2,1)S(1)}, bf16[256,1024]{1,0:T(8,128)(2,1)S(1)}, u32[]{:S(2)}, u32[]{:S(2)}) collective-permute-start(bf16[256,1024]{1,0:T(8,128)(2,1)S(1)} %copy-done.9), channel_id=1, source_target_pairs={{0,16},{8,56},{16,32},{24,8},{32,48},{40,24},{48,0},{56,40},{64,80... | collective-permute-start | bytes 1572872 | tf_op jit(solution)/shard_map/ppermute | solution.py:42
  123.0 4.2 %collective-permute-start.25 = (bf16[256,1024]{1,0:T(8,128)(2,1)S(1)}, bf16[256,1024]{1,0:T(8,128)(2,1)S(1)}, u32[]{:S(2)}, u32[]{:S(2)}) collective-permute-start(bf16[256,1024]{1,0:T(8,128)(2,1)S(1)} %get-tuple-element.46), channel_id=1, source_target_pairs={{0,8},{8,0},{16,24},{24,16},{32,40},{40,32},{48,56},{56,48},{64,72... | collective-permute-start | bytes 1572872 | tf_op jit(solution)/shard_map/ppermute | solution.py:38
  (9 other events, 12.7 us)

commit v4 on v3

--- a/solution.py
+++ b/solution.py
@@ -162,10 +162,10 @@
     )(place, drive, queries, rates, weights, carried)
 
 
-def project_kernel(place, *refs):
+def project_kernel(part, place, *refs):
     count_w, count_g = 2 * X, Y * 2
     weights, gated = refs[:count_w], refs[count_w : count_w + count_g]
-    mine, other, left, total, sem = refs[count_w + count_g :]
+    out, left, total, sem = refs[count_w + count_g :]
 
     def shard(s, r, columns):
         first, others = weights[2 * r], weights[2 * r + 1]
@@ -184,7 +184,7 @@
             n = 2 * j + i
             q = lax.rem(h + i, ZH) * Y + origin(y, j, Y)
             columns = pl.ds(pl.multiple_of(q * HALF, HALF), HALF)
-            copy = pltpu.make_async_copy(gated[n], left.at[:, columns], sem.at[n])
+            copy = pltpu.make_async_copy(gated[n].at[pl.ds(part * ROWS, ROWS), :], left.at[:, columns], sem.at[n])
             copy.start()
             copies.append(copy)
     for copy in copies:
@@ -200,26 +200,25 @@
             if s < ZL - 1:
                 total[:, col : col + 256] = product
             else:
-                mine[:, col : col + 256] = product[:ROWS]
-                other[:, col : col + 256] = product[ROWS:].astype(BF16)
-
-
-def project_call(place, weights, gated):
+                out[:, col : col + 256] = product.astype(out.dtype)
+
+
+def project_call(part, kind, place, weights, gated):
     whole = pl.BlockSpec(memory_space=pltpu.VMEM)
     return pl.pallas_call(
-        project_kernel,
+        functools.partial(project_kernel, part),
         in_specs=[pl.BlockSpec(memory_space=pltpu.SMEM)]
         + [whole] * len(weights)
         + [pl.BlockSpec(memory_space=pl.ANY)] * len(gated),
-        out_specs=(whole, whole),
-        out_shape=(jax.ShapeDtypeStruct((ROWS, CHANS), F32), jax.ShapeDtypeStruct((ROWS, CHANS), BF16)),
+        out_specs=whole,
+        out_shape=jax.ShapeDtypeStruct((ROWS, CHANS), kind),
         scratch_shapes=[
-            pltpu.VMEM((2 * ROWS, ZH * Y * HALF), BF16),
-            pltpu.VMEM((2 * ROWS, CHANS), F32),
+            pltpu.VMEM((ROWS, ZH * Y * HALF), BF16),
+            pltpu.VMEM((ROWS, CHANS), F32),
             pltpu.SemaphoreType.DMA((Y * 2,)),
         ],
         compiler_params=pltpu.CompilerParams(vmem_limit_bytes=28 * 1024 * 1024),
-        cost_estimate=pl.CostEstimate(flops=4_300_000_000, bytes_accessed=14_000_000, transcendentals=0),
+        cost_estimate=pl.CostEstimate(flops=2_150_000_000, bytes_accessed=10_000_000, transcendentals=0),
         name="projection",
     )(place, *weights, *gated)
 
@@ -277,20 +276,22 @@
     carried = jnp.where(core == 0, into_chip, decays(rates3, ROWS) * into_chip + in_chip)
     keep, send = response_call(place, drive, queries, rates3, weights3, carried)
     both = jnp.concatenate([keep, swap_core(send)], axis=0)
+    own = [both, around_y(both, 1), around_y(both, -1)]
     across = swap_zh(both)
-    own = around(around_y, both)
+    own.append(around_y(own[1], 1))
     _, a = fence(own[1], behind)
     far = around_x(a, 1)
 
-    across, _, _ = fence(across, own[1], own[2])
+    _, _, across = fence(own[1], own[2], across)
     _, a = fence(ahead, behind0)
     far0 = around_x(a, 1)
     across = around(around_y, across)
 
     weights = (out_weight, column, behind0, behind, ahead0, ahead, far0, far)
     pieces = [v for j in range(Y) for v in (own[j], across[j])]
-    mine, other = project_call(place, weights, pieces)
-    summed = stream.astype(F32) + mine + swap_core(other).astype(F32)
+    other = swap_core(project_call(1, BF16, place, weights, pieces))
+    mine = project_call(0, F32, place, weights, pieces)
+    summed = stream.astype(F32) + mine + other.astype(F32)
     return summed.astype(BF16)
 
 

time: 129 us -> 128 us (level)
  starting transfers between devices: 47 us -> 40 us
  waiting for transfers between devices: 55.5 us -> 60.4 us
  local copies, waits for them, and re-layouts: 9.16 us -> 11.4 us
    ppermute x6, starting transfers between devices: 10.5 us -> 5.59 us  [around_x(): lax.ppermute(v, 'ctx', ctx_pairs(lambda z, x, c: (z, (x + by * (1 - 2 * c...]
    ppermute x6, waiting for transfers between devices: 5 us -> 8.13 us  [around_x(): lax.ppermute(v, 'ctx', ctx_pairs(lambda z, x, c: (z, (x + by * (1 - 2 * c...]
    ppermute x3, waiting for transfers between devices: 7.59 us -> 10.3 us  [around_z(): lax.ppermute(v, 'ctx', ctx_pairs(lambda z, x, c: ((z + by * (1 - 2 * c))...]
    unnamed x33 -> x37, local copies, waits for them, and re-layouts: 7.39 us -> 9.58 us
    ppermute x6, waiting for transfers between devices: 24.6 us -> 22.9 us  [around_y(): return lax.ppermute(v, ('ctx', 'ch'), pairs)]
    pallas_call x1 -> x2, Pallas kernels: 6.68 us -> 6.36 us  [project_call(): pl.pallas_call(functools.partial(project_kernel, part), in_specs=[pl.Bloc...]
  transfers between devices with their start and end apart: 26 -> 26, of which waited for: 14 -> 15; matrix products, arithmetic and copies ran while one was open for 3% -> 3% of each run, Pallas kernels for 5% -> 7%
where the time goes in v4:
time: 128 us
  waiting for transfers between devices  60.4 us (47%)
  starting transfers between devices  40 us (31%)
  Pallas kernels  12.4 us (10%)
  local copies, waits for them, and re-layouts  11.4 us (9%)
  other arithmetic  3.28 us (3%)
    ppermute x6, waiting for transfers between devices, around_y(): return lax.ppermute(v, ('ctx', 'ch'), pairs)  22.9 us
    ppermute x1, waiting for transfers between devices, swap_zh(): return lax.ppermute(v, 'ch', ch_pairs(lambda h, y: (1 - h, y)))  13 us
    ppermute x3, waiting for transfers between devices, around_z(): lax.ppermute(v, 'ctx', ctx_pairs(lambda z, x, c: ((z + by * (1 - 2 * c))...  10.3 us
    unnamed x37, local copies, waits for them, and re-layouts  9.58 us
    ppermute x3, starting transfers between devices, ahead_z(): lax.ppermute(v, 'ctx', ctx_pairs(lambda z, x, c: (z + by, x, c) if z + by...  9.21 us
    ppermute x6, waiting for transfers between devices, around_x(): lax.ppermute(v, 'ctx', ctx_pairs(lambda z, x, c: (z, (x + by * (1 - 2 * c...  8.13 us
    ppermute x6, starting transfers between devices, around_y(): return lax.ppermute(v, ('ctx', 'ch'), pairs)  6.4 us
    pallas_call x2, Pallas kernels, project_call(): pl.pallas_call(functools.partial(project_kernel, part), in_specs=[pl.Bloc...  6.36 us
  transfers between devices with their start and end apart: 26, of which 15 were waited for; matrix products, arithmetic and copies ran while one was open for 3% of the time, Pallas kernels for 7%

profile of v4, /device:TPU:35, one launch (start us, length us, event | category | flops | bytes accessed | tf_op | source)
XLA Modules:
  0.0 127.8 jit_solution(13121296516649025619)
XLA Ops:
  0.9 3.7 %collective-permute-start = (bf16[2,3,1024]{2,0,1:T(2,128)(2,1)S(1)}, bf16[2,3,1024]{2,0,1:T(2,128)(2,1)S(1)}, u32[]{:S(2)}, u32[]{:S(2)}) collective-permute-start(bf16[2,3,1024]{2,0,1:T(2,128)(2,1)S(1)} %slice.3), channel_id=1, source_target_pairs={{0,8},{8,16},{16,24},{24,32},{32,40},{40,48},{48,56},{56,64},{64,7... | collective-permute-start | bytes 36872 | tf_op jit(solution)/shard_map/ppermute | solution.py:253
  7.0 1.4 %copy-done.6 = bf16[256,3,1024]{2,0,1:T(8,128)(2,1)S(1)} copy-done((bf16[256,3,1024]{2,0,1:T(8,128)(2,1)S(1)}, bf16[256,3,1024]{2,0,1:T(8,128)(2,1)}, u32[]{:S(2)}) %copy-start.6) | copy-done | bytes 1572888
  9.2 2.8 %drive_and_ends.1 = (f32[2112,128]{1,0:T(8,128)S(1)}, f32[256,1024]{1,0:T(8,128)S(1)}, f32[16,8,128]{2,1,0:T(8,128)S(1)}) custom-call(bf16[3,256,1024]{2,1,0:T(8,128)(2,1)S(1)} %bitcast.16, f32[3,2,1024]{2,1,0:T(2,128)S(1)} %convert_bitcast_fusion.halo, f32[9,1024]{1,0:T(8,128)S(1)} %reshape.10.taps, f32[16,1024]{1,0:T(8,128)S(1)} %copy-done.11), custom_call_target="tpu_custom_call" | custom-call | flops 1 | bytes 1 | tf_op jit(solution)/shard_map/drive_and_ends/pallas_call | solution.py:115
  14.1 1.4 %collective-permute-start.1 = (f32[16,8,128]{2,1,0:T(8,128)S(1)}, f32[16,8,128]{2,1,0:T(8,128)S(1)}, u32[]{:S(2)}, u32[]{:S(2)}) collective-permute-start(f32[16,8,128]{2,1,0:T(8,128)S(1)} %get-tuple-element.24), channel_id=1, source_target_pairs={{0,8},{8,0},{16,24},{24,16},{32,40},{40,32},{48,56},{56,48},{64,72... | collective-permute-start | bytes 196616 | tf_op jit(solution)/shard_map/ppermute | solution.py:38
  15.4 1.6 %collective-permute-start.8 = (bf16[256,1024]{1,0:T(8,128)(2,1)S(1)}, bf16[256,1024]{1,0:T(8,128)(2,1)S(1)}, u32[]{:S(2)}, u32[]{:S(2)}) collective-permute-start(bf16[256,1024]{1,0:T(8,128)(2,1)S(1)} %copy-done), channel_id=1, source_target_pairs={{0,192},{8,72},{16,208},{24,88},{32,224},{40,104},{48,240},{56,120... | collective-permute-start | bytes 1572872 | tf_op jit(solution)/shard_map/ppermute | solution.py:46
  19.0 1.9 %collective-permute-done.2 = bf16[256,1024]{1,0:T(8,128)(2,1)S(1)} collective-permute-done((bf16[256,1024]{1,0:T(8,128)(2,1)}, bf16[256,1024]{1,0:T(8,128)(2,1)S(1)}, u32[]{:S(2)}, u32[]{:S(2)}) %collective-permute-start.2) | collective-permute-done | bytes 524320 | tf_op jit(solution)/shard_map/ppermute | solution.py:46
  21.3 4.4 %collective-permute-start.6 = (f32[16,8,128]{2,1,0:T(8,128)S(1)}, f32[16,8,128]{2,1,0:T(8,128)S(1)}, u32[]{:S(2)}, u32[]{:S(2)}) collective-permute-start(f32[16,8,128]{2,1,0:T(8,128)S(1)} %select_add_fusion), channel_id=1, source_target_pairs={{0,32},{8,40},{16,48},{24,56},{32,0},{40,8},{48,16},{56,24},{64,96... | collective-permute-start | bytes 196616 | tf_op jit(solution)/shard_map/ppermute | solution.py:50
  25.7 1.7 %collective-permute-done.6 = f32[16,8,128]{2,1,0:T(8,128)S(1)} collective-permute-done((f32[16,8,128]{2,1,0:T(8,128)S(1)}, f32[16,8,128]{2,1,0:T(8,128)S(1)}, u32[]{:S(2)}, u32[]{:S(2)}) %collective-permute-start.6) | collective-permute-done | bytes 65568 | tf_op jit(solution)/shard_map/ppermute | solution.py:50
  27.5 1.7 %collective-permute-done.5 = f32[16,8,128]{2,1,0:T(8,128)S(1)} collective-permute-done((f32[16,8,128]{2,1,0:T(8,128)S(1)}, f32[16,8,128]{2,1,0:T(8,128)S(1)}, u32[]{:S(2)}, u32[]{:S(2)}) %collective-permute-start.5) | collective-permute-done | bytes 65568 | tf_op jit(solution)/shard_map/ppermute | solution.py:50
  29.2 8.5 %collective-permute-done.8 = bf16[256,1024]{1,0:T(8,128)(2,1)S(1)} collective-permute-done((bf16[256,1024]{1,0:T(8,128)(2,1)S(1)}, bf16[256,1024]{1,0:T(8,128)(2,1)S(1)}, u32[]{:S(2)}, u32[]{:S(2)}) %collective-permute-start.8) | collective-permute-done | bytes 524320 | tf_op jit(solution)/shard_map/ppermute | solution.py:46
  38.3 6.6 %collective-permute-start.10 = (f32[16,8,128]{2,1,0:T(8,128)S(1)}, f32[16,8,128]{2,1,0:T(8,128)S(1)}, u32[]{:S(2)}, u32[]{:S(2)}) collective-permute-start(f32[16,8,128]{2,1,0:T(8,128)S(1)} %multiply_add_fusion), channel_id=1, source_target_pairs={{0,128},{8,136},{16,144},{24,152},{32,160},{40,168},{48,176},{56,1... | collective-permute-start | bytes 196616 | tf_op jit(solution)/shard_map/ppermute | solution.py:54
  44.9 1.9 %collective-permute-start.9 = (f32[16,8,128]{2,1,0:T(8,128)S(1)}, f32[16,8,128]{2,1,0:T(8,128)S(1)}, u32[]{:S(2)}, u32[]{:S(2)}) collective-permute-start(f32[16,8,128]{2,1,0:T(8,128)S(1)} %multiply_add_fusion), channel_id=1, source_target_pairs={{0,64},{8,72},{16,80},{24,88},{32,96},{40,104},{48,112},{56,120},{... | collective-permute-start | bytes 196616 | tf_op jit(solution)/shard_map/ppermute | solution.py:54
  48.7 1.3 collective-permute-done.9
  50.6 1.6 %collective-permute-start.13 = (bf16[768,1024]{1,0:T(8,128)(2,1)S(1)}, bf16[768,1024]{1,0:T(8,128)(2,1)S(1)}, u32[]{:S(2)}, u32[]{:S(2)}) collective-permute-start(bf16[768,1024]{1,0:T(8,128)(2,1)S(1)} %pad_maximum_fusion.refs_1_), channel_id=1, source_target_pairs={{0,16},{8,56},{16,32},{24,8},{32,48},{40,24},{48,0},{56,40},{64,80... | collective-permute-start | bytes 4718600 | tf_op jit(solution)/shard_map/ppermute | solution.py:42
  54.1 1.2 copy-done.8
  55.4 1.2 copy-done.10
  56.6 3.3 %response_and_gate.1 = (bf16[256,512]{1,0:T(8,128)(2,1)S(1)}, bf16[256,512]{1,0:T(8,128)(2,1)S(1)}) custom-call(s32[5]{0:T(128)S(1)} %stack.23.place, f32[2112,128]{1,0:T(8,128)S(1)} %copy-done.8, f32[256,1024]{1,0:T(8,128)S(1)} %copy-done.10, f32[16,8,128]{2,1,0:T(8,128)S(1)} %bitcast.15, f32[16,8,128]{2,1,0:T(8,128)S(1)} %bitcast.17, ...), custom_call_target="tpu_custom_call" | custom-call | flops 1 | bytes 1 | tf_op jit(solution)/shard_map/response_and_gate/pallas_call | solution.py:154
  60.2 1.2 collective-permute-done.16
  61.5 2.8 %collective-permute-start.17 = (bf16[512,512]{1,0:T(8,128)(2,1)S(1)}, bf16[512,512]{1,0:T(8,128)(2,1)S(1)}, u32[]{:S(2)}, u32[]{:S(2)}) collective-permute-start(bf16[512,512]{1,0:T(8,128)(2,1)S(1)} %constant_dynamic-update-slice_fusion.refs_8_), channel_id=1, source_target_pairs={{0,1},{1,2},{2,3},{3,0},{4,5},{5,6},{6,7},{7,4},{8,11},{9,8},{10,9... | collective-permute-start | bytes 1572872 | tf_op jit(solution)/shard_map/ppermute | solution.py:67
  64.3 4.8 %collective-permute-start.20 = (bf16[512,512]{1,0:T(8,128)(2,1)S(1)}, bf16[512,512]{1,0:T(8,128)(2,1)S(1)}, u32[]{:S(2)}, u32[]{:S(2)}) collective-permute-start(bf16[512,512]{1,0:T(8,128)(2,1)S(1)} %constant_dynamic-update-slice_fusion.refs_8_), channel_id=1, source_target_pairs={{0,4},{1,5},{2,6},{3,7},{4,0},{5,1},{6,2},{7,3},{8,12},{9,13},{10,... | collective-permute-start | bytes 1572872 | tf_op jit(solution)/shard_map/ppermute | solution.py:58
  69.1 1.3 %collective-permute-done.17.refs_10_ = bf16[512,512]{1,0:T(8,128)(2,1)S(1)} collective-permute-done((bf16[512,512]{1,0:T(8,128)(2,1)S(1)}, bf16[512,512]{1,0:T(8,128)(2,1)S(1)}, u32[]{:S(2)}, u32[]{:S(2)}) %collective-permute-start.17) | collective-permute-done | bytes 524320 | tf_op jit(solution)/shard_map/ppermute | solution.py:67
  70.4 7.1 %collective-permute-done.13.refs_3_ = bf16[768,1024]{1,0:T(8,128)(2,1)S(1)} collective-permute-done((bf16[768,1024]{1,0:T(8,128)(2,1)S(1)}, bf16[768,1024]{1,0:T(8,128)(2,1)S(1)}, u32[]{:S(2)}, u32[]{:S(2)}) %collective-permute-start.13) | collective-permute-done | bytes 1572896 | tf_op jit(solution)/shard_map/ppermute | solution.py:42
  77.5 2.2 %collective-permute-start.18 = (bf16[768,1024]{1,0:T(8,128)(2,1)S(1)}, bf16[768,1024]{1,0:T(8,128)(2,1)S(1)}, u32[]{:S(2)}, u32[]{:S(2)}) collective-permute-start(bf16[768,1024]{1,0:T(8,128)(2,1)S(1)} %collective-permute-done.13.refs_3_), channel_id=1, source_target_pairs={{0,16},{8,56},{16,32},{24,8},{32,48},{40,24},{48,0},{56,40},{64,80... | collective-permute-start | bytes 4718600 | tf_op jit(solution)/shard_map/ppermute | solution.py:42
  79.7 13.0 %collective-permute-done.20.refs_9_ = bf16[512,512]{1,0:T(8,128)(2,1)S(1)} collective-permute-done((bf16[512,512]{1,0:T(8,128)(2,1)S(1)}, bf16[512,512]{1,0:T(8,128)(2,1)S(1)}, u32[]{:S(2)}, u32[]{:S(2)}) %collective-permute-start.20) | collective-permute-done | bytes 524320 | tf_op jit(solution)/shard_map/ppermute | solution.py:58
  94.2 2.1 %collective-permute-start.23 = (bf16[512,512]{1,0:T(8,128)(2,1)S(1)}, bf16[512,512]{1,0:T(8,128)(2,1)S(1)}, u32[]{:S(2)}, u32[]{:S(2)}) collective-permute-start(bf16[512,512]{1,0:T(8,128)(2,1)S(1)} %collective-permute-done.17.refs_10_), channel_id=1, source_target_pairs={{0,1},{1,2},{2,3},{3,0},{4,5},{5,6},{6,7},{7,4},{8,11},{9,8},{10,9... | collective-permute-start | bytes 1572872 | tf_op jit(solution)/shard_map/ppermute | solution.py:67
  96.3 9.6 %collective-permute-done.21.refs_11_ = bf16[512,512]{1,0:T(8,128)(2,1)S(1)} collective-permute-done((bf16[512,512]{1,0:T(8,128)(2,1)S(1)}, bf16[512,512]{1,0:T(8,128)(2,1)S(1)}, u32[]{:S(2)}, u32[]{:S(2)}) %collective-permute-start.21) | collective-permute-done | bytes 524320 | tf_op jit(solution)/shard_map/ppermute | solution.py:67
  106.0 2.8 %collective-permute-done.22.refs_13_ = bf16[512,512]{1,0:T(8,128)(2,1)S(1)} collective-permute-done((bf16[512,512]{1,0:T(8,128)(2,1)S(1)}, bf16[512,512]{1,0:T(8,128)(2,1)S(1)}, u32[]{:S(2)}, u32[]{:S(2)}) %collective-permute-start.22) | collective-permute-done | bytes 524320 | tf_op jit(solution)/shard_map/ppermute | solution.py:67
  108.8 3.5 %collective-permute-done.23.refs_14_ = bf16[512,512]{1,0:T(8,128)(2,1)S(1)} collective-permute-done((bf16[512,512]{1,0:T(8,128)(2,1)S(1)}, bf16[512,512]{1,0:T(8,128)(2,1)S(1)}, u32[]{:S(2)}, u32[]{:S(2)}) %collective-permute-start.23) | collective-permute-done | bytes 524320 | tf_op jit(solution)/shard_map/ppermute | solution.py:67
  112.3 5.6 %collective-permute-done.24.refs_15_ = bf16[512,512]{1,0:T(8,128)(2,1)S(1)} collective-permute-done((bf16[512,512]{1,0:T(8,128)(2,1)S(1)}, bf16[512,512]{1,0:T(8,128)(2,1)S(1)}, u32[]{:S(2)}, u32[]{:S(2)}) %collective-permute-start.24) | collective-permute-done | bytes 524320 | tf_op jit(solution)/shard_map/ppermute | solution.py:67
  118.0 3.2 %projection.3 = bf16[256,1024]{1,0:T(8,128)(2,1)S(1)} custom-call(s32[5]{0:T(128)S(1)} %stack.23.place, bf16[256,1024]{1,0:T(8,128)(2,1)S(1)} %copy-done.1, bf16[768,1024]{1,0:T(8,128)(2,1)S(1)} %pad_maximum_fusion.refs_1_, bf16[256,1024]{1,0:T(8,128)(2,1)S(1)} %copy-done.5, bf16[768,1024]{1,0:T(8,128)(2,1)S(1)} %collective-permute-done.13.refs_3_, ...), custom_call_target="tpu_custom_call" | custom-call | flops 2150000128 | bytes 10000000 | tf_op jit(solution)/shard_map/projection/pallas_call | solution.py:208
  121.2 2.3 %collective-permute-start.25 = (bf16[256,1024]{1,0:T(8,128)(2,1)S(1)}, bf16[256,1024]{1,0:T(8,128)(2,1)S(1)}, u32[]{:S(2)}, u32[]{:S(2)}) collective-permute-start(bf16[256,1024]{1,0:T(8,128)(2,1)S(1)} %projection.3), channel_id=1, source_target_pairs={{0,8},{8,0},{16,24},{24,16},{32,40},{40,32},{48,56},{56,48},{64,72... | collective-permute-start | bytes 1572872 | tf_op jit(solution)/shard_map/ppermute | solution.py:38
  123.5 3.2 %projection.2 = f32[256,1024]{1,0:T(8,128)S(1)} custom-call(s32[5]{0:T(128)S(1)} %stack.23.place, bf16[256,1024]{1,0:T(8,128)(2,1)S(1)} %copy-done.1, bf16[768,1024]{1,0:T(8,128)(2,1)S(1)} %pad_maximum_fusion.refs_1_, bf16[256,1024]{1,0:T(8,128)(2,1)S(1)} %copy-done.5, bf16[768,1024]{1,0:T(8,128)(2,1)S(1)} %collective-permute-done.13.refs_3_, ...), custom_call_target="tpu_custom_call" | custom-call | flops 2150000128 | bytes 10000000 | tf_op jit(solution)/shard_map/projection/pallas_call | solution.py:208
  (71 shorter events, 16.5 us)
Async XLA Ops:
  0.0 15.4 %copy-start = (bf16[256,1024]{1,0:T(8,128)(2,1)S(1)}, bf16[256,1024]{1,0:T(8,128)(2,1)}, u32[]{:S(2)}) copy-start(bf16[256,1024]{1,0:T(8,128)(2,1)} %refs_0_.3) | copy-start | bytes 1572868
  0.9 6.1 %collective-permute-start = (bf16[2,3,1024]{2,0,1:T(2,128)(2,1)S(1)}, bf16[2,3,1024]{2,0,1:T(2,128)(2,1)S(1)}, u32[]{:S(2)}, u32[]{:S(2)}) collective-permute-start(bf16[2,3,1024]{2,0,1:T(2,128)(2,1)S(1)} %slice.3), channel_id=1, source_target_pairs={{0,8},{8,16},{16,24},{24,32},{32,40},{40,48},{48,56},{56,64},{64,7... | collective-permute-start | bytes 36872 | tf_op jit(solution)/shard_map/ppermute | solution.py:253
  4.6 13.6 %collective-permute-start.4 = (bf16[256,1024]{1,0:T(8,128)(2,1)}, bf16[256,1024]{1,0:T(8,128)(2,1)S(1)}, u32[]{:S(2)}, u32[]{:S(2)}) collective-permute-start(bf16[256,1024]{1,0:T(8,128)(2,1)} %refs_0_.3), channel_id=1, source_target_pairs={{0,48},{8,24},{16,0},{24,40},{32,16},{40,56},{48,32},{56,8},{64,11... | collective-permute-start | bytes 1572872 | tf_op jit(solution)/shard_map/ppermute | solution.py:42
  5.6 13.4 %collective-permute-start.3 = (bf16[256,1024]{1,0:T(8,128)(2,1)}, bf16[256,1024]{1,0:T(8,128)(2,1)S(1)}, u32[]{:S(2)}, u32[]{:S(2)}) collective-permute-start(bf16[256,1024]{1,0:T(8,128)(2,1)} %refs_0_.3), channel_id=1, source_target_pairs={{0,16},{8,56},{16,32},{24,8},{32,48},{40,24},{48,0},{56,40},{64,80... | collective-permute-start | bytes 1572872 | tf_op jit(solution)/shard_map/ppermute | solution.py:42
  6.1 14.7 %collective-permute-start.2 = (bf16[256,1024]{1,0:T(8,128)(2,1)}, bf16[256,1024]{1,0:T(8,128)(2,1)S(1)}, u32[]{:S(2)}, u32[]{:S(2)}) collective-permute-start(bf16[256,1024]{1,0:T(8,128)(2,1)} %refs_0_.3), channel_id=1, source_target_pairs={{0,64},{8,200},{16,80},{24,216},{32,96},{40,232},{48,112},{56,248}... | collective-permute-start | bytes 1572872 | tf_op jit(solution)/shard_map/ppermute | solution.py:46
  9.2 7.9 %copy-start.12 = (f32[16,1024]{1,0:T(8,128)S(1)}, f32[16,1024]{1,0:T(8,128)}, u32[]{:S(2)}) copy-start(f32[16,1024]{1,0:T(8,128)} %rates.1) | copy-start | bytes 196612
  14.1 3.1 %collective-permute-start.1 = (f32[16,8,128]{2,1,0:T(8,128)S(1)}, f32[16,8,128]{2,1,0:T(8,128)S(1)}, u32[]{:S(2)}, u32[]{:S(2)}) collective-permute-start(f32[16,8,128]{2,1,0:T(8,128)S(1)} %get-tuple-element.24), channel_id=1, source_target_pairs={{0,8},{8,0},{16,24},{24,16},{32,40},{40,32},{48,56},{56,48},{64,72... | collective-permute-start | bytes 196616 | tf_op jit(solution)/shard_map/ppermute | solution.py:38
  15.4 22.2 %collective-permute-start.8 = (bf16[256,1024]{1,0:T(8,128)(2,1)S(1)}, bf16[256,1024]{1,0:T(8,128)(2,1)S(1)}, u32[]{:S(2)}, u32[]{:S(2)}) collective-permute-start(bf16[256,1024]{1,0:T(8,128)(2,1)S(1)} %copy-done), channel_id=1, source_target_pairs={{0,192},{8,72},{16,208},{24,88},{32,224},{40,104},{48,240},{56,120... | collective-permute-start | bytes 1572872 | tf_op jit(solution)/shard_map/ppermute | solution.py:46
  19.0 27.9 %copy-start.4 = (bf16[256,1024]{1,0:T(8,128)(2,1)}, bf16[256,1024]{1,0:T(8,128)(2,1)S(1)}, u32[]{:S(2)}) copy-start(bf16[256,1024]{1,0:T(8,128)(2,1)S(1)} %collective-permute-done.3.refs_2_) | copy-start | bytes 1572868
  20.9 26.0 %collective-permute-start.12 = (bf16[256,1024]{1,0:T(8,128)(2,1)S(1)}, bf16[256,1024]{1,0:T(8,128)(2,1)}, u32[]{:S(2)}, u32[]{:S(2)}) collective-permute-start(bf16[256,1024]{1,0:T(8,128)(2,1)S(1)} %collective-permute-done.2), channel_id=1, source_target_pairs={{0,64},{8,200},{16,80},{24,216},{32,96},{40,232},{48,112},{56,248}... | collective-permute-start | bytes 1572872 | tf_op jit(solution)/shard_map/ppermute | solution.py:46
  20.9 4.9 %collective-permute-start.7 = (f32[16,8,128]{2,1,0:T(8,128)S(1)}, f32[16,8,128]{2,1,0:T(8,128)S(1)}, u32[]{:S(2)}, u32[]{:S(2)}) collective-permute-start(f32[16,8,128]{2,1,0:T(8,128)S(1)} %select_add_fusion), channel_id=1, source_target_pairs={{0,48},{8,56},{16,32},{24,40},{32,16},{40,24},{48,0},{56,8},{64,11... | collective-permute-start | bytes 196616 | tf_op jit(solution)/shard_map/ppermute | solution.py:50
  21.3 6.1 %collective-permute-start.6 = (f32[16,8,128]{2,1,0:T(8,128)S(1)}, f32[16,8,128]{2,1,0:T(8,128)S(1)}, u32[]{:S(2)}, u32[]{:S(2)}) collective-permute-start(f32[16,8,128]{2,1,0:T(8,128)S(1)} %select_add_fusion), channel_id=1, source_target_pairs={{0,32},{8,40},{16,48},{24,56},{32,0},{40,8},{48,16},{56,24},{64,96... | collective-permute-start | bytes 196616 | tf_op jit(solution)/shard_map/ppermute | solution.py:50
  25.7 3.4 %collective-permute-start.5 = (f32[16,8,128]{2,1,0:T(8,128)S(1)}, f32[16,8,128]{2,1,0:T(8,128)S(1)}, u32[]{:S(2)}, u32[]{:S(2)}) collective-permute-start(f32[16,8,128]{2,1,0:T(8,128)S(1)} %select_add_fusion), channel_id=1, source_target_pairs={{0,16},{8,24},{16,0},{24,8},{32,48},{40,56},{48,32},{56,40},{64,80... | collective-permute-start | bytes 196616 | tf_op jit(solution)/shard_map/ppermute | solution.py:50
  37.6 10.4 %collective-permute-start.11 = (f32[16,8,128]{2,1,0:T(8,128)S(1)}, f32[16,8,128]{2,1,0:T(8,128)S(1)}, u32[]{:S(2)}, u32[]{:S(2)}) collective-permute-start(f32[16,8,128]{2,1,0:T(8,128)S(1)} %multiply_add_fusion), channel_id=1, source_target_pairs={{0,192},{8,200},{16,208},{24,216},{32,224},{40,232},{48,240},{56,2... | collective-permute-start | bytes 196616 | tf_op jit(solution)/shard_map/ppermute | solution.py:54
  38.3 9.9 %collective-permute-start.10 = (f32[16,8,128]{2,1,0:T(8,128)S(1)}, f32[16,8,128]{2,1,0:T(8,128)S(1)}, u32[]{:S(2)}, u32[]{:S(2)}) collective-permute-start(f32[16,8,128]{2,1,0:T(8,128)S(1)} %multiply_add_fusion), channel_id=1, source_target_pairs={{0,128},{8,136},{16,144},{24,152},{32,160},{40,168},{48,176},{56,1... | collective-permute-start | bytes 196616 | tf_op jit(solution)/shard_map/ppermute | solution.py:54
  44.9 5.0 %collective-permute-start.9 = (f32[16,8,128]{2,1,0:T(8,128)S(1)}, f32[16,8,128]{2,1,0:T(8,128)S(1)}, u32[]{:S(2)}, u32[]{:S(2)}) collective-permute-start(f32[16,8,128]{2,1,0:T(8,128)S(1)} %multiply_add_fusion), channel_id=1, source_target_pairs={{0,64},{8,72},{16,80},{24,88},{32,96},{40,104},{48,112},{56,120},{... | collective-permute-start | bytes 196616 | tf_op jit(solution)/shard_map/ppermute | solution.py:54
  50.6 26.9 %collective-permute-start.13 = (bf16[768,1024]{1,0:T(8,128)(2,1)S(1)}, bf16[768,1024]{1,0:T(8,128)(2,1)S(1)}, u32[]{:S(2)}, u32[]{:S(2)}) collective-permute-start(bf16[768,1024]{1,0:T(8,128)(2,1)S(1)} %pad_maximum_fusion.refs_1_), channel_id=1, source_target_pairs={{0,16},{8,56},{16,32},{24,8},{32,48},{40,24},{48,0},{56,40},{64,80... | collective-permute-start | bytes 4718600 | tf_op jit(solution)/shard_map/ppermute | solution.py:42
  56.6 49.4 %copy-start.5 = (bf16[256,1024]{1,0:T(8,128)(2,1)S(1)}, bf16[256,1024]{1,0:T(8,128)(2,1)}, u32[]{:S(2)}) copy-start(bf16[256,1024]{1,0:T(8,128)(2,1)} %copy-done.4) | copy-start | bytes 1572868
  56.6 61.4 %copy-start.1 = (bf16[256,1024]{1,0:T(8,128)(2,1)S(1)}, bf16[256,1024]{1,0:T(8,128)(2,1)}, u32[]{:S(2)}) copy-start(bf16[256,1024]{1,0:T(8,128)(2,1)} %refs_0_.3) | copy-start | bytes 1572868
  56.6 61.4 %copy-start.3 = (bf16[256,1024]{1,0:T(8,128)(2,1)S(1)}, bf16[256,1024]{1,0:T(8,128)(2,1)}, u32[]{:S(2)}) copy-start(bf16[256,1024]{1,0:T(8,128)(2,1)} %copy-done.2) | copy-start | bytes 1572868
  59.8 1.6 %collective-permute-start.16 = (bf16[256,512]{1,0:T(8,128)(2,1)S(1)}, bf16[256,512]{1,0:T(8,128)(2,1)S(1)}, u32[]{:S(2)}, u32[]{:S(2)}) collective-permute-start(bf16[256,512]{1,0:T(8,128)(2,1)S(1)} %get-tuple-element.40), channel_id=1, source_target_pairs={{0,8},{8,0},{16,24},{24,16},{32,40},{40,32},{48,56},{56,48},{64,72... | collective-permute-start | bytes 786440 | tf_op jit(solution)/shard_map/ppermute | solution.py:38
  60.0 46.0 %collective-permute-start.14 = (bf16[768,1024]{1,0:T(8,128)(2,1)S(1)}, bf16[768,1024]{1,0:T(8,128)(2,1)S(1)}, u32[]{:S(2)}, u32[]{:S(2)}) collective-permute-start(bf16[768,1024]{1,0:T(8,128)(2,1)S(1)} %pad_maximum_fusion.refs_1_), channel_id=1, source_target_pairs={{0,48},{8,24},{16,0},{24,40},{32,16},{40,56},{48,32},{56,8},{64,11... | collective-permute-start | bytes 4718600 | tf_op jit(solution)/shard_map/ppermute | solution.py:42
  61.5 8.9 %collective-permute-start.17 = (bf16[512,512]{1,0:T(8,128)(2,1)S(1)}, bf16[512,512]{1,0:T(8,128)(2,1)S(1)}, u32[]{:S(2)}, u32[]{:S(2)}) collective-permute-start(bf16[512,512]{1,0:T(8,128)(2,1)S(1)} %constant_dynamic-update-slice_fusion.refs_8_), channel_id=1, source_target_pairs={{0,1},{1,2},{2,3},{3,0},{4,5},{5,6},{6,7},{7,4},{8,11},{9,8},{10,9... | collective-permute-start | bytes 1572872 | tf_op jit(solution)/shard_map/ppermute | solution.py:67
  64.3 28.5 %collective-permute-start.20 = (bf16[512,512]{1,0:T(8,128)(2,1)S(1)}, bf16[512,512]{1,0:T(8,128)(2,1)S(1)}, u32[]{:S(2)}, u32[]{:S(2)}) collective-permute-start(bf16[512,512]{1,0:T(8,128)(2,1)S(1)} %constant_dynamic-update-slice_fusion.refs_8_), channel_id=1, source_target_pairs={{0,4},{1,5},{2,6},{3,7},{4,0},{5,1},{6,2},{7,3},{8,12},{9,13},{10,... | collective-permute-start | bytes 1572872 | tf_op jit(solution)/shard_map/ppermute | solution.py:58
  69.1 23.7 %collective-permute-start.19 = (bf16[512,512]{1,0:T(8,128)(2,1)S(1)}, bf16[512,512]{1,0:T(8,128)(2,1)S(1)}, u32[]{:S(2)}, u32[]{:S(2)}) collective-permute-start(bf16[512,512]{1,0:T(8,128)(2,1)S(1)} %constant_dynamic-update-slice_fusion.refs_8_), channel_id=1, source_target_pairs={{0,3},{1,0},{2,1},{3,2},{4,7},{5,4},{6,5},{7,6},{8,9},{9,10},{10,1... | collective-permute-start | bytes 1572872 | tf_op jit(solution)/shard_map/ppermute | solution.py:67
  77.5 40.4 %collective-permute-start.18 = (bf16[768,1024]{1,0:T(8,128)(2,1)S(1)}, bf16[768,1024]{1,0:T(8,128)(2,1)S(1)}, u32[]{:S(2)}, u32[]{:S(2)}) collective-permute-start(bf16[768,1024]{1,0:T(8,128)(2,1)S(1)} %collective-permute-done.13.refs_3_), channel_id=1, source_target_pairs={{0,16},{8,56},{16,32},{24,8},{32,48},{40,24},{48,0},{56,40},{64,80... | collective-permute-start | bytes 4718600 | tf_op jit(solution)/shard_map/ppermute | solution.py:42
  92.8 13.1 %collective-permute-start.21 = (bf16[512,512]{1,0:T(8,128)(2,1)S(1)}, bf16[512,512]{1,0:T(8,128)(2,1)S(1)}, u32[]{:S(2)}, u32[]{:S(2)}) collective-permute-start(bf16[512,512]{1,0:T(8,128)(2,1)S(1)} %collective-permute-done.20.refs_9_), channel_id=1, source_target_pairs={{0,1},{1,2},{2,3},{3,0},{4,5},{5,6},{6,7},{7,4},{8,11},{9,8},{10,9... | collective-permute-start | bytes 1572872 | tf_op jit(solution)/shard_map/ppermute | solution.py:67
  93.6 15.2 %collective-permute-start.22 = (bf16[512,512]{1,0:T(8,128)(2,1)S(1)}, bf16[512,512]{1,0:T(8,128)(2,1)S(1)}, u32[]{:S(2)}, u32[]{:S(2)}) collective-permute-start(bf16[512,512]{1,0:T(8,128)(2,1)S(1)} %collective-permute-done.20.refs_9_), channel_id=1, source_target_pairs={{0,3},{1,0},{2,1},{3,2},{4,7},{5,4},{6,5},{7,6},{8,9},{9,10},{10,1... | collective-permute-start | bytes 1572872 | tf_op jit(solution)/shard_map/ppermute | solution.py:67
  94.2 18.1 %collective-permute-start.23 = (bf16[512,512]{1,0:T(8,128)(2,1)S(1)}, bf16[512,512]{1,0:T(8,128)(2,1)S(1)}, u32[]{:S(2)}, u32[]{:S(2)}) collective-permute-start(bf16[512,512]{1,0:T(8,128)(2,1)S(1)} %collective-permute-done.17.refs_10_), channel_id=1, source_target_pairs={{0,1},{1,2},{2,3},{3,0},{4,5},{5,6},{6,7},{7,4},{8,11},{9,8},{10,9... | collective-permute-start | bytes 1572872 | tf_op jit(solution)/shard_map/ppermute | solution.py:67
  105.9 12.0 %collective-permute-start.24 = (bf16[512,512]{1,0:T(8,128)(2,1)S(1)}, bf16[512,512]{1,0:T(8,128)(2,1)S(1)}, u32[]{:S(2)}, u32[]{:S(2)}) collective-permute-start(bf16[512,512]{1,0:T(8,128)(2,1)S(1)} %collective-permute-done.21.refs_11_), channel_id=1, source_target_pairs={{0,1},{1,2},{2,3},{3,0},{4,5},{5,6},{6,7},{7,4},{8,11},{9,8},{10,9... | collective-permute-start | bytes 1572872 | tf_op jit(solution)/shard_map/ppermute | solution.py:67
  106.0 12.0 %collective-permute-start.15 = (bf16[256,1024]{1,0:T(8,128)(2,1)S(1)}, bf16[256,1024]{1,0:T(8,128)(2,1)S(1)}, u32[]{:S(2)}, u32[]{:S(2)}) collective-permute-start(bf16[256,1024]{1,0:T(8,128)(2,1)S(1)} %copy-done.5), channel_id=1, source_target_pairs={{0,16},{8,56},{16,32},{24,8},{32,48},{40,24},{48,0},{56,40},{64,80... | collective-permute-start | bytes 1572872 | tf_op jit(solution)/shard_map/ppermute | solution.py:42
  121.2 5.5 %collective-permute-start.25 = (bf16[256,1024]{1,0:T(8,128)(2,1)S(1)}, bf16[256,1024]{1,0:T(8,128)(2,1)S(1)}, u32[]{:S(2)}, u32[]{:S(2)}) collective-permute-start(bf16[256,1024]{1,0:T(8,128)(2,1)S(1)} %projection.3), channel_id=1, source_target_pairs={{0,8},{8,0},{16,24},{24,16},{32,40},{40,32},{48,56},{56,48},{64,72... | collective-permute-start | bytes 1572872 | tf_op jit(solution)/shard_map/ppermute | solution.py:38
  (11 other events, 15.6 us)

commit v5 on v4

--- a/solution.py
+++ b/solution.py
@@ -87,9 +87,9 @@
         for start in range(0, ROWS, step):
             filtered = []
             for s in range(3):
-                total = taps[s : s + 1, lanes] * wide[s, 8 + start : 8 + start + step, :]
-                total += taps[3 + s : 4 + s, lanes] * wide[s, 7 + start : 7 + start + step, :]
-                total += taps[6 + s : 7 + s, lanes] * wide[s, 6 + start : 6 + start + step, :]
+                total = taps[0, s : s + 1, lanes] * wide[s, 8 + start : 8 + start + step, :]
+                total += taps[1, s : s + 1, lanes] * wide[s, 7 + start : 7 + start + step, :]
+                total += taps[2, s : s + 1, lanes] * wide[s, 6 + start : 6 + start + step, :]
                 filtered.append(total)
             queries[start : start + step, lanes] = filtered[0]
             drive[pl.ds(base + start, step), :] = filtered[1] * filtered[2]
@@ -254,7 +254,7 @@
     z_behind, z_ahead = around_z(out_weight, 1), around_z(out_weight, -1)
     behind0, ahead0 = around_x(out_weight, 1), around_x(out_weight, -1)
     halo = halo.transpose(1, 0, 2).astype(F32)
-    drive, queries, ends = drive_call(proj, halo, short_taps.reshape(9, CHANS), decay_rates)
+    drive, queries, ends = drive_call(proj, halo, short_taps, decay_rates)
 
     rates3 = decay_rates.reshape(MODES, LANES, 128)
     weights3 = residues.reshape(MODES, LANES, 128)

time: 128 us -> 129 us (level)
    unnamed x37 -> x39, local copies, waits for them, and re-layouts: 9.58 us -> 10.4 us
  transfers between devices with their start and end apart: 26 -> 26, of which waited for: 15 -> 14; matrix products, arithmetic and copies ran while one was open for 3% -> 3% of each run, Pallas kernels for 7% -> 7%
where the time goes in v5:
time: 129 us
  waiting for transfers between devices  61.1 us (47%)
  starting transfers between devices  40 us (31%)
  Pallas kernels  12.5 us (10%)
  local copies, waits for them, and re-layouts  11.4 us (9%)
  other arithmetic  3.28 us (3%)
    ppermute x6, waiting for transfers between devices, around_y(): return lax.ppermute(v, ('ctx', 'ch'), pairs)  23.8 us
    ppermute x1, waiting for transfers between devices, swap_zh(): return lax.ppermute(v, 'ch', ch_pairs(lambda h, y: (1 - h, y)))  13 us
    ppermute x3, waiting for transfers between devices, around_z(): lax.ppermute(v, 'ctx', ctx_pairs(lambda z, x, c: ((z + by * (1 - 2 * c))...  10.8 us
    unnamed x39, local copies, waits for them, and re-layouts  10.4 us
    ppermute x3, starting transfers between devices, ahead_z(): lax.ppermute(v, 'ctx', ctx_pairs(lambda z, x, c: (z + by, x, c) if z + by...  9.21 us
    ppermute x6, waiting for transfers between devices, around_x(): lax.ppermute(v, 'ctx', ctx_pairs(lambda z, x, c: (z, (x + by * (1 - 2 * c...  7.41 us
    ppermute x6, starting transfers between devices, around_x(): lax.ppermute(v, 'ctx', ctx_pairs(lambda z, x, c: (z, (x + by * (1 - 2 * c...  6.63 us
    ppermute x6, starting transfers between devices, around_y(): return lax.ppermute(v, ('ctx', 'ch'), pairs)  6.5 us
  transfers between devices with their start and end apart: 26, of which 14 were waited for; matrix products, arithmetic and copies ran while one was open for 3% of the time, Pallas kernels for 7%

profile of v5, /device:TPU:35, one launch (start us, length us, event | category | flops | bytes accessed | tf_op | source)
XLA Modules:
  0.0 128.5 jit_solution(7312430042190682276)
XLA Ops:
  0.9 3.7 %collective-permute-start = (bf16[2,3,1024]{2,0,1:T(2,128)(2,1)S(1)}, bf16[2,3,1024]{2,0,1:T(2,128)(2,1)S(1)}, u32[]{:S(2)}, u32[]{:S(2)}) collective-permute-start(bf16[2,3,1024]{2,0,1:T(2,128)(2,1)S(1)} %slice.3), channel_id=1, source_target_pairs={{0,8},{8,16},{16,24},{24,32},{32,40},{40,48},{48,56},{56,64},{64,7... | collective-permute-start | bytes 36872 | tf_op jit(solution)/shard_map/ppermute | solution.py:253
  6.1 1.4 %copy-done.6 = bf16[256,3,1024]{2,0,1:T(8,128)(2,1)S(1)} copy-done((bf16[256,3,1024]{2,0,1:T(8,128)(2,1)S(1)}, bf16[256,3,1024]{2,0,1:T(8,128)(2,1)}, u32[]{:S(2)}) %copy-start.6) | copy-done | bytes 1572888
  9.2 2.8 %drive_and_ends.1 = (f32[2112,128]{1,0:T(8,128)S(1)}, f32[256,1024]{1,0:T(8,128)S(1)}, f32[16,8,128]{2,1,0:T(8,128)S(1)}) custom-call(bf16[3,256,1024]{2,1,0:T(8,128)(2,1)S(1)} %bitcast.16, f32[3,2,1024]{2,1,0:T(2,128)S(1)} %convert_bitcast_fusion.halo, f32[3,3,1024]{2,1,0:T(4,128)S(1)} %copy-done.13, f32[16,1024]{1,0:T(8,128)S(1)} %copy-done.11), custom_call_target="tpu_custom_call" | custom-call | flops 1 | bytes 1 | tf_op jit(solution)/shard_map/drive_and_ends/pallas_call | solution.py:115
  14.0 1.4 %collective-permute-start.1 = (f32[16,8,128]{2,1,0:T(8,128)S(1)}, f32[16,8,128]{2,1,0:T(8,128)S(1)}, u32[]{:S(2)}, u32[]{:S(2)}) collective-permute-start(f32[16,8,128]{2,1,0:T(8,128)S(1)} %get-tuple-element.24), channel_id=1, source_target_pairs={{0,8},{8,0},{16,24},{24,16},{32,40},{40,32},{48,56},{56,48},{64,72... | collective-permute-start | bytes 196616 | tf_op jit(solution)/shard_map/ppermute | solution.py:38
  15.4 1.6 %collective-permute-start.8 = (bf16[256,1024]{1,0:T(8,128)(2,1)S(1)}, bf16[256,1024]{1,0:T(8,128)(2,1)S(1)}, u32[]{:S(2)}, u32[]{:S(2)}) collective-permute-start(bf16[256,1024]{1,0:T(8,128)(2,1)S(1)} %copy-done), channel_id=1, source_target_pairs={{0,192},{8,72},{16,208},{24,88},{32,224},{40,104},{48,240},{56,120... | collective-permute-start | bytes 1572872 | tf_op jit(solution)/shard_map/ppermute | solution.py:46
  19.0 1.9 %collective-permute-done.2 = bf16[256,1024]{1,0:T(8,128)(2,1)S(1)} collective-permute-done((bf16[256,1024]{1,0:T(8,128)(2,1)}, bf16[256,1024]{1,0:T(8,128)(2,1)S(1)}, u32[]{:S(2)}, u32[]{:S(2)}) %collective-permute-start.2) | collective-permute-done | bytes 524320 | tf_op jit(solution)/shard_map/ppermute | solution.py:46
  21.3 4.0 %collective-permute-start.6 = (f32[16,8,128]{2,1,0:T(8,128)S(1)}, f32[16,8,128]{2,1,0:T(8,128)S(1)}, u32[]{:S(2)}, u32[]{:S(2)}) collective-permute-start(f32[16,8,128]{2,1,0:T(8,128)S(1)} %select_add_fusion), channel_id=1, source_target_pairs={{0,32},{8,40},{16,48},{24,56},{32,0},{40,8},{48,16},{56,24},{64,96... | collective-permute-start | bytes 196616 | tf_op jit(solution)/shard_map/ppermute | solution.py:50
  25.3 1.7 %collective-permute-done.6 = f32[16,8,128]{2,1,0:T(8,128)S(1)} collective-permute-done((f32[16,8,128]{2,1,0:T(8,128)S(1)}, f32[16,8,128]{2,1,0:T(8,128)S(1)}, u32[]{:S(2)}, u32[]{:S(2)}) %collective-permute-start.6) | collective-permute-done | bytes 65568 | tf_op jit(solution)/shard_map/ppermute | solution.py:50
  27.0 1.7 %collective-permute-done.5 = f32[16,8,128]{2,1,0:T(8,128)S(1)} collective-permute-done((f32[16,8,128]{2,1,0:T(8,128)S(1)}, f32[16,8,128]{2,1,0:T(8,128)S(1)}, u32[]{:S(2)}, u32[]{:S(2)}) %collective-permute-start.5) | collective-permute-done | bytes 65568 | tf_op jit(solution)/shard_map/ppermute | solution.py:50
  28.8 8.9 %collective-permute-done.8 = bf16[256,1024]{1,0:T(8,128)(2,1)S(1)} collective-permute-done((bf16[256,1024]{1,0:T(8,128)(2,1)S(1)}, bf16[256,1024]{1,0:T(8,128)(2,1)S(1)}, u32[]{:S(2)}, u32[]{:S(2)}) %collective-permute-start.8) | collective-permute-done | bytes 524320 | tf_op jit(solution)/shard_map/ppermute | solution.py:46
  38.4 6.6 %collective-permute-start.10 = (f32[16,8,128]{2,1,0:T(8,128)S(1)}, f32[16,8,128]{2,1,0:T(8,128)S(1)}, u32[]{:S(2)}, u32[]{:S(2)}) collective-permute-start(f32[16,8,128]{2,1,0:T(8,128)S(1)} %multiply_add_fusion), channel_id=1, source_target_pairs={{0,128},{8,136},{16,144},{24,152},{32,160},{40,168},{48,176},{56,1... | collective-permute-start | bytes 196616 | tf_op jit(solution)/shard_map/ppermute | solution.py:54
  45.0 1.9 %collective-permute-start.9 = (f32[16,8,128]{2,1,0:T(8,128)S(1)}, f32[16,8,128]{2,1,0:T(8,128)S(1)}, u32[]{:S(2)}, u32[]{:S(2)}) collective-permute-start(f32[16,8,128]{2,1,0:T(8,128)S(1)} %multiply_add_fusion), channel_id=1, source_target_pairs={{0,64},{8,72},{16,80},{24,88},{32,96},{40,104},{48,112},{56,120},{... | collective-permute-start | bytes 196616 | tf_op jit(solution)/shard_map/ppermute | solution.py:54
  48.7 1.3 collective-permute-done.9
  50.6 2.3 %collective-permute-start.13 = (bf16[768,1024]{1,0:T(8,128)(2,1)S(1)}, bf16[768,1024]{1,0:T(8,128)(2,1)S(1)}, u32[]{:S(2)}, u32[]{:S(2)}) collective-permute-start(bf16[768,1024]{1,0:T(8,128)(2,1)S(1)} %pad_maximum_fusion.refs_1_), channel_id=1, source_target_pairs={{0,16},{8,56},{16,32},{24,8},{32,48},{40,24},{48,0},{56,40},{64,80... | collective-permute-start | bytes 4718600 | tf_op jit(solution)/shard_map/ppermute | solution.py:42
  54.8 1.2 copy-done.8
  56.1 1.2 copy-done.10
  57.3 3.3 %response_and_gate.1 = (bf16[256,512]{1,0:T(8,128)(2,1)S(1)}, bf16[256,512]{1,0:T(8,128)(2,1)S(1)}) custom-call(s32[5]{0:T(128)S(1)} %stack.23.place, f32[2112,128]{1,0:T(8,128)S(1)} %copy-done.8, f32[256,1024]{1,0:T(8,128)S(1)} %copy-done.10, f32[16,8,128]{2,1,0:T(8,128)S(1)} %bitcast.15, f32[16,8,128]{2,1,0:T(8,128)S(1)} %bitcast.17, ...), custom_call_target="tpu_custom_call" | custom-call | flops 1 | bytes 1 | tf_op jit(solution)/shard_map/response_and_gate/pallas_call | solution.py:154
  60.8 1.4 %collective-permute-done.16 = bf16[256,512]{1,0:T(8,128)(2,1)S(1)} collective-permute-done((bf16[256,512]{1,0:T(8,128)(2,1)S(1)}, bf16[256,512]{1,0:T(8,128)(2,1)S(1)}, u32[]{:S(2)}, u32[]{:S(2)}) %collective-permute-start.16) | collective-permute-done | bytes 262176 | tf_op jit(solution)/shard_map/ppermute | solution.py:38
  62.2 2.8 %collective-permute-start.17 = (bf16[512,512]{1,0:T(8,128)(2,1)S(1)}, bf16[512,512]{1,0:T(8,128)(2,1)S(1)}, u32[]{:S(2)}, u32[]{:S(2)}) collective-permute-start(bf16[512,512]{1,0:T(8,128)(2,1)S(1)} %constant_dynamic-update-slice_fusion.refs_8_), channel_id=1, source_target_pairs={{0,1},{1,2},{2,3},{3,0},{4,5},{5,6},{6,7},{7,4},{8,11},{9,8},{10,9... | collective-permute-start | bytes 1572872 | tf_op jit(solution)/shard_map/ppermute | solution.py:67
  65.0 4.0 %collective-permute-start.20 = (bf16[512,512]{1,0:T(8,128)(2,1)S(1)}, bf16[512,512]{1,0:T(8,128)(2,1)S(1)}, u32[]{:S(2)}, u32[]{:S(2)}) collective-permute-start(bf16[512,512]{1,0:T(8,128)(2,1)S(1)} %constant_dynamic-update-slice_fusion.refs_8_), channel_id=1, source_target_pairs={{0,4},{1,5},{2,6},{3,7},{4,0},{5,1},{6,2},{7,3},{8,12},{9,13},{10,... | collective-permute-start | bytes 1572872 | tf_op jit(solution)/shard_map/ppermute | solution.py:58
  69.0 2.9 %collective-permute-done.17.refs_10_ = bf16[512,512]{1,0:T(8,128)(2,1)S(1)} collective-permute-done((bf16[512,512]{1,0:T(8,128)(2,1)S(1)}, bf16[512,512]{1,0:T(8,128)(2,1)S(1)}, u32[]{:S(2)}, u32[]{:S(2)}) %collective-permute-start.17) | collective-permute-done | bytes 524320 | tf_op jit(solution)/shard_map/ppermute | solution.py:67
  71.9 6.4 %collective-permute-done.13.refs_3_ = bf16[768,1024]{1,0:T(8,128)(2,1)S(1)} collective-permute-done((bf16[768,1024]{1,0:T(8,128)(2,1)S(1)}, bf16[768,1024]{1,0:T(8,128)(2,1)S(1)}, u32[]{:S(2)}, u32[]{:S(2)}) %collective-permute-start.13) | collective-permute-done | bytes 1572896 | tf_op jit(solution)/shard_map/ppermute | solution.py:42
  78.3 2.2 %collective-permute-start.18 = (bf16[768,1024]{1,0:T(8,128)(2,1)S(1)}, bf16[768,1024]{1,0:T(8,128)(2,1)S(1)}, u32[]{:S(2)}, u32[]{:S(2)}) collective-permute-start(bf16[768,1024]{1,0:T(8,128)(2,1)S(1)} %collective-permute-done.13.refs_3_), channel_id=1, source_target_pairs={{0,16},{8,56},{16,32},{24,8},{32,48},{40,24},{48,0},{56,40},{64,80... | collective-permute-start | bytes 4718600 | tf_op jit(solution)/shard_map/ppermute | solution.py:42
  80.5 13.0 %collective-permute-done.20.refs_9_ = bf16[512,512]{1,0:T(8,128)(2,1)S(1)} collective-permute-done((bf16[512,512]{1,0:T(8,128)(2,1)S(1)}, bf16[512,512]{1,0:T(8,128)(2,1)S(1)}, u32[]{:S(2)}, u32[]{:S(2)}) %collective-permute-start.20) | collective-permute-done | bytes 524320 | tf_op jit(solution)/shard_map/ppermute | solution.py:58
  95.0 2.1 %collective-permute-start.23 = (bf16[512,512]{1,0:T(8,128)(2,1)S(1)}, bf16[512,512]{1,0:T(8,128)(2,1)S(1)}, u32[]{:S(2)}, u32[]{:S(2)}) collective-permute-start(bf16[512,512]{1,0:T(8,128)(2,1)S(1)} %collective-permute-done.17.refs_10_), channel_id=1, source_target_pairs={{0,1},{1,2},{2,3},{3,0},{4,5},{5,6},{6,7},{7,4},{8,11},{9,8},{10,9... | collective-permute-start | bytes 1572872 | tf_op jit(solution)/shard_map/ppermute | solution.py:67
  97.1 9.5 %collective-permute-done.21.refs_11_ = bf16[512,512]{1,0:T(8,128)(2,1)S(1)} collective-permute-done((bf16[512,512]{1,0:T(8,128)(2,1)S(1)}, bf16[512,512]{1,0:T(8,128)(2,1)S(1)}, u32[]{:S(2)}, u32[]{:S(2)}) %collective-permute-start.21) | collective-permute-done | bytes 524320 | tf_op jit(solution)/shard_map/ppermute | solution.py:67
  107.3 2.3 %collective-permute-done.22.refs_13_ = bf16[512,512]{1,0:T(8,128)(2,1)S(1)} collective-permute-done((bf16[512,512]{1,0:T(8,128)(2,1)S(1)}, bf16[512,512]{1,0:T(8,128)(2,1)S(1)}, u32[]{:S(2)}, u32[]{:S(2)}) %collective-permute-start.22) | collective-permute-done | bytes 524320 | tf_op jit(solution)/shard_map/ppermute | solution.py:67
  109.5 3.5 %collective-permute-done.23.refs_14_ = bf16[512,512]{1,0:T(8,128)(2,1)S(1)} collective-permute-done((bf16[512,512]{1,0:T(8,128)(2,1)S(1)}, bf16[512,512]{1,0:T(8,128)(2,1)S(1)}, u32[]{:S(2)}, u32[]{:S(2)}) %collective-permute-start.23) | collective-permute-done | bytes 524320 | tf_op jit(solution)/shard_map/ppermute | solution.py:67
  113.1 5.6 %collective-permute-done.24.refs_15_ = bf16[512,512]{1,0:T(8,128)(2,1)S(1)} collective-permute-done((bf16[512,512]{1,0:T(8,128)(2,1)S(1)}, bf16[512,512]{1,0:T(8,128)(2,1)S(1)}, u32[]{:S(2)}, u32[]{:S(2)}) %collective-permute-start.24) | collective-permute-done | bytes 524320 | tf_op jit(solution)/shard_map/ppermute | solution.py:67
  118.7 3.2 %projection.3 = bf16[256,1024]{1,0:T(8,128)(2,1)S(1)} custom-call(s32[5]{0:T(128)S(1)} %stack.23.place, bf16[256,1024]{1,0:T(8,128)(2,1)S(1)} %copy-done.1, bf16[768,1024]{1,0:T(8,128)(2,1)S(1)} %pad_maximum_fusion.refs_1_, bf16[256,1024]{1,0:T(8,128)(2,1)S(1)} %copy-done.5, bf16[768,1024]{1,0:T(8,128)(2,1)S(1)} %collective-permute-done.13.refs_3_, ...), custom_call_target="tpu_custom_call" | custom-call | flops 2150000128 | bytes 10000000 | tf_op jit(solution)/shard_map/projection/pallas_call | solution.py:208
  121.9 2.4 %collective-permute-start.25 = (bf16[256,1024]{1,0:T(8,128)(2,1)S(1)}, bf16[256,1024]{1,0:T(8,128)(2,1)S(1)}, u32[]{:S(2)}, u32[]{:S(2)}) collective-permute-start(bf16[256,1024]{1,0:T(8,128)(2,1)S(1)} %projection.3), channel_id=1, source_target_pairs={{0,8},{8,0},{16,24},{24,16},{32,40},{40,32},{48,56},{56,48},{64,72... | collective-permute-start | bytes 1572872 | tf_op jit(solution)/shard_map/ppermute | solution.py:38
  124.3 3.2 %projection.2 = f32[256,1024]{1,0:T(8,128)S(1)} custom-call(s32[5]{0:T(128)S(1)} %stack.23.place, bf16[256,1024]{1,0:T(8,128)(2,1)S(1)} %copy-done.1, bf16[768,1024]{1,0:T(8,128)(2,1)S(1)} %pad_maximum_fusion.refs_1_, bf16[256,1024]{1,0:T(8,128)(2,1)S(1)} %copy-done.5, bf16[768,1024]{1,0:T(8,128)(2,1)S(1)} %collective-permute-done.13.refs_3_, ...), custom_call_target="tpu_custom_call" | custom-call | flops 2150000128 | bytes 10000000 | tf_op jit(solution)/shard_map/projection/pallas_call | solution.py:208
  (72 shorter events, 16.9 us)
Async XLA Ops:
  0.0 15.4 %copy-start = (bf16[256,1024]{1,0:T(8,128)(2,1)S(1)}, bf16[256,1024]{1,0:T(8,128)(2,1)}, u32[]{:S(2)}) copy-start(bf16[256,1024]{1,0:T(8,128)(2,1)} %refs_0_.3) | copy-start | bytes 1572868
  0.9 5.2 %collective-permute-start = (bf16[2,3,1024]{2,0,1:T(2,128)(2,1)S(1)}, bf16[2,3,1024]{2,0,1:T(2,128)(2,1)S(1)}, u32[]{:S(2)}, u32[]{:S(2)}) collective-permute-start(bf16[2,3,1024]{2,0,1:T(2,128)(2,1)S(1)} %slice.3), channel_id=1, source_target_pairs={{0,8},{8,16},{16,24},{24,32},{32,40},{40,48},{48,56},{56,64},{64,7... | collective-permute-start | bytes 36872 | tf_op jit(solution)/shard_map/ppermute | solution.py:253
  4.6 13.6 %collective-permute-start.4 = (bf16[256,1024]{1,0:T(8,128)(2,1)}, bf16[256,1024]{1,0:T(8,128)(2,1)S(1)}, u32[]{:S(2)}, u32[]{:S(2)}) collective-permute-start(bf16[256,1024]{1,0:T(8,128)(2,1)} %refs_0_.3), channel_id=1, source_target_pairs={{0,48},{8,24},{16,0},{24,40},{32,16},{40,56},{48,32},{56,8},{64,11... | collective-permute-start | bytes 1572872 | tf_op jit(solution)/shard_map/ppermute | solution.py:42
  5.6 13.4 %collective-permute-start.3 = (bf16[256,1024]{1,0:T(8,128)(2,1)}, bf16[256,1024]{1,0:T(8,128)(2,1)S(1)}, u32[]{:S(2)}, u32[]{:S(2)}) collective-permute-start(bf16[256,1024]{1,0:T(8,128)(2,1)} %refs_0_.3), channel_id=1, source_target_pairs={{0,16},{8,56},{16,32},{24,8},{32,48},{40,24},{48,0},{56,40},{64,80... | collective-permute-start | bytes 1572872 | tf_op jit(solution)/shard_map/ppermute | solution.py:42
  6.1 14.8 %collective-permute-start.2 = (bf16[256,1024]{1,0:T(8,128)(2,1)}, bf16[256,1024]{1,0:T(8,128)(2,1)S(1)}, u32[]{:S(2)}, u32[]{:S(2)}) collective-permute-start(bf16[256,1024]{1,0:T(8,128)(2,1)} %refs_0_.3), channel_id=1, source_target_pairs={{0,64},{8,200},{16,80},{24,216},{32,96},{40,232},{48,112},{56,248}... | collective-permute-start | bytes 1572872 | tf_op jit(solution)/shard_map/ppermute | solution.py:46
  9.2 7.9 %copy-start.12 = (f32[16,1024]{1,0:T(8,128)S(1)}, f32[16,1024]{1,0:T(8,128)}, u32[]{:S(2)}) copy-start(f32[16,1024]{1,0:T(8,128)} %rates.1) | copy-start | bytes 196612
  14.0 3.1 %collective-permute-start.1 = (f32[16,8,128]{2,1,0:T(8,128)S(1)}, f32[16,8,128]{2,1,0:T(8,128)S(1)}, u32[]{:S(2)}, u32[]{:S(2)}) collective-permute-start(f32[16,8,128]{2,1,0:T(8,128)S(1)} %get-tuple-element.24), channel_id=1, source_target_pairs={{0,8},{8,0},{16,24},{24,16},{32,40},{40,32},{48,56},{56,48},{64,72... | collective-permute-start | bytes 196616 | tf_op jit(solution)/shard_map/ppermute | solution.py:38
  15.4 22.3 %collective-permute-start.8 = (bf16[256,1024]{1,0:T(8,128)(2,1)S(1)}, bf16[256,1024]{1,0:T(8,128)(2,1)S(1)}, u32[]{:S(2)}, u32[]{:S(2)}) collective-permute-start(bf16[256,1024]{1,0:T(8,128)(2,1)S(1)} %copy-done), channel_id=1, source_target_pairs={{0,192},{8,72},{16,208},{24,88},{32,224},{40,104},{48,240},{56,120... | collective-permute-start | bytes 1572872 | tf_op jit(solution)/shard_map/ppermute | solution.py:46
  19.0 27.9 %copy-start.4 = (bf16[256,1024]{1,0:T(8,128)(2,1)}, bf16[256,1024]{1,0:T(8,128)(2,1)S(1)}, u32[]{:S(2)}) copy-start(bf16[256,1024]{1,0:T(8,128)(2,1)S(1)} %collective-permute-done.3.refs_2_) | copy-start | bytes 1572868
  20.9 26.1 %collective-permute-start.12 = (bf16[256,1024]{1,0:T(8,128)(2,1)S(1)}, bf16[256,1024]{1,0:T(8,128)(2,1)}, u32[]{:S(2)}, u32[]{:S(2)}) collective-permute-start(bf16[256,1024]{1,0:T(8,128)(2,1)S(1)} %collective-permute-done.2), channel_id=1, source_target_pairs={{0,64},{8,200},{16,80},{24,216},{32,96},{40,232},{48,112},{56,248}... | collective-permute-start | bytes 1572872 | tf_op jit(solution)/shard_map/ppermute | solution.py:46
  20.9 4.4 %collective-permute-start.7 = (f32[16,8,128]{2,1,0:T(8,128)S(1)}, f32[16,8,128]{2,1,0:T(8,128)S(1)}, u32[]{:S(2)}, u32[]{:S(2)}) collective-permute-start(f32[16,8,128]{2,1,0:T(8,128)S(1)} %select_add_fusion), channel_id=1, source_target_pairs={{0,48},{8,56},{16,32},{24,40},{32,16},{40,24},{48,0},{56,8},{64,11... | collective-permute-start | bytes 196616 | tf_op jit(solution)/shard_map/ppermute | solution.py:50
  21.3 5.7 %collective-permute-start.6 = (f32[16,8,128]{2,1,0:T(8,128)S(1)}, f32[16,8,128]{2,1,0:T(8,128)S(1)}, u32[]{:S(2)}, u32[]{:S(2)}) collective-permute-start(f32[16,8,128]{2,1,0:T(8,128)S(1)} %select_add_fusion), channel_id=1, source_target_pairs={{0,32},{8,40},{16,48},{24,56},{32,0},{40,8},{48,16},{56,24},{64,96... | collective-permute-start | bytes 196616 | tf_op jit(solution)/shard_map/ppermute | solution.py:50
  25.3 3.4 %collective-permute-start.5 = (f32[16,8,128]{2,1,0:T(8,128)S(1)}, f32[16,8,128]{2,1,0:T(8,128)S(1)}, u32[]{:S(2)}, u32[]{:S(2)}) collective-permute-start(f32[16,8,128]{2,1,0:T(8,128)S(1)} %select_add_fusion), channel_id=1, source_target_pairs={{0,16},{8,24},{16,0},{24,8},{32,48},{40,56},{48,32},{56,40},{64,80... | collective-permute-start | bytes 196616 | tf_op jit(solution)/shard_map/ppermute | solution.py:50
  37.7 10.4 %collective-permute-start.11 = (f32[16,8,128]{2,1,0:T(8,128)S(1)}, f32[16,8,128]{2,1,0:T(8,128)S(1)}, u32[]{:S(2)}, u32[]{:S(2)}) collective-permute-start(f32[16,8,128]{2,1,0:T(8,128)S(1)} %multiply_add_fusion), channel_id=1, source_target_pairs={{0,192},{8,200},{16,208},{24,216},{32,224},{40,232},{48,240},{56,2... | collective-permute-start | bytes 196616 | tf_op jit(solution)/shard_map/ppermute | solution.py:54
  38.4 9.8 %collective-permute-start.10 = (f32[16,8,128]{2,1,0:T(8,128)S(1)}, f32[16,8,128]{2,1,0:T(8,128)S(1)}, u32[]{:S(2)}, u32[]{:S(2)}) collective-permute-start(f32[16,8,128]{2,1,0:T(8,128)S(1)} %multiply_add_fusion), channel_id=1, source_target_pairs={{0,128},{8,136},{16,144},{24,152},{32,160},{40,168},{48,176},{56,1... | collective-permute-start | bytes 196616 | tf_op jit(solution)/shard_map/ppermute | solution.py:54
  45.0 5.0 %collective-permute-start.9 = (f32[16,8,128]{2,1,0:T(8,128)S(1)}, f32[16,8,128]{2,1,0:T(8,128)S(1)}, u32[]{:S(2)}, u32[]{:S(2)}) collective-permute-start(f32[16,8,128]{2,1,0:T(8,128)S(1)} %multiply_add_fusion), channel_id=1, source_target_pairs={{0,64},{8,72},{16,80},{24,88},{32,96},{40,104},{48,112},{56,120},{... | collective-permute-start | bytes 196616 | tf_op jit(solution)/shard_map/ppermute | solution.py:54
  50.6 27.6 %collective-permute-start.13 = (bf16[768,1024]{1,0:T(8,128)(2,1)S(1)}, bf16[768,1024]{1,0:T(8,128)(2,1)S(1)}, u32[]{:S(2)}, u32[]{:S(2)}) collective-permute-start(bf16[768,1024]{1,0:T(8,128)(2,1)S(1)} %pad_maximum_fusion.refs_1_), channel_id=1, source_target_pairs={{0,16},{8,56},{16,32},{24,8},{32,48},{40,24},{48,0},{56,40},{64,80... | collective-permute-start | bytes 4718600 | tf_op jit(solution)/shard_map/ppermute | solution.py:42
  57.3 49.4 %copy-start.5 = (bf16[256,1024]{1,0:T(8,128)(2,1)S(1)}, bf16[256,1024]{1,0:T(8,128)(2,1)}, u32[]{:S(2)}) copy-start(bf16[256,1024]{1,0:T(8,128)(2,1)} %copy-done.4) | copy-start | bytes 1572868
  57.3 61.4 %copy-start.1 = (bf16[256,1024]{1,0:T(8,128)(2,1)S(1)}, bf16[256,1024]{1,0:T(8,128)(2,1)}, u32[]{:S(2)}) copy-start(bf16[256,1024]{1,0:T(8,128)(2,1)} %refs_0_.3) | copy-start | bytes 1572868
  57.3 61.4 %copy-start.3 = (bf16[256,1024]{1,0:T(8,128)(2,1)S(1)}, bf16[256,1024]{1,0:T(8,128)(2,1)}, u32[]{:S(2)}) copy-start(bf16[256,1024]{1,0:T(8,128)(2,1)} %copy-done.2) | copy-start | bytes 1572868
  60.6 1.6 %collective-permute-start.16 = (bf16[256,512]{1,0:T(8,128)(2,1)S(1)}, bf16[256,512]{1,0:T(8,128)(2,1)S(1)}, u32[]{:S(2)}, u32[]{:S(2)}) collective-permute-start(bf16[256,512]{1,0:T(8,128)(2,1)S(1)} %get-tuple-element.40), channel_id=1, source_target_pairs={{0,8},{8,0},{16,24},{24,16},{32,40},{40,32},{48,56},{56,48},{64,72... | collective-permute-start | bytes 786440 | tf_op jit(solution)/shard_map/ppermute | solution.py:38
  60.7 46.0 %collective-permute-start.14 = (bf16[768,1024]{1,0:T(8,128)(2,1)S(1)}, bf16[768,1024]{1,0:T(8,128)(2,1)S(1)}, u32[]{:S(2)}, u32[]{:S(2)}) collective-permute-start(bf16[768,1024]{1,0:T(8,128)(2,1)S(1)} %pad_maximum_fusion.refs_1_), channel_id=1, source_target_pairs={{0,48},{8,24},{16,0},{24,40},{32,16},{40,56},{48,32},{56,8},{64,11... | collective-permute-start | bytes 4718600 | tf_op jit(solution)/shard_map/ppermute | solution.py:42
  62.2 9.7 %collective-permute-start.17 = (bf16[512,512]{1,0:T(8,128)(2,1)S(1)}, bf16[512,512]{1,0:T(8,128)(2,1)S(1)}, u32[]{:S(2)}, u32[]{:S(2)}) collective-permute-start(bf16[512,512]{1,0:T(8,128)(2,1)S(1)} %constant_dynamic-update-slice_fusion.refs_8_), channel_id=1, source_target_pairs={{0,1},{1,2},{2,3},{3,0},{4,5},{5,6},{6,7},{7,4},{8,11},{9,8},{10,9... | collective-permute-start | bytes 1572872 | tf_op jit(solution)/shard_map/ppermute | solution.py:67
  65.0 28.5 %collective-permute-start.20 = (bf16[512,512]{1,0:T(8,128)(2,1)S(1)}, bf16[512,512]{1,0:T(8,128)(2,1)S(1)}, u32[]{:S(2)}, u32[]{:S(2)}) collective-permute-start(bf16[512,512]{1,0:T(8,128)(2,1)S(1)} %constant_dynamic-update-slice_fusion.refs_8_), channel_id=1, source_target_pairs={{0,4},{1,5},{2,6},{3,7},{4,0},{5,1},{6,2},{7,3},{8,12},{9,13},{10,... | collective-permute-start | bytes 1572872 | tf_op jit(solution)/shard_map/ppermute | solution.py:58
  69.0 24.4 %collective-permute-start.19 = (bf16[512,512]{1,0:T(8,128)(2,1)S(1)}, bf16[512,512]{1,0:T(8,128)(2,1)S(1)}, u32[]{:S(2)}, u32[]{:S(2)}) collective-permute-start(bf16[512,512]{1,0:T(8,128)(2,1)S(1)} %constant_dynamic-update-slice_fusion.refs_8_), channel_id=1, source_target_pairs={{0,3},{1,0},{2,1},{3,2},{4,7},{5,4},{6,5},{7,6},{8,9},{9,10},{10,1... | collective-permute-start | bytes 1572872 | tf_op jit(solution)/shard_map/ppermute | solution.py:67
  78.3 40.4 %collective-permute-start.18 = (bf16[768,1024]{1,0:T(8,128)(2,1)S(1)}, bf16[768,1024]{1,0:T(8,128)(2,1)S(1)}, u32[]{:S(2)}, u32[]{:S(2)}) collective-permute-start(bf16[768,1024]{1,0:T(8,128)(2,1)S(1)} %collective-permute-done.13.refs_3_), channel_id=1, source_target_pairs={{0,16},{8,56},{16,32},{24,8},{32,48},{40,24},{48,0},{56,40},{64,80... | collective-permute-start | bytes 4718600 | tf_op jit(solution)/shard_map/ppermute | solution.py:42
  93.5 13.1 %collective-permute-start.21 = (bf16[512,512]{1,0:T(8,128)(2,1)S(1)}, bf16[512,512]{1,0:T(8,128)(2,1)S(1)}, u32[]{:S(2)}, u32[]{:S(2)}) collective-permute-start(bf16[512,512]{1,0:T(8,128)(2,1)S(1)} %collective-permute-done.20.refs_9_), channel_id=1, source_target_pairs={{0,1},{1,2},{2,3},{3,0},{4,5},{5,6},{6,7},{7,4},{8,11},{9,8},{10,9... | collective-permute-start | bytes 1572872 | tf_op jit(solution)/shard_map/ppermute | solution.py:67
  94.4 15.2 %collective-permute-start.22 = (bf16[512,512]{1,0:T(8,128)(2,1)S(1)}, bf16[512,512]{1,0:T(8,128)(2,1)S(1)}, u32[]{:S(2)}, u32[]{:S(2)}) collective-permute-start(bf16[512,512]{1,0:T(8,128)(2,1)S(1)} %collective-permute-done.20.refs_9_), channel_id=1, source_target_pairs={{0,3},{1,0},{2,1},{3,2},{4,7},{5,4},{6,5},{7,6},{8,9},{9,10},{10,1... | collective-permute-start | bytes 1572872 | tf_op jit(solution)/shard_map/ppermute | solution.py:67
  95.0 18.1 %collective-permute-start.23 = (bf16[512,512]{1,0:T(8,128)(2,1)S(1)}, bf16[512,512]{1,0:T(8,128)(2,1)S(1)}, u32[]{:S(2)}, u32[]{:S(2)}) collective-permute-start(bf16[512,512]{1,0:T(8,128)(2,1)S(1)} %collective-permute-done.17.refs_10_), channel_id=1, source_target_pairs={{0,1},{1,2},{2,3},{3,0},{4,5},{5,6},{6,7},{7,4},{8,11},{9,8},{10,9... | collective-permute-start | bytes 1572872 | tf_op jit(solution)/shard_map/ppermute | solution.py:67
  106.6 12.1 %collective-permute-start.24 = (bf16[512,512]{1,0:T(8,128)(2,1)S(1)}, bf16[512,512]{1,0:T(8,128)(2,1)S(1)}, u32[]{:S(2)}, u32[]{:S(2)}) collective-permute-start(bf16[512,512]{1,0:T(8,128)(2,1)S(1)} %collective-permute-done.21.refs_11_), channel_id=1, source_target_pairs={{0,1},{1,2},{2,3},{3,0},{4,5},{5,6},{6,7},{7,4},{8,11},{9,8},{10,9... | collective-permute-start | bytes 1572872 | tf_op jit(solution)/shard_map/ppermute | solution.py:67
  106.7 12.0 %collective-permute-start.15 = (bf16[256,1024]{1,0:T(8,128)(2,1)S(1)}, bf16[256,1024]{1,0:T(8,128)(2,1)S(1)}, u32[]{:S(2)}, u32[]{:S(2)}) collective-permute-start(bf16[256,1024]{1,0:T(8,128)(2,1)S(1)} %copy-done.5), channel_id=1, source_target_pairs={{0,16},{8,56},{16,32},{24,8},{32,48},{40,24},{48,0},{56,40},{64,80... | collective-permute-start | bytes 1572872 | tf_op jit(solution)/shard_map/ppermute | solution.py:42
  121.9 5.6 %collective-permute-start.25 = (bf16[256,1024]{1,0:T(8,128)(2,1)S(1)}, bf16[256,1024]{1,0:T(8,128)(2,1)S(1)}, u32[]{:S(2)}, u32[]{:S(2)}) collective-permute-start(bf16[256,1024]{1,0:T(8,128)(2,1)S(1)} %projection.3), channel_id=1, source_target_pairs={{0,8},{8,0},{16,24},{24,16},{32,40},{40,32},{48,56},{56,48},{64,72... | collective-permute-start | bytes 1572872 | tf_op jit(solution)/shard_map/ppermute | solution.py:38
  (12 other events, 16.4 us)
